TPU v7x, 32 devices: a whole 2x2x4 slice. The times are simulated.
32 devices in a mesh: blk: 16 (over z, y, core), ffn: 2 (over x).
Axes of the slice: x: 2, y: 2, z: 4, core: 2. Of those that a mesh axis runs over, the one named last changes fastest.
Arguments:
- tokens: bfloat16 [4096, 4608], P('blk'), may hold values from -6 to 6
- ln_gain: float32 [4608], replicated, may hold values from 0.5 to 2
- ln_bias: float32 [4608], replicated, may hold values from -3 to 3
- fc1_tiles: bfloat16 [16, 2, 101, 128, 128], P('blk', 'ffn'), may hold values from -0.125 to 0.125
- fc1_index: int32 [16, 2, 101], P('blk', 'ffn'), may hold values from 0 to 2591, as said below
- fc1_count: int32 [16, 2], P('blk', 'ffn'), may hold values from 60 to 101, as said below
- fc1_bias: float32 [18432], P('ffn'), may hold values from -3 to 3
- fc2_tiles: bfloat16 [16, 2, 101, 128, 128], P('blk', 'ffn'), may hold values from -0.09375 to 0.09375
- fc2_index: int32 [16, 2, 101], P('blk', 'ffn'), may hold values from 0 to 2591, as said below
- fc2_count: int32 [16, 2], P('blk', 'ffn'), may hold values from 60 to 101, as said below
- fc2_bias: float32 [4608], P('ffn'), may hold values from -3 to 3
Outputs:
- result: bfloat16 [4096, 4608], P('blk', 'ffn')
Inputs may be any that keep to these rules, and one draw needn't show every extreme that they name: `fc1_index`: within one index f of ffn, the positions of all live slots (s < the shard's count) are distinct. `fc2_index`: as for fc1_index. `fc1_count`: some shard of every index of ffn has all 101 slots live. `fc2_count`: as for fc1_count.
All inputs are finite; a program needn't handle non-finite values.
Results may differ from a plain program's by a relative error of at most 0.01.
Values may be sent and summed in bfloat16 or wider, within the bound.
No kernel may reach another device: no remote copies, remote signals or barrier semaphores. Data moves between devices by JAX's collectives and lax.ppermute only.
A program may use at most 256 MiB of HBM per device.

v0:
```python
import functools

import jax
import jax.numpy as jnp
from jax import lax
from jax.experimental import pallas as pl
from jax.experimental.pallas import tpu as pltpu
from jax.sharding import PartitionSpec as P

UNROLL = 4
VMEM_BYTES = 56 * 1024 * 1024


def add_tiles(row_ref, col_ref, live, base, x_ref, w_ref, acc):
    def one(slot):
        row, col = row_ref[base + slot], col_ref[base + slot]
        return col, jnp.dot(x_ref[row], w_ref[0, 0, slot], preferred_element_type=jnp.float32)

    def several(step, carry):
        products = [one(step * UNROLL + u) for u in range(UNROLL)]
        for col, product in products:
            acc[col] += product
        return carry

    def single(slot, carry):
        col, product = one(slot)
        acc[col] += product
        return carry

    whole = lax.div(live, jnp.int32(UNROLL))
    lax.fori_loop(0, whole, several, 0)
    lax.fori_loop(whole * UNROLL, live, single, 0)


def first_kernel(row_ref, col_ref, count_ref, x_ref, bias_ref, w_ref, out_ref, acc):
    step = pl.program_id(0)
    blocks = acc.shape[0]

    @pl.when(step == 0)
    def _():
        def fill(c, carry):
            acc[c] = jnp.broadcast_to(bias_ref[c], acc.shape[1:])
            return carry

        lax.fori_loop(0, blocks, fill, 0)

    add_tiles(row_ref, col_ref, count_ref[step], step * w_ref.shape[2], x_ref, w_ref, acc)

    @pl.when(step == pl.num_programs(0) - 1)
    def _():
        def finish(c, carry):
            out_ref[c] = jnp.maximum(acc[c], 0.0).astype(out_ref.dtype)
            return carry

        lax.fori_loop(0, blocks, finish, 0)


def second_kernel(row_ref, col_ref, count_ref, x_ref, sum_ref, w_ref, out_ref, acc):
    step = pl.program_id(0)
    blocks = acc.shape[0]

    @pl.when(step == 0)
    def _():
        acc[...] = sum_ref[...]

    add_tiles(row_ref, col_ref, count_ref[step], step * w_ref.shape[2], x_ref, w_ref, acc)

    @pl.when(step == pl.num_programs(0) - 1)
    def _():
        if len(out_ref.shape) == 3:
            out_ref[...] = acc[...]
        else:
            width = acc.shape[2]
            for c in range(blocks):
                out_ref[:, c * width : (c + 1) * width] = acc[c].astype(out_ref.dtype)


def whole_block(shape):
    return pl.BlockSpec(shape, lambda i, *_: (0,) * len(shape))


def tile_pass(kernel, rows, cols, counts, x, start, tiles, out_shape, blocks):
    shards, slots, side = tiles.shape[0], tiles.shape[2], tiles.shape[3]
    tokens = x.shape[1]
    return pl.pallas_call(
        kernel,
        out_shape=out_shape,
        grid_spec=pltpu.PrefetchScalarGridSpec(
            num_scalar_prefetch=3,
            grid=(shards,),
            in_specs=[
                whole_block(x.shape),
                whole_block(start.shape),
                pl.BlockSpec((1, 1, slots, side, side), lambda i, *_: (i, 0, 0, 0, 0)),
            ],
            out_specs=whole_block(out_shape.shape),
            scratch_shapes=[pltpu.VMEM((blocks, tokens, side), jnp.float32)],
        ),
        compiler_params=pltpu.CompilerParams(vmem_limit_bytes=VMEM_BYTES),
        cost_estimate=pl.CostEstimate(
            flops=8 * shards * slots * tokens * side * side,
            bytes_accessed=shards * slots * side * side * 2,
            transcendentals=0,
        ),
    )(rows.reshape(-1), cols.reshape(-1), counts, x, start, tiles)


def on_device(
    tokens,
    ln_gain,
    ln_bias,
    fc1_tiles,
    fc1_index,
    fc1_count,
    fc1_bias,
    fc2_tiles,
    fc2_index,
    fc2_count,
    fc2_bias,
    ffn_size,
):
    side = fc1_tiles.shape[-1]
    slots = fc1_tiles.shape[2]
    token_rows, width = tokens.shape
    first_blocks = fc1_bias.shape[0] // side
    second_blocks = width // side

    gathered1 = lax.all_gather(fc1_tiles, "blk", axis=0, tiled=True)
    cuts = [0, slots // 2, slots - slots // 6, slots]
    gathered2 = [
        lax.all_gather(fc2_tiles[:, :, lo:hi], "blk", axis=0, tiled=True)
        for lo, hi in zip(cuts[:-1], cuts[1:])
    ]
    meta = jnp.concatenate(
        [fc1_index[:, 0], fc2_index[:, 0], fc1_count, fc2_count], axis=1
    )
    meta = lax.all_gather(meta, "blk", axis=0, tiled=True)
    index1, index2 = meta[:, :slots], meta[:, slots : 2 * slots]
    count1, count2 = meta[:, 2 * slots], meta[:, 2 * slots + 1]

    rows_f = tokens.astype(jnp.float32)
    center = jnp.mean(rows_f, axis=1, keepdims=True)
    spread = jnp.mean((rows_f - center) ** 2, axis=1, keepdims=True)
    normed = ((rows_f - center) / jnp.sqrt(spread + 1e-05) * ln_gain + ln_bias).astype(jnp.bfloat16)
    normed_blocks = normed.reshape(token_rows, second_blocks, side).transpose(1, 0, 2)

    hidden = tile_pass(
        first_kernel,
        index1 // first_blocks,
        index1 % first_blocks,
        count1,
        normed_blocks,
        fc1_bias.reshape(first_blocks, 1, side),
        gathered1,
        jax.ShapeDtypeStruct((first_blocks, token_rows, side), jnp.bfloat16),
        first_blocks,
    )

    partial_value = jnp.zeros((second_blocks, token_rows, side), jnp.float32)
    for part, (lo, hi) in enumerate(zip(cuts[:-1], cuts[1:])):
        last = part == len(gathered2) - 1
        shape = (
            jax.ShapeDtypeStruct((token_rows, width), jnp.bfloat16)
            if last
            else jax.ShapeDtypeStruct(partial_value.shape, jnp.float32)
        )
        partial_value = tile_pass(
            second_kernel,
            index2[:, lo:hi] // second_blocks,
            index2[:, lo:hi] % second_blocks,
            jnp.clip(count2 - lo, 0, hi - lo),
            hidden,
            partial_value,
            gathered2[part],
            shape,
            second_blocks,
        )

    me = lax.axis_index("ffn")
    share = width // ffn_size
    branch = lax.dynamic_slice_in_dim(partial_value, me * share, share, 1).astype(jnp.float32)
    for shift in range(1, ffn_size):
        to = lax.rem(me + shift, ffn_size)
        piece = lax.dynamic_slice_in_dim(partial_value, to * share, share, 1)
        arrived = lax.ppermute(
            piece, "ffn", [(i, (i + shift) % ffn_size) for i in range(ffn_size)]
        )
        branch = branch + arrived.astype(jnp.float32)
    own_cols = lax.dynamic_slice_in_dim(rows_f, me * share, share, 1)
    return (own_cols + branch + fc2_bias).astype(jnp.bfloat16)


def solution(mesh):
    placed = (
        P("blk", None),
        P(),
        P(),
        P("blk", "ffn", None, None, None),
        P("blk", "ffn", None),
        P("blk", "ffn"),
        P("ffn"),
        P("blk", "ffn", None, None, None),
        P("blk", "ffn", None),
        P("blk", "ffn"),
        P("ffn"),
    )
    return jax.shard_map(
        functools.partial(on_device, ffn_size=mesh.shape["ffn"]),
        mesh=mesh,
        in_specs=placed,
        out_specs=P("blk", "ffn"),
        check_vma=False,
    )
```

profile of v0, /device:TPU:0, one launch (start us, length us, event | category | flops | bytes accessed | tf_op | source)
XLA Modules:
  0.0 639.3 jit_solution(1452155524235808468)
XLA Ops:
  6.5 0.7 all-gather.6.cloned.1.call-update
  7.3 2.8 slice.40
  10.2 2.5 slice.41
  12.8 1.9 slice.42
  16.2 23.1 %all-gather = s32[16,1,204]{2,1,0:T(1,128)S(1)} all-gather(s32[1,1,204]{2,1,0:T(1,128)S(1)} %add_bitcast_fusion), channel_id=1, replica_groups=mesh['blk'=16,'ffn'=2] {'blk'}, dimensions={0}, use_global_device_ids=true | all-gather | bytes 13872 | tf_op jit(solution)/shard_map/all_gather | solution.py:137
  39.4 0.7 reshape.60.row_ref
  40.0 0.7 reshape.61.col_ref
  41.1 0.8 multiply_reduce_fusion
  41.9 2.6 add_convert_fusion
  44.5 4.3 copy.17
  48.7 4.3 copy.18
  53.3 0.7 reshape.66.row_ref
  53.9 0.7 reshape.67.col_ref
  54.8 0.7 reshape.64.row_ref
  55.4 0.7 reshape.65.col_ref
  56.3 0.7 reshape.58.row_ref
  57.0 0.6 reshape.59.col_ref
  57.6 0.8 clamp_reduce_fusion
  58.4 212.8 %all-gather.6.cloned.1.call-done.w_ref = bf16[16,1,101,128,128]{4,3,2,1,0:T(8,128)(2,1)} async-done(((bf16[1,1,101,128,128]{4,3,2,1,0:T(8,128)(2,1)}), bf16[16,1,101,128,128]{4,3,2,1,0:T(8,128)(2,1)}) %all-gather.6.cloned.1.call-update) | async-done | bytes 52953104 | tf_op jit(solution)/shard_map/all_gather | solution.py:128
  271.2 83.4 %shard_map.109.x_ref = bf16[72,256,128]{2,1,0:T(8,128)(2,1)} custom-call(s32[1616]{0:T(1024)} %reshape.60.row_ref, s32[1616]{0:T(1024)} %reshape.61.col_ref, s32[16]{0:T(128)} %get-tuple-element.7.count_ref, bf16[36,256,128]{2,1,0:T(8,128)(2,1)} %bitcast.11, f32[72,1,128]{2,1,0:T(1,128)} %bitcast.23, ...), custom_call_target="tpu_custom_call" | custom-call | flops 54223962112 | bytes 52953088 | tf_op jit(solution)/shard_map/pallas_call | solution.py:85
  354.5 51.9 %all-gather.8.cloned.1.call-done.w_ref = bf16[16,1,50,128,128]{4,3,2,1,0:T(8,128)(2,1)} async-done(((bf16[1,1,50,128,128]{4,3,2,1,0:T(8,128)(2,1)}), bf16[16,1,50,128,128]{4,3,2,1,0:T(8,128)(2,1)}) %all-gather.8.cloned.1.call-update) | async-done | bytes 26214416 | tf_op jit(solution)/shard_map/all_gather | solution.py:131
  406.4 2.7 broadcast_in_dim.2.sum_ref
  409.1 56.7 %shard_map.110.sum_ref = f32[36,256,128]{2,1,0:T(8,128)} custom-call(s32[800]{0:T(1024)} %reshape.66.row_ref, s32[800]{0:T(1024)} %reshape.67.col_ref, s32[16]{0:T(128)} %get-tuple-element.5.count_ref, bf16[72,256,128]{2,1,0:T(8,128)(2,1)} %shard_map.109.x_ref, f32[36,256,128]{2,1,0:T(8,128)} %broadcast_in_dim.2.sum_ref, ...), custom_call_target="tpu_custom_call" | custom-call | flops 26843545600 | bytes 26214400 | tf_op jit(solution)/shard_map/pallas_call | solution.py:85
  465.8 38.7 %all-gather.10.cloned.1.call-done.w_ref = bf16[16,1,35,128,128]{4,3,2,1,0:T(8,128)(2,1)} async-done(((bf16[1,1,35,128,128]{4,3,2,1,0:T(8,128)(2,1)}), bf16[16,1,35,128,128]{4,3,2,1,0:T(8,128)(2,1)}) %all-gather.10.cloned.1.call-update) | async-done | bytes 18350096 | tf_op jit(solution)/shard_map/all_gather | solution.py:131
  504.5 36.6 %shard_map.111.sum_ref = f32[36,256,128]{2,1,0:T(8,128)} custom-call(s32[560]{0:T(1024)} %reshape.64.row_ref, s32[560]{0:T(1024)} %reshape.65.col_ref, s32[16]{0:T(128)} %get-tuple-element.6.count_ref, bf16[72,256,128]{2,1,0:T(8,128)(2,1)} %shard_map.109.x_ref, f32[36,256,128]{2,1,0:T(8,128)} %shard_map.110.sum_ref, ...), custom_call_target="tpu_custom_call" | custom-call | flops 18790481920 | bytes 18350080 | tf_op jit(solution)/shard_map/pallas_call | solution.py:85
  541.1 40.4 %all-gather.12.cloned.1.call-done.w_ref = bf16[16,1,16,128,128]{4,3,2,1,0:T(8,128)(2,1)} async-done(((bf16[1,1,16,128,128]{4,3,2,1,0:T(8,128)(2,1)}), bf16[16,1,16,128,128]{4,3,2,1,0:T(8,128)(2,1)}) %all-gather.12.cloned.1.call-update) | async-done | bytes 8388624 | tf_op jit(solution)/shard_map/all_gather | solution.py:131
  581.5 17.8 %shard_map.112 = bf16[256,4608]{1,0:T(8,128)(2,1)} custom-call(s32[256]{0:T(256)} %reshape.58.row_ref, s32[256]{0:T(256)} %reshape.59.col_ref, s32[16]{0:T(128)} %get-tuple-element.8.count_ref, bf16[72,256,128]{2,1,0:T(8,128)(2,1)} %shard_map.109.x_ref, f32[36,256,128]{2,1,0:T(8,128)} %shard_map.111.sum_ref, ...), custom_call_target="tpu_custom_call" | custom-call | flops 8589934592 | bytes 8388608 | tf_op jit(solution)/shard_map/pallas_call | solution.py:85
  599.3 1.3 constant_dynamic-slice_fusion
  600.7 0.4 collective-permute-start
  601.1 2.7 convert_element_type.15
  603.8 25.2 %collective-permute-done = bf16[256,2304]{1,0:T(8,128)(2,1)} collective-permute-done((bf16[256,2304]{1,0:T(8,128)(2,1)S(1)}, bf16[256,2304]{1,0:T(8,128)(2,1)}, u32[]{:S(2)}, u32[]{:S(2)}) %collective-permute-start) | collective-permute-done | bytes 1179680 | tf_op jit(solution)/shard_map/ppermute | solution.py:185
  629.0 3.8 add_convert_fusion.1
  (32 shorter events, 1.2 us)
Async XLA Ops:
  6.5 264.6 %all-gather.6.cloned.1.call-start = ((), (), s32[]{:S(2)}) async-start(), calls=%async_computation | async-start | bytes 56262656 | tf_op jit(solution)/shard_map/all_gather | solution.py:128
  7.3 399.2 %all-gather.8.cloned.1.call-start = ((), (), s32[]{:S(2)}) async-start(), calls=%async_computation.1 | async-start | bytes 27852800 | tf_op jit(solution)/shard_map/all_gather | solution.py:131
  10.1 5.9 copy-start.4
  10.2 5.9 copy-start.5
  10.2 30.5 %copy-start = (bf16[256,4608]{1,0:T(8,128)(2,1)S(1)}, bf16[256,4608]{1,0:T(8,128)(2,1)}, u32[]{:S(2)}) copy-start(bf16[256,4608]{1,0:T(8,128)(2,1)} %param.11) | copy-start | bytes 7077892
  10.2 494.4 %all-gather.10.cloned.1.call-start = ((), (), s32[]{:S(2)}) async-start(), calls=%async_computation.2 | async-start | bytes 19496960 | tf_op jit(solution)/shard_map/all_gather | solution.py:131
  12.8 568.8 %all-gather.12.cloned.1.call-start = ((), (), s32[]{:S(2)}) async-start(), calls=%async_computation.3 | async-start | bytes 8912896 | tf_op jit(solution)/shard_map/all_gather | solution.py:131
  40.7 1.2 copy-start.1
  40.7 1.2 copy-start.2
  600.7 28.3 %collective-permute-start = (bf16[256,2304]{1,0:T(8,128)(2,1)S(1)}, bf16[256,2304]{1,0:T(8,128)(2,1)}, u32[]{:S(2)}, u32[]{:S(2)}) collective-permute-start(bf16[256,2304]{1,0:T(8,128)(2,1)S(1)} %constant_dynamic-slice_fusion), channel_id=1, source_target_pairs={{0,1},{1,0},{2,3},{3,2},{4,5},{5,4},{6,7},{7,6},{8,9},{9,8},{10,11... | collective-permute-start | bytes 3538952 | tf_op jit(solution)/shard_map/ppermute | solution.py:185
  601.1 27.9 %copy-start.3 = (f32[2304]{0:T(1024)S(1)}, f32[2304]{0:T(1024)}, u32[]{:S(2)}) copy-start(f32[2304]{0:T(1024)} %param.21) | copy-start | bytes 27652
Sparse Core Ops, SparseCore 0:
  9.0 262.1 all-gather.5
  272.8 133.6 all-gather.7
  408.0 96.4 all-gather.9
  506.5 74.9 all-gather.11
where the time goes:
time: 641 us; the launch traced here: 639 us
  waiting for transfers between devices  370 us (58%)
  Pallas kernels  194 us (30%)
  local copies, waits for them, and re-layouts  25.3 us (4%)
  blocking collectives  23.1 us (4%)
  between operations  14.5 us (2%)
  other arithmetic  11.6 us (2%)
    all_gather x1, waiting for transfers between devices, on_device(): gathered1 = lax.all_gather(fc1_tiles, 'blk', axis=0, tiled=True)  213 us
    pallas_call x4, Pallas kernels, tile_pass(): pl.pallas_call(kernel, out_shape=out_shape, grid_spec=pltpu.PrefetchScala...  194 us
    all_gather x3, waiting for transfers between devices, on_device(): lax.all_gather(fc2_tiles[:, :, lo:hi], 'blk', axis=0, tiled=True)  131 us
    ppermute x1, waiting for transfers between devices, on_device(): lax.ppermute(piece, 'ffn', [(i, (i + shift) % ffn_size) for i in range(ff...  25.2 us
    all_gather x1, blocking collectives, on_device(): meta = lax.all_gather(meta, 'blk', axis=0, tiled=True)  23.1 us
  transfers between devices with their start and end apart: 5, of which 5 were waited for; matrix products, arithmetic and copies ran while one was open for 5% of the time, Pallas kernels for 28%

commit v1 on v0

v1 whole, which is shorter than its diff:
```python
import functools

import jax
import jax.numpy as jnp
from jax import lax
from jax.experimental import pallas as pl
from jax.experimental.pallas import tpu as pltpu
from jax.sharding import PartitionSpec as P

UNROLL = 4
VMEM_BYTES = 56 * 1024 * 1024


def add_tiles(row_ref, col_ref, live, base, x_ref, w_ref, acc):
    def one(slot):
        row, col = row_ref[base + slot], col_ref[base + slot]
        return col, jnp.dot(x_ref[row], w_ref[0, 0, slot], preferred_element_type=jnp.float32)

    def several(step, carry):
        products = [one(step * UNROLL + u) for u in range(UNROLL)]
        for col, product in products:
            acc[col] += product
        return carry

    def single(slot, carry):
        col, product = one(slot)
        acc[col] += product
        return carry

    whole = lax.div(live, jnp.int32(UNROLL))
    lax.fori_loop(0, whole, several, 0)
    lax.fori_loop(whole * UNROLL, live, single, 0)


def pass_kernel(row_ref, col_ref, count_ref, x_ref, sum_ref, w_ref, out_ref, acc):
    step = pl.program_id(0)
    blocks = acc.shape[0]

    @pl.when(step == 0)
    def _():
        acc[...] = sum_ref[...]

    add_tiles(row_ref, col_ref, count_ref[step], step * w_ref.shape[2], x_ref, w_ref, acc)

    @pl.when(step == pl.num_programs(0) - 1)
    def _():
        if len(out_ref.shape) == 3:
            out_ref[...] = acc[...]
        else:
            width = acc.shape[2]
            for c in range(blocks):
                out_ref[:, c * width : (c + 1) * width] = acc[c].astype(out_ref.dtype)


def tile_pass(rows, cols, counts, x, start, tiles, rows_of=None):
    shards, slots, side = tiles.shape[0], tiles.shape[2], tiles.shape[3]
    blocks, tokens = start.shape[0], x.shape[1]
    place = 0
    out_shape = jax.ShapeDtypeStruct(start.shape, jnp.float32)
    if rows_of is not None:
        place, tokens = rows_of[0] // rows_of[1], rows_of[1]
        out_shape = jax.ShapeDtypeStruct((tokens, blocks * side), jnp.bfloat16)
    return pl.pallas_call(
        pass_kernel,
        out_shape=out_shape,
        grid_spec=pltpu.PrefetchScalarGridSpec(
            num_scalar_prefetch=3,
            grid=(shards,),
            in_specs=[
                pl.BlockSpec((x.shape[0], tokens, side), lambda i, *_: (0, place, 0)),
                pl.BlockSpec((blocks, tokens, side), lambda i, *_: (0, place, 0)),
                pl.BlockSpec((1, 1, slots, side, side), lambda i, *_: (i, 0, 0, 0, 0)),
            ],
            out_specs=pl.BlockSpec(out_shape.shape, lambda i, *_: (0,) * len(out_shape.shape)),
            scratch_shapes=[pltpu.VMEM((blocks, tokens, side), jnp.float32)],
        ),
        compiler_params=pltpu.CompilerParams(vmem_limit_bytes=VMEM_BYTES),
        cost_estimate=pl.CostEstimate(
            flops=8 * shards * slots * tokens * side * side,
            bytes_accessed=shards * slots * side * side * 2,
            transcendentals=0,
        ),
    )(rows.reshape(-1), cols.reshape(-1), counts, x, start, tiles)


def pick(mask, size, values):
    marks = mask.astype(jnp.int32)
    rank = jnp.cumsum(marks, axis=-1) - marks
    hit = mask[..., None, :] & (rank[..., None, :] == jnp.arange(size, dtype=jnp.int32)[:, None])
    return jnp.sum(jnp.where(hit, values[..., None, :], 0), axis=-1)


def after(mask, size):
    marks = mask.astype(jnp.int32)
    return mask & (jnp.cumsum(marks, axis=-1) - marks >= size)


def norm(tokens, gain, bias, side):
    rows_f = tokens.astype(jnp.float32)
    center = jnp.mean(rows_f, axis=1, keepdims=True)
    spread = jnp.mean((rows_f - center) ** 2, axis=1, keepdims=True)
    normed = ((rows_f - center) / jnp.sqrt(spread + 1e-05) * gain + bias).astype(jnp.bfloat16)
    return normed.reshape(tokens.shape[0], -1, side).transpose(1, 0, 2)


def on_device(
    tokens,
    ln_gain,
    ln_bias,
    fc1_tiles,
    fc1_index,
    fc1_count,
    fc1_bias,
    fc2_tiles,
    fc2_index,
    fc2_count,
    fc2_bias,
    blk_size,
    ffn_size,
):
    side = fc1_tiles.shape[-1]
    slots = fc1_tiles.shape[2]
    token_rows, width = tokens.shape
    first_blocks = fc1_bias.shape[0] // side
    second_blocks = width // side
    half_blocks = (first_blocks + 1) // 2
    half_size = blk_size // 2
    listed = min(slots, -(-slots * 5 // 8))
    spare = slots - listed
    blk, ffn = lax.axis_index("blk"), lax.axis_index("ffn")
    half = lax.div(blk, half_size)
    halves = [list(range(half_size)), list(range(half_size, blk_size))]
    across = [(i, (i + half_size) % blk_size) for i in range(blk_size)]
    slot_ids = jnp.arange(slots, dtype=jnp.int32)

    def first_place(p):
        row, col = p // first_blocks, p % first_blocks
        group = (col >= half_blocks).astype(jnp.int32)
        return group, row, col - group * half_blocks

    def second_place(p):
        row, col = p // second_blocks, p % second_blocks
        group = (row >= half_blocks).astype(jnp.int32)
        return group, row - group * half_blocks, col

    def split(tiles, index, count, place):
        live = slot_ids < count[0, 0]
        group = place(index[0, 0])[0]
        mine, other = live & (group == half), live & (group != half)
        order = pick(jnp.stack([mine, other]), listed, slot_ids[None])
        kept = jnp.take(tiles[0, 0], order[0], axis=0, mode="clip")[None, None]
        sent = jnp.take(tiles[0, 0], order[1], axis=0, mode="clip")[None, None]
        left = pick(after(mine, listed) | after(other, listed), max(spare, 1), slot_ids)
        return kept, lax.ppermute(sent, "blk", across), left

    def share_out(tiles):
        return lax.all_gather(tiles, "blk", axis=0, axis_index_groups=halves, tiled=True)

    kept1, got1, left1 = split(fc1_tiles, fc1_index, fc1_count, first_place)
    kept2, got2, left2 = split(fc2_tiles, fc2_index, fc2_count, second_place)
    other_tokens = lax.ppermute(tokens, "blk", across)
    kept1, kept2 = share_out(kept1), share_out(kept2)
    got1, got2 = share_out(got1), share_out(got2)

    meta = jnp.concatenate([fc1_index[:, 0], fc2_index[:, 0], fc1_count, fc2_count], axis=1)
    meta = lax.all_gather(meta, ("blk", "ffn"), axis=0, tiled=True)
    meta = meta.reshape(blk_size, ffn_size, -1)
    own_meta = lax.dynamic_index_in_dim(meta, ffn, 1, keepdims=False)

    def lists(index, counts, place):
        group, row, col = place(index)
        wanted = (slot_ids < counts[:, None]) & (group == half)
        total = jnp.sum(wanted.astype(jnp.int32), axis=1)
        fields = [
            pick(wanted, listed, row),
            pick(wanted, listed, col),
            jnp.minimum(total, listed),
        ]
        kept = [lax.dynamic_slice_in_dim(f, half * half_size, half_size) for f in fields]
        got = [lax.dynamic_slice_in_dim(f, (1 - half) * half_size, half_size) for f in fields]
        late = after(wanted, listed)
        left = [
            pick(late, max(spare, 1), row),
            pick(late, max(spare, 1), col),
            jnp.maximum(total - listed, 0),
        ]
        return kept, got, left

    def overflow(index, counts, place):
        group = place(index)[0]
        live = slot_ids < counts[..., None]
        ones = jnp.sum((live & (group == 1)).astype(jnp.int32), axis=-1)
        return jnp.any(jnp.maximum(ones, counts - ones) > listed)

    fields1 = lists(own_meta[:, :slots], own_meta[:, 2 * slots], first_place)
    fields2 = lists(own_meta[:, slots : 2 * slots], own_meta[:, 2 * slots + 1], second_place)
    over1 = overflow(meta[..., :slots], meta[..., 2 * slots], first_place)
    over2 = overflow(meta[..., slots : 2 * slots], meta[..., 2 * slots + 1], second_place)

    def with_left(over, tiles, order, fields, x, start):
        if spare == 0:
            return start

        def extra(x, start):
            rest = jnp.take(tiles[0, 0], order, axis=0, mode="clip")[None, None]
            return tile_pass(*fields, x, start, lax.all_gather(rest, "blk", axis=0, tiled=True))

        return lax.cond(over, extra, lambda x, start: start, x, start)

    normed = jnp.concatenate(
        [norm(tokens, ln_gain, ln_bias, side), norm(other_tokens, ln_gain, ln_bias, side)], axis=1
    )
    bias = jnp.pad(fc1_bias, (0, (2 * half_blocks - first_blocks) * side))
    bias = lax.dynamic_slice_in_dim(bias, half * half_blocks * side, half_blocks * side)
    total = jnp.broadcast_to(bias.reshape(-1, 1, side), (half_blocks, 2 * token_rows, side))
    total = with_left(over1, fc1_tiles, left1, fields1[2], normed, total)
    total = tile_pass(*fields1[0], normed, total, kept1)
    total = tile_pass(*fields1[1], normed, total, got1)
    hidden = jnp.maximum(total, 0.0).astype(jnp.bfloat16)

    total = jnp.zeros((second_blocks, 2 * token_rows, side), jnp.float32)
    total = with_left(over2, fc2_tiles, left2, fields2[2], hidden, total)
    total = tile_pass(*fields2[0], hidden, total, kept2)
    other_part = tile_pass(*fields2[1], hidden, total, got2, (token_rows, token_rows))
    own_part = tile_pass(*fields2[1], hidden, total, got2, (0, token_rows))

    share = width // ffn_size

    def over_ffn(part):
        branch = lax.dynamic_slice_in_dim(part, ffn * share, share, 1).astype(jnp.float32)
        for shift in range(1, ffn_size):
            to = lax.rem(ffn + shift, ffn_size)
            arrived = lax.ppermute(
                lax.dynamic_slice_in_dim(part, to * share, share, 1),
                "ffn",
                [(i, (i + shift) % ffn_size) for i in range(ffn_size)],
            )
            branch = branch + arrived.astype(jnp.float32)
        return branch

    from_other = lax.ppermute(over_ffn(other_part).astype(jnp.bfloat16), "blk", across)
    branch = over_ffn(own_part) + from_other.astype(jnp.float32)
    own_cols = lax.dynamic_slice_in_dim(tokens, ffn * share, share, 1).astype(jnp.float32)
    return (own_cols + branch + fc2_bias).astype(jnp.bfloat16)


def solution(mesh):
    placed = (
        P("blk", None),
        P(),
        P(),
        P("blk", "ffn", None, None, None),
        P("blk", "ffn", None),
        P("blk", "ffn"),
        P("ffn"),
        P("blk", "ffn", None, None, None),
        P("blk", "ffn", None),
        P("blk", "ffn"),
        P("ffn"),
    )
    return jax.shard_map(
        functools.partial(on_device, blk_size=mesh.shape["blk"], ffn_size=mesh.shape["ffn"]),
        mesh=mesh,
        in_specs=placed,
        out_specs=P("blk", "ffn"),
        check_vma=False,
    )
```

time: 641 us -> 806 us (1.26)
  blocking collectives: 23.1 us -> 111 us
  starting transfers between devices: 0.53 us -> 50.1 us
  other arithmetic: 11.6 us -> 41.8 us
  Pallas kernels: 194 us -> 166 us
  local copies, waits for them, and re-layouts: 25.3 us -> 45.1 us
    ppermute x1 -> x6, waiting for transfers between devices: 25.2 us -> 233 us  [the longest x2 182 us: split(): return (kept, lax.ppermute(sent, 'blk', across), left)]
    all_gather x4, waiting for transfers between devices: 344 us -> 141 us  [share_out(): lax.all_gather(tiles, 'blk', axis=0, axis_index_groups=halves, tiled=True)]
    all_gather x1, blocking collectives: 23.1 us -> 111 us  [on_device(): meta = lax.all_gather(meta, ('blk', 'ffn'), axis=0, tiled=True)]
    ppermute x1 -> x6, starting transfers between devices: 0.41 us -> 49.6 us  [the longest x2 37.6 us: split(): return (kept, lax.ppermute(sent, 'blk', across), left)]
    pallas_call x4 -> x5, Pallas kernels: 194 us -> 166 us  [tile_pass(): pl.pallas_call(pass_kernel, out_shape=out_shape, grid_spec=pltpu.Prefetch...]
    gather x0 -> x4, local copies, waits for them, and re-layouts: none -> 10.6 us  [the longest x2 6.26 us: split(): kept = jnp.take(tiles[0, 0], order[0], axis=0, mode='clip')[None, None]]
    convert_element_type x2 -> x17, other arithmetic: 5.23 us -> 14.4 us  [the longest x1 6.97 us: on_device(): hidden = jnp.maximum(total, 0.0).astype(jnp.bfloat16)]
    reduce_sum x2 -> x9, other arithmetic: 1.16 us -> 9.36 us  [the longest x2 3.01 us: norm(): spread = jnp.mean((rows_f - center) ** 2, axis=1, keepdims=True)]
  transfers between devices with their start and end apart: 5 -> 10, of which waited for: 5 -> 8; matrix products, arithmetic and copies ran while one was open for 5% -> 5% of each run, Pallas kernels for 28% -> 12%
where the time goes in v1:
time: 806 us; the launch traced here: 807 us
  waiting for transfers between devices  376 us (47%)
  Pallas kernels  166 us (21%)
  blocking collectives  111 us (14%)
  starting transfers between devices  50.1 us (6%)
  local copies, waits for them, and re-layouts  45.1 us (6%)
  other arithmetic  41.8 us (5%)
  between operations  17.9 us (2%)
    ppermute x2, waiting for transfers between devices, split(): return (kept, lax.ppermute(sent, 'blk', across), left)  182 us
    pallas_call x5, Pallas kernels, tile_pass(): pl.pallas_call(pass_kernel, out_shape=out_shape, grid_spec=pltpu.Prefetch...  166 us
    all_gather x4, waiting for transfers between devices, share_out(): lax.all_gather(tiles, 'blk', axis=0, axis_index_groups=halves, tiled=True)  141 us
    all_gather x1, blocking collectives, on_device(): meta = lax.all_gather(meta, ('blk', 'ffn'), axis=0, tiled=True)  111 us
    ppermute x2, starting transfers between devices, split(): return (kept, lax.ppermute(sent, 'blk', across), left)  37.6 us
    ppermute x1, waiting for transfers between devices, on_device(): lax.ppermute(over_ffn(other_part).astype(jnp.bfloat16), 'blk', across)  31.3 us
    ppermute x2, waiting for transfers between devices, over_ffn(): lax.ppermute(lax.dynamic_slice_in_dim(part, to * share, share, 1), 'ffn',...  20.1 us
  transfers between devices with their start and end apart: 10, of which 8 were waited for; matrix products, arithmetic and copies ran while one was open for 5% of the time, Pallas kernels for 12%

profile of v1, /device:TPU:0, one launch (start us, length us, event | category | flops | bytes accessed | tf_op | source)
XLA Modules:
  0.0 807.2 jit_solution(7281551143943624106)
XLA Ops:
  7.4 2.9 copy.58
  10.2 4.1 collective-permute-start
  15.8 110.9 %all-gather.4 = s32[32,1,204]{2,1,0:T(1,128)S(1)} all-gather(s32[1,1,204]{2,1,0:T(1,128)S(1)} %add_bitcast_fusion), channel_id=1, replica_groups=mesh['blk'=16,'ffn'=2] {'blk','ffn'}, dimensions={0}, use_global_device_ids=true | all-gather | bytes 26928 | tf_op jit(solution)/shard_map/all_gather | solution.py:166
  134.2 4.1 gather_fusion.2
  141.1 2.3 convert_reduce_fusion
  143.4 2.3 fusion.4
  145.7 5.7 fusion.11
  151.4 4.4 copy.59
  155.8 2.4 copy.61
  158.3 5.0 pad_maximum_fusion.x_ref
  163.3 4.2 broadcast_in_dim.199
  171.0 2.2 gather_fusion.3
  173.2 37.6 %collective-permute-start.1 = (bf16[1,1,64,128,128]{4,3,2,1,0:T(8,128)(2,1)}, bf16[1,1,64,128,128]{4,3,2,1,0:T(8,128)(2,1)}, u32[]{:S(2)}, u32[]{:S(2)}) collective-permute-start(bf16[1,1,64,128,128]{4,3,2,1,0:T(8,128)(2,1)} %bitcast.100), channel_id=1, source_target_pairs={{0,16},{2,18},{4,20},{6,22},{8,24},{10,26},{12,28},{14,30},{16,0},... | collective-permute-start | bytes 6291464 | tf_op jit(solution)/shard_map/ppermute | solution.py:154
  210.8 87.9 %collective-permute-done.1 = bf16[1,1,64,128,128]{4,3,2,1,0:T(8,128)(2,1)} collective-permute-done((bf16[1,1,64,128,128]{4,3,2,1,0:T(8,128)(2,1)}, bf16[1,1,64,128,128]{4,3,2,1,0:T(8,128)(2,1)}, u32[]{:S(2)}, u32[]{:S(2)}) %collective-permute-start.1) | collective-permute-done | bytes 2097184 | tf_op jit(solution)/shard_map/ppermute | solution.py:154
  310.1 2.2 gather_fusion.4
  314.2 19.5 %all-gather.20.cloned.1.call-done = bf16[512,128,128]{2,1,0:T(8,128)(2,1)} async-done(((bf16[64,128,128]{2,1,0:T(8,128)(2,1)}), bf16[512,128,128]{2,1,0:T(8,128)(2,1)}) %all-gather.20.cloned.1.call-update) | async-done | bytes 16777232 | tf_op jit(solution)/shard_map/all_gather | solution.py:157
  333.7 35.8 %shard_map.109.sum_ref = f32[36,512,128]{2,1,0:T(8,128)} custom-call(s32[512]{0:T(512)} %reshape.719.row_ref, s32[512]{0:T(512)} %reshape.720.col_ref, s32[8]{0:T(128)} %get-tuple-element.357.count_ref, bf16[36,512,128]{2,1,0:T(8,128)(2,1)} %pad_maximum_fusion.x_ref, f32[36,512,128]{2,1,0:T(8,128)} %get-tuple-element.365.sum_ref, ...), custom_call_target="tpu_custom_call" | custom-call | flops 34359738368 | bytes 16777216 | tf_op jit(solution)/shard_map/pallas_call | solution.py:63
  369.6 48.1 %all-gather.16.cloned.1.call-done.w_ref = bf16[8,1,64,128,128]{4,3,2,1,0:T(8,128)(2,1)} async-done(((bf16[1,1,64,128,128]{4,3,2,1,0:T(8,128)(2,1)}), bf16[8,1,64,128,128]{4,3,2,1,0:T(8,128)(2,1)}) %all-gather.16.cloned.1.call-update) | async-done | bytes 16777232 | tf_op jit(solution)/shard_map/all_gather | solution.py:157
  417.7 39.2 %shard_map.110 = f32[36,512,128]{2,1,0:T(8,128)} custom-call(s32[512]{0:T(512)} %reshape.715.row_ref, s32[512]{0:T(512)} %reshape.716.col_ref, s32[8]{0:T(128)} %get-tuple-element.358.count_ref, bf16[36,512,128]{2,1,0:T(8,128)(2,1)} %pad_maximum_fusion.x_ref, f32[36,512,128]{2,1,0:T(8,128)} %shard_map.109.sum_ref, ...), custom_call_target="tpu_custom_call" | custom-call | flops 34359738368 | bytes 16777216 | tf_op jit(solution)/shard_map/pallas_call | solution.py:63
  456.9 7.0 maximum_convert_fusion.x_ref
  464.6 4.8 conditional.3
  464.7 4.7 broadcast.800
  470.3 2.1 gather_fusion.5
  472.4 94.0 %collective-permute-done.2 = bf16[1,1,64,128,128]{4,3,2,1,0:T(8,128)(2,1)S(1)} collective-permute-done((bf16[1,1,64,128,128]{4,3,2,1,0:T(8,128)(2,1)}, bf16[1,1,64,128,128]{4,3,2,1,0:T(8,128)(2,1)S(1)}, u32[]{:S(2)}, u32[]{:S(2)}) %collective-permute-start.2) | collective-permute-done | bytes 2097184 | tf_op jit(solution)/shard_map/ppermute | solution.py:154
  571.1 27.4 %all-gather.22.cloned.1.call-done = bf16[512,128,128]{2,1,0:T(8,128)(2,1)} async-done(((bf16[64,128,128]{2,1,0:T(8,128)(2,1)}), bf16[512,128,128]{2,1,0:T(8,128)(2,1)}) %all-gather.22.cloned.1.call-update) | async-done | bytes 16777232 | tf_op jit(solution)/shard_map/all_gather | solution.py:157
  598.5 37.0 %shard_map.111.sum_ref = f32[36,512,128]{2,1,0:T(8,128)} custom-call(s32[512]{0:T(512)} %reshape.724.row_ref, s32[512]{0:T(512)} %reshape.725.col_ref, s32[8]{0:T(128)} %get-tuple-element.351.count_ref, bf16[36,512,128]{2,1,0:T(8,128)(2,1)} %maximum_convert_fusion.x_ref, f32[36,512,128]{2,1,0:T(8,128)} %get-tuple-element.366.sum_ref, ...), custom_call_target="tpu_custom_call" | custom-call | flops 34359738368 | bytes 16777216 | tf_op jit(solution)/shard_map/pallas_call | solution.py:63
  635.5 46.2 %all-gather.18.cloned.1.call-done.w_ref = bf16[8,1,64,128,128]{4,3,2,1,0:T(8,128)(2,1)} async-done(((bf16[1,1,64,128,128]{4,3,2,1,0:T(8,128)(2,1)}), bf16[8,1,64,128,128]{4,3,2,1,0:T(8,128)(2,1)}) %all-gather.18.cloned.1.call-update) | async-done | bytes 16777232 | tf_op jit(solution)/shard_map/all_gather | solution.py:157
  681.7 26.8 %shard_map.113 = bf16[256,4608]{1,0:T(8,128)(2,1)} custom-call(s32[512]{0:T(512)} %reshape.713.row_ref, s32[512]{0:T(512)} %reshape.714.col_ref, s32[8]{0:T(128)} %get-tuple-element.352.count_ref, bf16[36,512,128]{2,1,0:T(8,128)(2,1)} %maximum_convert_fusion.x_ref, f32[36,512,128]{2,1,0:T(8,128)} %shard_map.111.sum_ref, ...), custom_call_target="tpu_custom_call" | custom-call | flops 17179869184 | bytes 16777216 | tf_op jit(solution)/shard_map/pallas_call | solution.py:63
  710.0 27.0 %shard_map.112 = bf16[256,4608]{1,0:T(8,128)(2,1)} custom-call(s32[512]{0:T(512)} %reshape.713.row_ref, s32[512]{0:T(512)} %reshape.714.col_ref, s32[8]{0:T(128)} %get-tuple-element.352.count_ref, bf16[36,512,128]{2,1,0:T(8,128)(2,1)} %maximum_convert_fusion.x_ref, f32[36,512,128]{2,1,0:T(8,128)} %shard_map.111.sum_ref, ...), custom_call_target="tpu_custom_call" | custom-call | flops 17179869184 | bytes 16777216 | tf_op jit(solution)/shard_map/pallas_call | solution.py:63
  739.4 7.1 collective-permute-start.5
  746.5 20.1 %collective-permute-done.3 = bf16[256,2304]{1,0:T(8,128)(2,1)S(1)} collective-permute-done((bf16[256,2304]{1,0:T(8,128)(2,1)S(1)}, bf16[256,2304]{1,0:T(8,128)(2,1)S(1)}, u32[]{:S(2)}, u32[]{:S(2)}) %collective-permute-start.3) | collective-permute-done | bytes 1179680 | tf_op jit(solution)/shard_map/ppermute | solution.py:233
  766.6 31.3 %collective-permute-done.5 = bf16[256,2304]{1,0:T(8,128)(2,1)S(1)} collective-permute-done((bf16[256,2304]{1,0:T(8,128)(2,1)S(1)}, bf16[256,2304]{1,0:T(8,128)(2,1)S(1)}, u32[]{:S(2)}, u32[]{:S(2)}) %collective-permute-start.5) | collective-permute-done | bytes 1179680 | tf_op jit(solution)/shard_map/ppermute | solution.py:241
  (171 shorter events, 37.8 us)
Async XLA Ops:
  7.4 130.9 %copy-start = (f32[9216]{0:T(1024)S(1)}, f32[9216]{0:T(1024)}, u32[]{:S(2)}) copy-start(f32[9216]{0:T(1024)} %param.21) | copy-start | bytes 110596
  7.4 8.3 %copy-start.17 = (s32[1,1,101]{2,1,0:T(1,128)S(1)}, s32[1,1,101]{2,1,0:T(1,128)}, u32[]{:S(2)}) copy-start(s32[1,1,101]{2,1,0:T(1,128)} %param.19) | copy-start | bytes 1216
  7.4 8.3 %copy-start.13 = (s32[1,1,101]{2,1,0:T(1,128)S(1)}, s32[1,1,101]{2,1,0:T(1,128)}, u32[]{:S(2)}) copy-start(s32[1,1,101]{2,1,0:T(1,128)} %param.23) | copy-start | bytes 1216
  10.2 130.8 %collective-permute-start = (bf16[256,4608]{0,1:T(8,128)(2,1)S(1)}, bf16[256,4608]{0,1:T(8,128)(2,1)}, u32[]{:S(2)}, u32[]{:S(2)}) collective-permute-start(bf16[256,4608]{0,1:T(8,128)(2,1)S(1)} %copy.58), channel_id=1, source_target_pairs={{0,16},{2,18},{4,20},{6,22},{8,24},{10,26},{12,28},{14,30},{16,0},... | collective-permute-start | bytes 7077896 | tf_op jit(solution)/shard_map/ppermute | solution.py:161
  130.8 8.2 %copy-start.15 = (s32[1,1,101]{2,1,0:T(1,128)}, s32[1,1,101]{2,1,0:T(1,128)S(1)}, u32[]{:S(2)}) copy-start(s32[1,1,101]{2,1,0:T(1,128)S(1)} %get-tuple-element.306) | copy-start | bytes 1216
  141.1 4.7 copy-start.11
  141.1 4.7 copy-start.12
  163.3 6.8 copy-start.3
  163.3 6.8 copy-start.23
  170.1 163.6 %all-gather.20.cloned.1.call-start = ((), (), s32[]{:S(2)}) async-start(), calls=%async_computation.4 | async-start | bytes 18874368 | tf_op jit(solution)/shard_map/all_gather | solution.py:157
  170.7 247.0 %all-gather.16.cloned.1.call-start = ((), (), s32[]{:S(2)}) async-start(), calls=%async_computation.2 | async-start | bytes 18874368 | tf_op jit(solution)/shard_map/all_gather | solution.py:157
  171.0 128.0 %copy-start.18 = (pred[16,101]{1,0:T(8,128)(4,1)S(1)}, pred[16,101]{1,0:T(8,128)(4,1)}, u32[]{:S(2)}) copy-start(pred[16,101]{1,0:T(8,128)(4,1)} %get-tuple-element.336) | copy-start | bytes 4852
  171.0 132.5 %copy-start.22 = (pred[101,1]{0,1:T(4,128)(4,1)S(1)}, pred[101,1]{0,1:T(4,128)(4,1)}, u32[]{:S(2)}) copy-start(pred[101,1]{0,1:T(4,128)(4,1)} %get-tuple-element.350) | copy-start | bytes 307
  171.0 132.7 %copy-start.16 = (s32[1,1,101]{2,1,0:T(1,128)S(1)}, s32[1,1,101]{2,1,0:T(1,128)}, u32[]{:S(2)}) copy-start(s32[1,1,101]{2,1,0:T(1,128)} %copy-done.15) | copy-start | bytes 1216
  173.2 136.9 %copy-start.4 = (bf16[1,1,101,128,128]{4,3,2,1,0:T(8,128)(2,1)S(1)}, bf16[1,1,101,128,128]{4,3,2,1,0:T(8,128)(2,1)}, u32[]{:S(2)}) copy-start(bf16[1,1,101,128,128]{4,3,2,1,0:T(8,128)(2,1)} %param.22) | copy-start | bytes 9928708
  173.2 125.5 %collective-permute-start.1 = (bf16[1,1,64,128,128]{4,3,2,1,0:T(8,128)(2,1)}, bf16[1,1,64,128,128]{4,3,2,1,0:T(8,128)(2,1)}, u32[]{:S(2)}, u32[]{:S(2)}) collective-permute-start(bf16[1,1,64,128,128]{4,3,2,1,0:T(8,128)(2,1)} %bitcast.100), channel_id=1, source_target_pairs={{0,16},{2,18},{4,20},{6,22},{8,24},{10,26},{12,28},{14,30},{16,0},... | collective-permute-start | bytes 6291464 | tf_op jit(solution)/shard_map/ppermute | solution.py:154
  305.4 8.2 %copy-start.20 = (s32[101]{0:T(128)S(1)}, s32[101]{0:T(128)}, u32[]{:S(2)}) copy-start(s32[101]{0:T(128)} %reduce.6) | copy-start | bytes 1216
  305.4 8.2 %copy-start.21 = (s32[101]{0:T(128)S(1)}, s32[101]{0:T(128)}, u32[]{:S(2)}) copy-start(s32[101]{0:T(128)} %reduce.5) | copy-start | bytes 1216
  456.9 7.7 copy-start.19
  469.4 129.1 %all-gather.22.cloned.1.call-start = ((), (), s32[]{:S(2)}) async-start(), calls=%async_computation.5 | async-start | bytes 18874368 | tf_op jit(solution)/shard_map/all_gather | solution.py:157
  470.0 211.7 %all-gather.18.cloned.1.call-start = ((), (), s32[]{:S(2)}) async-start(), calls=%async_computation.3 | async-start | bytes 18874368 | tf_op jit(solution)/shard_map/all_gather | solution.py:157
  470.3 97.5 %copy-start.10 = (s32[16,64]{1,0:T(8,128)S(1)}, s32[16,64]{1,0:T(8,128)}, u32[]{:S(2)}) copy-start(s32[16,64]{1,0:T(8,128)} %get-tuple-element.364) | copy-start | bytes 12292
  470.3 98.2 %copy-start.9 = (s32[16,64]{1,0:T(8,128)S(1)}, s32[16,64]{1,0:T(8,128)}, u32[]{:S(2)}) copy-start(s32[16,64]{1,0:T(8,128)} %get-tuple-element.363) | copy-start | bytes 12292
  472.4 94.0 %collective-permute-start.2 = (bf16[1,1,64,128,128]{4,3,2,1,0:T(8,128)(2,1)}, bf16[1,1,64,128,128]{4,3,2,1,0:T(8,128)(2,1)S(1)}, u32[]{:S(2)}, u32[]{:S(2)}) collective-permute-start(bf16[1,1,64,128,128]{4,3,2,1,0:T(8,128)(2,1)} %bitcast.101), channel_id=1, source_target_pairs={{0,16},{2,18},{4,20},{6,22},{8,24},{10,26},{12,28},{14,30},{16,0},... | collective-permute-start | bytes 6291464 | tf_op jit(solution)/shard_map/ppermute | solution.py:154
  709.9 29.3 %collective-permute-start.4 = (bf16[256,2304]{1,0:T(8,128)(2,1)S(1)}, bf16[256,2304]{1,0:T(8,128)(2,1)S(1)}, u32[]{:S(2)}, u32[]{:S(2)}) collective-permute-start(bf16[256,2304]{1,0:T(8,128)(2,1)S(1)} %constant_dynamic-slice_fusion.3), channel_id=1, source_target_pairs={{0,1},{1,0},{2,3},{3,2},{4,5},{5,4},{6,7},{7,6},{8,9},{9,8},{10,11... | collective-permute-start | bytes 3538952 | tf_op jit(solution)/shard_map/ppermute | solution.py:233
  710.0 29.1 %copy-start.7 = (bf16[256,4608]{1,0:T(8,128)(2,1)S(1)}, bf16[256,4608]{1,0:T(8,128)(2,1)}, u32[]{:S(2)}) copy-start(bf16[256,4608]{1,0:T(8,128)(2,1)} %shard_map.113) | copy-start | bytes 7077892
  737.0 60.9 %copy-start.6 = (bf16[256,4608]{1,0:T(8,128)(2,1)S(1)}, bf16[256,4608]{1,0:T(8,128)(2,1)}, u32[]{:S(2)}) copy-start(bf16[256,4608]{1,0:T(8,128)(2,1)} %shard_map.112) | copy-start | bytes 7077892
  738.5 59.4 %copy-start.5 = (bf16[256,4608]{1,0:T(8,128)(2,1)S(1)}, bf16[256,4608]{1,0:T(8,128)(2,1)}, u32[]{:S(2)}) copy-start(bf16[256,4608]{1,0:T(8,128)(2,1)} %param.15) | copy-start | bytes 7077892
  738.5 59.4 %copy-start.14 = (f32[2304]{0:T(1024)S(1)}, f32[2304]{0:T(1024)}, u32[]{:S(2)}) copy-start(f32[2304]{0:T(1024)} %param.25) | copy-start | bytes 27652
  738.5 28.1 %collective-permute-start.3 = (bf16[256,2304]{1,0:T(8,128)(2,1)S(1)}, bf16[256,2304]{1,0:T(8,128)(2,1)S(1)}, u32[]{:S(2)}, u32[]{:S(2)}) collective-permute-start(bf16[256,2304]{1,0:T(8,128)(2,1)S(1)} %constant_dynamic-slice_fusion), channel_id=1, source_target_pairs={{0,1},{1,0},{2,3},{3,2},{4,5},{5,4},{6,7},{7,6},{8,9},{9,8},{10,11... | collective-permute-start | bytes 3538952 | tf_op jit(solution)/shard_map/ppermute | solution.py:233
  739.2 60.5 %copy-start.1 = (f32[9216]{0:T(1024)S(1)}, f32[9216]{0:T(1024)}, u32[]{:S(2)}) copy-start(f32[9216]{0:T(1024)} %param.21) | copy-start | bytes 110596
  739.4 58.5 %collective-permute-start.5 = (bf16[256,2304]{1,0:T(8,128)(2,1)S(1)}, bf16[256,2304]{1,0:T(8,128)(2,1)S(1)}, u32[]{:S(2)}, u32[]{:S(2)}) collective-permute-start(bf16[256,2304]{1,0:T(8,128)(2,1)S(1)} %add_convert_fusion.1), channel_id=1, source_target_pairs={{0,16},{2,18},{4,20},{6,22},{8,24},{10,26},{12,28},{14,30},{16,0},... | collective-permute-start | bytes 3538952 | tf_op jit(solution)/shard_map/ppermute | solution.py:241
  (3 other events, 6.6 us)
Sparse Core Ops, SparseCore 1:
  172.2 161.5 all-gather.19
  335.2 82.4 all-gather.15
  471.5 127.0 all-gather.21
  600.1 81.5 all-gather.17

commit v2 on v0

v2 whole, which is shorter than its diff:
```python
import functools

import jax
import jax.numpy as jnp
from jax import lax
from jax.experimental import pallas as pl
from jax.experimental.pallas import tpu as pltpu
from jax.sharding import PartitionSpec as P

UNROLL = 4
VMEM_BYTES = 56 * 1024 * 1024


def add_tiles(row_ref, col_ref, live, base, x_ref, w_ref, acc):
    def one(slot):
        row, col = row_ref[base + slot], col_ref[base + slot]
        return col, jnp.dot(x_ref[row], w_ref[0, 0, slot], preferred_element_type=jnp.float32)

    def several(step, carry):
        products = [one(step * UNROLL + u) for u in range(UNROLL)]
        for col, product in products:
            acc[col] += product
        return carry

    def single(slot, carry):
        col, product = one(slot)
        acc[col] += product
        return carry

    whole = lax.div(live, jnp.int32(UNROLL))
    lax.fori_loop(0, whole, several, 0)
    lax.fori_loop(whole * UNROLL, live, single, 0)


def second_kernel(row_ref, col_ref, count_ref, x_ref, sum_ref, w_ref, out_ref, acc):
    step = pl.program_id(0)
    blocks = acc.shape[0]

    @pl.when(step == 0)
    def _():
        acc[...] = sum_ref[...]

    add_tiles(row_ref, col_ref, count_ref[step], step * w_ref.shape[2], x_ref, w_ref, acc)

    @pl.when(step == pl.num_programs(0) - 1)
    def _():
        if out_ref.dtype == jnp.float32:
            out_ref[...] = acc[...]
        elif len(out_ref.shape) == 3:
            for c in range(blocks):
                out_ref[c] = jnp.maximum(acc[c], 0.0).astype(out_ref.dtype)
        else:
            width = acc.shape[2]
            for c in range(blocks):
                out_ref[:, c * width : (c + 1) * width] = acc[c].astype(out_ref.dtype)


def whole_block(shape):
    return pl.BlockSpec(shape, lambda i, *_: (0,) * len(shape))


def tile_pass(kernel, rows, cols, counts, x, start, tiles, out_shape, blocks):
    shards, slots, side = tiles.shape[0], tiles.shape[2], tiles.shape[3]
    tokens = x.shape[1]
    return pl.pallas_call(
        kernel,
        out_shape=out_shape,
        grid_spec=pltpu.PrefetchScalarGridSpec(
            num_scalar_prefetch=3,
            grid=(shards,),
            in_specs=[
                whole_block(x.shape),
                whole_block(start.shape),
                pl.BlockSpec((1, 1, slots, side, side), lambda i, *_: (i, 0, 0, 0, 0)),
            ],
            out_specs=whole_block(out_shape.shape),
            scratch_shapes=[pltpu.VMEM((blocks, tokens, side), jnp.float32)],
        ),
        compiler_params=pltpu.CompilerParams(vmem_limit_bytes=VMEM_BYTES),
        cost_estimate=pl.CostEstimate(
            flops=8 * shards * slots * tokens * side * side,
            bytes_accessed=shards * slots * side * side * 2,
            transcendentals=0,
        ),
    )(rows.reshape(-1), cols.reshape(-1), counts, x, start, tiles)


def on_device(
    tokens,
    ln_gain,
    ln_bias,
    fc1_tiles,
    fc1_index,
    fc1_count,
    fc1_bias,
    fc2_tiles,
    fc2_index,
    fc2_count,
    fc2_bias,
    blk_size,
    ffn_size,
):
    side = fc1_tiles.shape[-1]
    slots = fc1_tiles.shape[2]
    token_rows, width = tokens.shape
    first_blocks = fc1_bias.shape[0] // side
    second_blocks = width // side
    both = ("blk", "ffn")
    part_size = blk_size // ffn_size
    blk, ffn = lax.axis_index("blk"), lax.axis_index("ffn")
    part = lax.div(blk, part_size)

    def device(h, j, f):
        return (h * part_size + j) * ffn_size + f

    ids = [(h, j, f) for h in range(ffn_size) for j in range(part_size) for f in range(ffn_size)]
    swap = [(device(h, j, f), device(f, j, h)) for h, j, f in ids]
    parts = [[device(h, j, f) for j in range(part_size) for f in range(ffn_size)] for h in range(ffn_size)]

    def swapped(value):
        return lax.ppermute(value, both, swap)

    def gathered(value):
        return lax.all_gather(value, both, axis=0, axis_index_groups=parts, tiled=True)

    meta = jnp.concatenate([fc1_index[:, 0], fc2_index[:, 0], fc1_count, fc2_count], axis=1)
    meta = gathered(swapped(meta))
    index1, index2 = meta[:, :slots], meta[:, slots : 2 * slots]
    count1, count2 = meta[:, 2 * slots], meta[:, 2 * slots + 1]

    cuts1 = [0, slots // 2, slots]
    cuts2 = [0, slots // 2, slots]
    tiles1 = [gathered(swapped(fc1_tiles[:, :, lo:hi])) for lo, hi in zip(cuts1[:-1], cuts1[1:])]
    tiles2 = [gathered(swapped(fc2_tiles[:, :, lo:hi])) for lo, hi in zip(cuts2[:-1], cuts2[1:])]

    rows_f = swapped(tokens).astype(jnp.float32)
    center = jnp.mean(rows_f, axis=1, keepdims=True)
    spread = jnp.mean((rows_f - center) ** 2, axis=1, keepdims=True)
    normed = ((rows_f - center) / jnp.sqrt(spread + 1e-05) * ln_gain + ln_bias).astype(jnp.bfloat16)
    normed_blocks = normed.reshape(token_rows, second_blocks, side).transpose(1, 0, 2)

    def passes(x, total, tiles, cuts, index, counts, blocks, last_shape):
        for number, (lo, hi) in enumerate(zip(cuts[:-1], cuts[1:])):
            last = number == len(tiles) - 1
            total = tile_pass(
                second_kernel,
                index[:, lo:hi] // blocks,
                index[:, lo:hi] % blocks,
                jnp.clip(counts - lo, 0, hi - lo),
                x,
                total,
                tiles[number],
                last_shape if last else jax.ShapeDtypeStruct(total.shape, jnp.float32),
                blocks,
            )
        return total

    bias = swapped(fc1_bias).reshape(first_blocks, 1, side)
    total = jnp.broadcast_to(bias, (first_blocks, token_rows, side))
    hidden = passes(
        normed_blocks, total, tiles1, cuts1, index1, count1, first_blocks,
        jax.ShapeDtypeStruct(total.shape, jnp.bfloat16),
    )
    total = jnp.zeros((second_blocks, token_rows, side), jnp.float32)
    partial_value = passes(
        hidden, total, tiles2, cuts2, index2, count2, second_blocks,
        jax.ShapeDtypeStruct((token_rows, width), jnp.bfloat16),
    )

    share = width // ffn_size
    branch = jnp.zeros((token_rows, share), jnp.float32)
    for shift in range(ffn_size):
        to = lax.rem(part + shift, ffn_size)
        piece = lax.dynamic_slice_in_dim(partial_value, to * share, share, 1)
        route = [(device(h, j, f), device(f, j, (h + shift) % ffn_size)) for h, j, f in ids]
        branch = branch + lax.ppermute(piece, both, route).astype(jnp.float32)
    own_cols = lax.dynamic_slice_in_dim(tokens, ffn * share, share, 1).astype(jnp.float32)
    return (own_cols + branch + fc2_bias).astype(jnp.bfloat16)


def solution(mesh):
    placed = (
        P("blk", None),
        P(),
        P(),
        P("blk", "ffn", None, None, None),
        P("blk", "ffn", None),
        P("blk", "ffn"),
        P("ffn"),
        P("blk", "ffn", None, None, None),
        P("blk", "ffn", None),
        P("blk", "ffn"),
        P("ffn"),
    )
    return jax.shard_map(
        functools.partial(on_device, blk_size=mesh.shape["blk"], ffn_size=mesh.shape["ffn"]),
        mesh=mesh,
        in_specs=placed,
        out_specs=P("blk", "ffn"),
        check_vma=False,
    )
```

time: 641 us -> 1010 us (1.58)
  blocking collectives: 23.1 us -> 430 us
  waiting for transfers between devices: 370 us -> 314 us
  starting transfers between devices: 0.53 us -> 19.3 us
    all_gather x1, blocking collectives: 23.1 us -> 430 us  [gathered(): lax.all_gather(value, both, axis=0, axis_index_groups=parts, tiled=True)]
    all_gather x4, waiting for transfers between devices: 344 us -> 213 us  [gathered(): lax.all_gather(value, both, axis=0, axis_index_groups=parts, tiled=True)]
    ppermute x1 -> x9, waiting for transfers between devices: 25.2 us -> 101 us  [the longest x2 101 us: on_device(): branch = branch + lax.ppermute(piece, both, route).astype(jnp.float32)]
    ppermute x1 -> x9, starting transfers between devices: 0.41 us -> 19.2 us  [the longest x2 10.4 us: on_device(): branch = branch + lax.ppermute(piece, both, route).astype(jnp.float32)]
  transfers between devices with their start and end apart: 5 -> 13, of which waited for: 5 -> 4; matrix products, arithmetic and copies ran while one was open for 5% -> 3% of each run, Pallas kernels for 28% -> 16%
where the time goes in v2:
time: 1010 us
  blocking collectives  430 us (43%)
  waiting for transfers between devices  314 us (31%)
  Pallas kernels  197 us (20%)
  local copies, waits for them, and re-layouts  29.4 us (3%)
  starting transfers between devices  19.3 us (2%)
  between operations  14.7 us (1%)
    all_gather x1, blocking collectives, gathered(): lax.all_gather(value, both, axis=0, axis_index_groups=parts, tiled=True)  430 us
    all_gather x4, waiting for transfers between devices, gathered(): lax.all_gather(value, both, axis=0, axis_index_groups=parts, tiled=True)  213 us
    pallas_call x4, Pallas kernels, tile_pass(): pl.pallas_call(kernel, out_shape=out_shape, grid_spec=pltpu.PrefetchScala...  197 us
    ppermute x2, waiting for transfers between devices, on_device(): branch = branch + lax.ppermute(piece, both, route).astype(jnp.float32)  101 us
  transfers between devices with their start and end apart: 13, of which 4 were waited for; matrix products, arithmetic and copies ran while one was open for 3% of the time, Pallas kernels for 16%

profile of v2, /device:TPU:0, one launch (start us, length us, event | category | flops | bytes accessed | tf_op | source)
XLA Modules:
  0.0 1014.0 jit_solution(15499747613768702435)
XLA Ops:
  6.5 1.7 slice.45
  8.2 1.8 collective-permute-start.3
  10.3 0.8 collective-permute-start.4
  11.1 1.2 copy-done.3
  12.3 1.5 slice.48
  13.8 0.8 collective-permute-start.5
  14.6 1.2 copy-done.4
  15.9 1.7 slice.49
  17.6 1.8 collective-permute-start.6
  19.6 2.5 copy.16
  22.0 2.3 collective-permute-start.1
  27.1 430.2 %all-gather = s32[16,1,204]{2,1,0:T(1,128)S(1)} all-gather(s32[1,1,204]{2,1,0:T(1,128)S(1)} %bitcast.19), channel_id=1, replica_groups={{0,1,2,3,4,5,6,7,8,9,10,11,12,13,14,15},{16,17,18,19,20,21,22,23,24,25,..., dimensions={0}, use_global_device_ids=true | all-gather | bytes 13872 | tf_op jit(solution)/shard_map/all_gather | solution.py:124
  459.0 0.7 reshape.62.row_ref
  461.1 0.7 reshape.68.col_ref
  461.8 0.7 reshape.60.row_ref
  462.5 0.7 reshape.61.col_ref
  463.2 0.8 clamp_reduce_fusion
  465.3 3.5 fusion.5
  468.7 4.3 copy.17
  473.1 4.1 broadcast_in_dim.7.sum_ref
  477.2 59.7 %shard_map.109.sum_ref = f32[72,256,128]{2,1,0:T(8,128)} custom-call(s32[800]{0:T(1024)} %reshape.65.row_ref, s32[800]{0:T(1024)} %reshape.66.col_ref, s32[16]{0:T(128)} %get-tuple-element.6.count_ref, bf16[36,256,128]{2,1,0:T(8,128)(2,1)} %bitcast.10, f32[72,256,128]{2,1,0:T(8,128)} %broadcast_in_dim.7.sum_ref, ...), custom_call_target="tpu_custom_call" | custom-call | flops 26843545600 | bytes 26214400 | tf_op jit(solution)/shard_map/pallas_call | solution.py:65
  536.9 29.5 %all-gather.8.cloned.1.call-done.w_ref = bf16[16,1,51,128,128]{4,3,2,1,0:T(8,128)(2,1)} async-done(((bf16[1,1,51,128,128]{4,3,2,1,0:T(8,128)(2,1)}), bf16[16,1,51,128,128]{4,3,2,1,0:T(8,128)(2,1)}) %all-gather.8.cloned.1.call-update) | async-done | bytes 26738704 | tf_op jit(solution)/shard_map/all_gather | solution.py:124
  566.5 43.0 %shard_map.110.x_ref = bf16[72,256,128]{2,1,0:T(8,128)(2,1)} custom-call(s32[816]{0:T(1024)} %reshape.62.row_ref, s32[816]{0:T(1024)} %reshape.63.col_ref, s32[16]{0:T(128)} %get-tuple-element.7.count_ref, bf16[36,256,128]{2,1,0:T(8,128)(2,1)} %bitcast.11, f32[72,256,128]{2,1,0:T(8,128)} %shard_map.109.sum_ref, ...), custom_call_target="tpu_custom_call" | custom-call | flops 27380416512 | bytes 26738688 | tf_op jit(solution)/shard_map/pallas_call | solution.py:65
  609.5 98.2 %all-gather.10.cloned.1.call-done.w_ref = bf16[16,1,50,128,128]{4,3,2,1,0:T(8,128)(2,1)} async-done(((bf16[1,1,50,128,128]{4,3,2,1,0:T(8,128)(2,1)}), bf16[16,1,50,128,128]{4,3,2,1,0:T(8,128)(2,1)}) %all-gather.10.cloned.1.call-update) | async-done | bytes 26214416 | tf_op jit(solution)/shard_map/all_gather | solution.py:124
  707.7 2.7 broadcast_in_dim.8.sum_ref
  710.4 56.9 %shard_map.111.sum_ref = f32[36,256,128]{2,1,0:T(8,128)} custom-call(s32[800]{0:T(1024)} %reshape.67.row_ref, s32[800]{0:T(1024)} %reshape.68.col_ref, s32[16]{0:T(128)} %get-tuple-element.5.count_ref, bf16[72,256,128]{2,1,0:T(8,128)(2,1)} %shard_map.110.x_ref, f32[36,256,128]{2,1,0:T(8,128)} %broadcast_in_dim.8.sum_ref, ...), custom_call_target="tpu_custom_call" | custom-call | flops 26843545600 | bytes 26214400 | tf_op jit(solution)/shard_map/pallas_call | solution.py:65
  767.2 85.5 %all-gather.12.cloned.1.call-done.w_ref = bf16[16,1,51,128,128]{4,3,2,1,0:T(8,128)(2,1)} async-done(((bf16[1,1,51,128,128]{4,3,2,1,0:T(8,128)(2,1)}), bf16[16,1,51,128,128]{4,3,2,1,0:T(8,128)(2,1)}) %all-gather.12.cloned.1.call-update) | async-done | bytes 26738704 | tf_op jit(solution)/shard_map/all_gather | solution.py:124
  852.8 37.2 %shard_map.112 = bf16[256,4608]{1,0:T(8,128)(2,1)} custom-call(s32[816]{0:T(1024)} %reshape.60.row_ref, s32[816]{0:T(1024)} %reshape.61.col_ref, s32[16]{0:T(128)} %get-tuple-element.8.count_ref, bf16[72,256,128]{2,1,0:T(8,128)(2,1)} %shard_map.110.x_ref, f32[36,256,128]{2,1,0:T(8,128)} %shard_map.111.sum_ref, ...), custom_call_target="tpu_custom_call" | custom-call | flops 27380416512 | bytes 26738688 | tf_op jit(solution)/shard_map/pallas_call | solution.py:65
  890.0 2.9 constant_dynamic-slice_fusion.1
  892.9 10.4 %collective-permute-start.7 = (bf16[256,2304]{1,0:T(8,128)(2,1)}, bf16[256,2304]{1,0:T(8,128)(2,1)}, u32[]{:S(2)}, u32[]{:S(2)}) collective-permute-start(bf16[256,2304]{1,0:T(8,128)(2,1)} %get-tuple-element.17), channel_id=1, source_target_pairs={{0,0},{1,16},{2,2},{3,18},{4,4},{5,20},{6,6},{7,22},{8,8},{9,24},{... | collective-permute-start | bytes 3538952 | tf_op jit(solution)/shard_map/ppermute | solution.py:176
  903.3 101.0 %collective-permute-done.8 = bf16[256,2304]{1,0:T(8,128)(2,1)} collective-permute-done((bf16[256,2304]{1,0:T(8,128)(2,1)S(1)}, bf16[256,2304]{1,0:T(8,128)(2,1)}, u32[]{:S(2)}, u32[]{:S(2)}) %collective-permute-start.8) | collective-permute-done | bytes 1179680 | tf_op jit(solution)/shard_map/ppermute | solution.py:176
  1004.3 3.1 add_convert_fusion
  (56 shorter events, 6.2 us)
Async XLA Ops:
  6.5 3.6 copy-start.2
  6.5 466.6 %all-gather.6.cloned.1.call-start = ((), (), s32[]{:S(2)}) async-start(), calls=%async_computation | async-start | bytes 27852800 | tf_op jit(solution)/shard_map/all_gather | solution.py:124
  8.2 1.8 collective-permute-start.3
  10.1 556.4 %all-gather.8.cloned.1.call-start = ((), (), s32[]{:S(2)}) async-start(), calls=%async_computation.1 | async-start | bytes 28409856 | tf_op jit(solution)/shard_map/all_gather | solution.py:124
  10.3 0.8 collective-permute-start.4
  11.0 1.2 copy-start.3
  12.2 695.4 %all-gather.10.cloned.1.call-start = ((), (), s32[]{:S(2)}) async-start(), calls=%async_computation.2 | async-start | bytes 27852800 | tf_op jit(solution)/shard_map/all_gather | solution.py:124
  13.8 0.8 collective-permute-start.5
  14.6 1.2 copy-start.4
  15.9 3.6 copy-start
  15.9 836.9 %all-gather.12.cloned.1.call-start = ((), (), s32[]{:S(2)}) async-start(), calls=%async_computation.3 | async-start | bytes 28409856 | tf_op jit(solution)/shard_map/all_gather | solution.py:124
  17.6 1.8 collective-permute-start.6
  19.5 6.1 copy-start.8
  19.5 6.1 copy-start.9
  19.6 6.8 copy-start.10
  22.0 441.9 %collective-permute-start.1 = (bf16[256,4608]{0,1:T(8,128)(2,1)}, bf16[256,4608]{0,1:T(8,128)(2,1)S(1)}, u32[]{:S(2)}, u32[]{:S(2)}) collective-permute-start(bf16[256,4608]{0,1:T(8,128)(2,1)} %copy.16), channel_id=1, source_target_pairs={{0,0},{1,16},{2,2},{3,18},{4,4},{5,20},{6,6},{7,22},{8,8},{9,24},{... | collective-permute-start | bytes 7077896 | tf_op jit(solution)/shard_map/ppermute | solution.py:121
  25.7 1.4 collective-permute-start
  26.4 446.7 %collective-permute-start.2 = (f32[9216]{0:T(1024)S(1)}, f32[9216]{0:T(1024)S(1)}, u32[]{:S(2)}, u32[]{:S(2)}) collective-permute-start(f32[9216]{0:T(1024)S(1)} %copy-done.10), channel_id=1, source_target_pairs={{0,0},{1,16},{2,2},{3,18},{4,4},{5,20},{6,6},{7,22},{8,8},{9,24},{... | collective-permute-start | bytes 110600 | tf_op jit(solution)/shard_map/ppermute | solution.py:121
  464.0 1.3 copy-start.5
  464.0 1.3 copy-start.6
  890.0 114.3 %copy-start.1 = (bf16[256,4608]{1,0:T(8,128)(2,1)S(1)}, bf16[256,4608]{1,0:T(8,128)(2,1)}, u32[]{:S(2)}) copy-start(bf16[256,4608]{1,0:T(8,128)(2,1)} %param.11) | copy-start | bytes 7077892
  890.0 114.3 %copy-start.7 = (f32[2304]{0:T(1024)S(1)}, f32[2304]{0:T(1024)}, u32[]{:S(2)}) copy-start(f32[2304]{0:T(1024)} %param.21) | copy-start | bytes 27652
  892.9 10.4 %collective-permute-start.7 = (bf16[256,2304]{1,0:T(8,128)(2,1)}, bf16[256,2304]{1,0:T(8,128)(2,1)}, u32[]{:S(2)}, u32[]{:S(2)}) collective-permute-start(bf16[256,2304]{1,0:T(8,128)(2,1)} %get-tuple-element.17), channel_id=1, source_target_pairs={{0,0},{1,16},{2,2},{3,18},{4,4},{5,20},{6,6},{7,22},{8,8},{9,24},{... | collective-permute-start | bytes 3538952 | tf_op jit(solution)/shard_map/ppermute | solution.py:176
  903.3 101.0 %collective-permute-start.8 = (bf16[256,2304]{1,0:T(8,128)(2,1)S(1)}, bf16[256,2304]{1,0:T(8,128)(2,1)}, u32[]{:S(2)}, u32[]{:S(2)}) collective-permute-start(bf16[256,2304]{1,0:T(8,128)(2,1)S(1)} %get-tuple-element.18), channel_id=1, source_target_pairs={{0,1},{1,17},{2,3},{3,19},{4,5},{5,21},{6,7},{7,23},{8,9},{9,25},{... | collective-permute-start | bytes 3538952 | tf_op jit(solution)/shard_map/ppermute | solution.py:176
Sparse Core Ops, SparseCore 0:
  10.2 324.5 all-gather.5
  336.4 230.0 all-gather.7
  568.0 139.6 all-gather.9
  709.1 143.6 all-gather.11

commit v3 on v0

v3 whole, which is shorter than its diff:
```python
import functools

import jax
import jax.numpy as jnp
from jax import lax
from jax.experimental import pallas as pl
from jax.experimental.pallas import tpu as pltpu
from jax.sharding import PartitionSpec as P

UNROLL = 4
VMEM_BYTES = 56 * 1024 * 1024


def add_tiles(row_ref, col_ref, first, last, base, x_ref, w_ref, acc):
    def one(slot):
        row, col = row_ref[base + slot], col_ref[base + slot]
        acc[col] += jnp.dot(x_ref[row], w_ref[0, 0, slot], preferred_element_type=jnp.float32)

    def several(step, carry):
        for u in range(UNROLL):
            one(first + step * UNROLL + u)
        return carry

    def single(slot, carry):
        one(slot)
        return carry

    whole = lax.div(jnp.maximum(last - first, 0), jnp.int32(UNROLL))
    lax.fori_loop(0, whole, several, 0)
    lax.fori_loop(first + whole * UNROLL, last, single, 0)


def add_block(row_ref, col_ref, first_ref, last_ref, x_ref, w_ref, acc):
    step = pl.program_id(0)
    base = step * w_ref.shape[2]
    add_tiles(row_ref, col_ref, first_ref[step], last_ref[step], base, x_ref, w_ref, acc)


def at_end(work):
    pl.when(pl.program_id(0) == pl.num_programs(0) - 1)(work)


def hidden_kernel(row_ref, col_ref, first_ref, last_ref, at_ref, x_ref, w_ref, bias_ref, out_ref, acc):
    blocks = acc.shape[0]

    @pl.when(pl.program_id(0) == 0)
    def _():
        def fill(c, carry):
            acc[c] = jnp.broadcast_to(bias_ref[c], acc.shape[1:])
            return carry

        lax.fori_loop(0, blocks, fill, 0)

    add_block(row_ref, col_ref, first_ref, last_ref, x_ref, w_ref, acc)

    @at_end
    def _():
        def finish(c, carry):
            out_ref[c] = jnp.maximum(acc[c], 0.0).astype(out_ref.dtype)
            return carry

        lax.fori_loop(0, blocks, finish, 0)


def partial_kernel(row_ref, col_ref, first_ref, last_ref, at_ref, x_ref, w_ref, sum_ref, out_ref, acc):
    @pl.when(pl.program_id(0) == 0)
    def _():
        acc[...] = jnp.zeros_like(acc)

    add_block(row_ref, col_ref, first_ref, last_ref, x_ref, w_ref, acc)

    @at_end
    def _():
        width = acc.shape[2]
        sum_ref[...] = acc[...]
        for c in range(acc.shape[0]):
            out_ref[:, c * width : (c + 1) * width] = acc[c].astype(out_ref.dtype)


def result_kernel(
    row_ref, col_ref, first_ref, last_ref, at_ref,
    x_ref, w_ref, sum_ref, token_ref, other_ref, bias_ref, out_ref, acc,
):
    @pl.when(pl.program_id(0) == 0)
    def _():
        acc[...] = sum_ref[...]

    add_block(row_ref, col_ref, first_ref, last_ref, x_ref, w_ref, acc)

    @at_end
    def _():
        width = acc.shape[2]
        for c in range(acc.shape[0]):
            cols = slice(c * width, (c + 1) * width)
            branch = acc[c] + other_ref[:, cols]
            value = token_ref[:, cols].astype(jnp.float32) + branch + bias_ref[:, cols]
            out_ref[:, cols] = value.astype(out_ref.dtype)


def fixed(shape):
    return pl.BlockSpec(shape, lambda i, *_: (0,) * len(shape))


def tile_pass(kernel, rows, cols, first, last, at, x, tiles, more, more_specs, out_shapes, blocks):
    shards, slots, side = tiles.shape[0], tiles.shape[2], tiles.shape[3]
    tokens = x.shape[1]
    out_specs = [fixed(o.shape) for o in out_shapes]
    return pl.pallas_call(
        kernel,
        out_shape=out_shapes,
        grid_spec=pltpu.PrefetchScalarGridSpec(
            num_scalar_prefetch=5,
            grid=(shards,),
            in_specs=[
                fixed(x.shape),
                pl.BlockSpec((1, 1, slots, side, side), lambda i, *_: (i, 0, 0, 0, 0)),
                *more_specs,
            ],
            out_specs=out_specs,
            scratch_shapes=[pltpu.VMEM((blocks, tokens, side), jnp.float32)],
        ),
        compiler_params=pltpu.CompilerParams(vmem_limit_bytes=VMEM_BYTES),
        cost_estimate=pl.CostEstimate(
            flops=8 * shards * slots * tokens * side * side,
            bytes_accessed=shards * slots * side * side * 2,
            transcendentals=0,
        ),
    )(rows.reshape(-1), cols.reshape(-1), first, last, at.reshape(1), x, tiles, *more)


def on_device(
    tokens,
    ln_gain,
    ln_bias,
    fc1_tiles,
    fc1_index,
    fc1_count,
    fc1_bias,
    fc2_tiles,
    fc2_index,
    fc2_count,
    fc2_bias,
    ffn_size,
):
    side = fc1_tiles.shape[-1]
    slots = fc1_tiles.shape[2]
    shards = lax.axis_size("blk")
    token_rows, width = tokens.shape
    first_blocks = fc1_bias.shape[0] // side
    second_blocks = width // side
    share = width // ffn_size
    ffn = lax.axis_index("ffn")
    slot_ids = jnp.arange(slots, dtype=jnp.int32)
    aligned = share % side == 0
    early = slots - slots * 7 // 20

    def in_share(index, at):
        if not aligned:
            return jnp.zeros(index.shape, jnp.bool_)
        return index % second_blocks // (share // side) == at

    def ordered(index, count, values):
        live = slot_ids < count[:, None]
        own = in_share(index, ffn)
        other = (live & ~own).astype(jnp.int32)
        mine = (live & own).astype(jnp.int32)
        others = jnp.sum(other, axis=1, keepdims=True)
        place = jnp.where(own, others + jnp.cumsum(mine, axis=1) - 1, jnp.cumsum(other, axis=1) - 1)
        hit = live[:, None, :] & (place[:, None, :] == slot_ids[:, None])
        return jnp.sum(jnp.where(hit, values[:, None, :], 0), axis=2), others[:, 0]

    def gathered(value):
        return lax.all_gather(value, "blk", axis=0, tiled=True)

    tiles1 = gathered(fc1_tiles)
    order, _ = ordered(fc2_index[:, 0], fc2_count[:, 0], slot_ids[None])
    pieces = [
        jnp.take(fc2_tiles[0, 0], part, axis=0, mode="clip")[None, None]
        for part in (order[0, :early], order[0, early:])
    ]
    tiles2a, tiles2b = gathered(pieces[0]), gathered(pieces[1])

    meta = jnp.concatenate([fc1_index[:, 0], fc2_index[:, 0], fc1_count, fc2_count], axis=1)
    meta = lax.all_gather(meta, ("blk", "ffn"), axis=0, tiled=True).reshape(shards, ffn_size, -1)
    all_index2, all_count2 = meta[..., slots : 2 * slots], meta[..., 2 * slots + 1]
    all_other = (slot_ids < all_count2[..., None]) & ~in_share(
        all_index2, jnp.arange(ffn_size, dtype=jnp.int32)[:, None]
    )
    some_late = jnp.any(jnp.sum(all_other.astype(jnp.int32), axis=2) > early)
    meta = lax.dynamic_index_in_dim(meta, ffn, 1, keepdims=False)
    index1, count1, count2 = meta[:, :slots], meta[:, 2 * slots], meta[:, 2 * slots + 1]
    index2, others = ordered(meta[:, slots : 2 * slots], count2, meta[:, slots : 2 * slots])
    none = jnp.zeros_like(count1)

    rows_f = tokens.astype(jnp.float32)
    center = jnp.mean(rows_f, axis=1, keepdims=True)
    spread = jnp.mean((rows_f - center) ** 2, axis=1, keepdims=True)
    normed = ((rows_f - center) / jnp.sqrt(spread + 1e-05) * ln_gain + ln_bias).astype(jnp.bfloat16)
    normed_blocks = normed.reshape(token_rows, second_blocks, side).transpose(1, 0, 2)

    (hidden,) = tile_pass(
        hidden_kernel,
        index1 // first_blocks,
        index1 % first_blocks,
        none,
        count1,
        ffn,
        normed_blocks,
        tiles1,
        [fc1_bias.reshape(first_blocks, 1, side)],
        [fixed((first_blocks, 1, side))],
        [jax.ShapeDtypeStruct((first_blocks, token_rows, side), jnp.bfloat16)],
        first_blocks,
    )

    def second_pass(lo, hi, first, last, tiles):
        return tile_pass(
            partial_kernel,
            index2[:, lo:hi] // second_blocks,
            index2[:, lo:hi] % second_blocks,
            first,
            last,
            ffn,
            hidden,
            tiles,
            [],
            [],
            [
                jax.ShapeDtypeStruct((second_blocks, token_rows, side), jnp.float32),
                jax.ShapeDtypeStruct((token_rows, width), jnp.bfloat16),
            ],
            second_blocks,
        )

    def from_others(partial_value):
        branch = jnp.zeros((token_rows, share), jnp.float32)
        for shift in range(1, ffn_size):
            to = lax.rem(ffn + shift, ffn_size)
            arrived = lax.ppermute(
                lax.dynamic_slice_in_dim(partial_value, to * share, share, 1),
                "ffn",
                [(i, (i + shift) % ffn_size) for i in range(ffn_size)],
            )
            branch = branch + arrived.astype(jnp.float32)
        return branch

    count2a, count2b = jnp.minimum(count2, early), jnp.maximum(count2 - early, 0)
    total, partial_value = second_pass(0, early, none, count2a, tiles2a)

    if not aligned:
        more, late_value = second_pass(early, slots, none, count2b, tiles2b)
        both = total + more
        partial_value = both.transpose(1, 0, 2).reshape(token_rows, width).astype(jnp.bfloat16)
        own = lax.dynamic_slice_in_dim(partial_value, ffn * share, share, 1).astype(jnp.float32)
        own_cols = lax.dynamic_slice_in_dim(rows_f, ffn * share, share, 1)
        return (own_cols + own + from_others(partial_value) + fc2_bias).astype(jnp.bfloat16)

    branch = from_others(partial_value)
    late = jnp.maximum(others - early, 0)

    def with_late(branch, hidden, tiles):
        return branch + from_others(second_pass(early, slots, none, late, tiles)[1])

    branch = lax.cond(some_late, with_late, lambda branch, *_: branch, branch, hidden, tiles2b)
    share_blocks = share // side
    (result,) = tile_pass(
        result_kernel,
        index2[:, early:] // second_blocks,
        index2[:, early:] % second_blocks % share_blocks,
        late,
        count2b,
        ffn,
        hidden,
        tiles2b,
        [total, tokens, branch, fc2_bias.reshape(1, share)],
        [
            pl.BlockSpec((share_blocks, token_rows, side), lambda i, r, c, f, l, at: (at[0], 0, 0)),
            pl.BlockSpec((token_rows, share), lambda i, r, c, f, l, at: (0, at[0])),
            fixed((token_rows, share)),
            fixed((1, share)),
        ],
        [jax.ShapeDtypeStruct((token_rows, share), jnp.bfloat16)],
        share_blocks,
    )
    return result


def solution(mesh):
    placed = (
        P("blk", None),
        P(),
        P(),
        P("blk", "ffn", None, None, None),
        P("blk", "ffn", None),
        P("blk", "ffn"),
        P("ffn"),
        P("blk", "ffn", None, None, None),
        P("blk", "ffn", None),
        P("blk", "ffn"),
        P("ffn"),
    )
    return jax.shard_map(
        functools.partial(on_device, ffn_size=mesh.shape["ffn"]),
        mesh=mesh,
        in_specs=placed,
        out_specs=P("blk", "ffn"),
        check_vma=False,
    )
```

time: 641 us -> 584 us (0.911)
  waiting for transfers between devices: 370 us -> 277 us
  blocking collectives: 23.1 us -> 69.9 us
  Pallas kernels: 194 us -> 184 us
    all_gather x4 -> x3, waiting for transfers between devices: 344 us -> 254 us  [gathered(): return lax.all_gather(value, 'blk', axis=0, tiled=True)]
    all_gather x1, blocking collectives: 23.1 us -> 69.9 us  [on_device(): lax.all_gather(meta, ('blk', 'ffn'), axis=0, tiled=True)]
    pallas_call x4 -> x3, Pallas kernels: 194 us -> 184 us  [tile_pass(): pl.pallas_call(kernel, out_shape=out_shapes, grid_spec=pltpu.PrefetchScal...]
  transfers between devices with their start and end apart: 5 -> 4, of which waited for: 5 -> 3; matrix products, arithmetic and copies ran while one was open for 5% -> 6% of each run, Pallas kernels for 28% -> 27%
where the time goes in v3:
time: 584 us; the launch traced here: 582 us
  waiting for transfers between devices  277 us (47%)
  Pallas kernels  184 us (32%)
  blocking collectives  69.9 us (12%)
  local copies, waits for them, and re-layouts  19.5 us (3%)
  between operations  15.4 us (3%)
  other arithmetic  14.7 us (3%)
    all_gather x3, waiting for transfers between devices, gathered(): return lax.all_gather(value, 'blk', axis=0, tiled=True)  254 us
    pallas_call x3, Pallas kernels, tile_pass(): pl.pallas_call(kernel, out_shape=out_shapes, grid_spec=pltpu.PrefetchScal...  184 us
    all_gather x1, blocking collectives, on_device(): lax.all_gather(meta, ('blk', 'ffn'), axis=0, tiled=True)  69.9 us
    ppermute x1, waiting for transfers between devices, from_others(): lax.ppermute(lax.dynamic_slice_in_dim(partial_value, to * share, share, 1...  22.1 us
  transfers between devices with their start and end apart: 4, of which 3 were waited for; matrix products, arithmetic and copies ran while one was open for 6% of the time, Pallas kernels for 27%

profile of v3, /device:TPU:0, one launch (start us, length us, event | category | flops | bytes accessed | tf_op | source)
XLA Modules:
  0.0 582.3 jit_solution(4415247316041508307)
XLA Ops:
  6.5 0.7 all-gather.7.cloned.1.call-update
  8.7 0.7 fusion.20
  9.4 0.6 select_bitcast_fusion
  10.0 1.9 fusion.9
  12.0 2.4 gather_fusion.1
  14.5 1.8 gather_fusion
  17.1 69.9 %all-gather.2 = s32[32,1,204]{2,1,0:T(1,128)S(1)} all-gather(s32[1,1,204]{2,1,0:T(1,128)S(1)} %add_bitcast_fusion), channel_id=1, replica_groups=mesh['blk'=16,'ffn'=2] {'blk','ffn'}, dimensions={0}, use_global_device_ids=true | all-gather | bytes 26928 | tf_op jit(solution)/shard_map/all_gather | solution.py:184
  87.1 0.7 slice_reduce_fusion
  88.0 0.7 reshape.296.row_ref
  88.7 0.7 reshape.297.col_ref
  89.4 2.8 copy.47
  92.2 0.6 convert_reduce_fusion
  92.9 0.7 fusion.4
  93.6 3.4 fusion.7
  97.0 4.3 copy.48
  102.0 1.8 select_reduce_fusion
  103.9 0.7 reshape.300.row_ref
  104.7 0.7 reshape.301.col_ref
  105.9 165.5 %all-gather.7.cloned.1.call-done.w_ref = bf16[16,1,101,128,128]{4,3,2,1,0:T(8,128)(2,1)} async-done(((bf16[1,1,101,128,128]{4,3,2,1,0:T(8,128)(2,1)}), bf16[16,1,101,128,128]{4,3,2,1,0:T(8,128)(2,1)}) %all-gather.7.cloned.1.call-update) | async-done | bytes 52953104 | tf_op jit(solution)/shard_map/all_gather | solution.py:173
  271.3 0.6 broadcast_19_first_ref.2.first_ref
  271.9 85.7 %shard_map.109.x_ref = bf16[72,256,128]{2,1,0:T(8,128)(2,1)} custom-call(s32[1616]{0:T(1024)} %reshape.296.row_ref, s32[1616]{0:T(1024)} %reshape.297.col_ref, s32[16]{0:T(128)} %broadcast_19_first_ref.2.first_ref, s32[16]{0:T(128)} %get-tuple-element.56.last_ref, s32[1]{0:T(128)} %bitcast.4.at_ref, bf16[36,256,128]{2,1,0:T(8,128)(2,1)} %bitcast.32, ...), custom_call_target="tpu_custom_call" | custom-call | flops 54223962112 | bytes 52953088 | tf_op jit(solution)/shard_map/pallas_call | solution.py:108
  357.6 88.4 %all-gather.11.cloned.1.call-done = bf16[1056,128,128]{2,1,0:T(8,128)(2,1)} async-done(((bf16[66,128,128]{2,1,0:T(8,128)(2,1)}), bf16[1056,128,128]{2,1,0:T(8,128)(2,1)}) %all-gather.11.cloned.1.call-update) | async-done | bytes 34603024 | tf_op jit(solution)/shard_map/all_gather | solution.py:173
  445.9 70.6 %shard_map.110 = (f32[36,256,128]{2,1,0:T(8,128)}, bf16[256,4608]{1,0:T(8,128)(2,1)}) custom-call(s32[1056]{0:T(1024)} %reshape.300.row_ref, s32[1056]{0:T(1024)} %reshape.301.col_ref, s32[16]{0:T(128)} %broadcast_19_first_ref.2.first_ref, s32[16]{0:T(128)} %get-tuple-element.76.last_ref, s32[1]{0:T(128)} %bitcast.4.at_ref, ...), custom_call_target="tpu_custom_call" | custom-call | flops 35433480192 | bytes 34603008 | tf_op jit(solution)/shard_map/pallas_call | solution.py:108
  516.6 1.4 constant_dynamic-slice_fusion.1
  517.9 1.7 collective-permute-start.1
  520.5 0.7 compare_reduce_fusion
  522.0 0.7 reshape.293.row_ref
  522.7 0.7 reshape.294.col_ref
  523.4 0.6 reshape.302.bias_ref
  524.0 22.1 %collective-permute-done.1 = bf16[256,2304]{1,0:T(8,128)(2,1)S(1)} collective-permute-done((bf16[256,2304]{1,0:T(8,128)(2,1)S(1)}, bf16[256,2304]{1,0:T(8,128)(2,1)S(1)}, u32[]{:S(2)}, u32[]{:S(2)}) %collective-permute-start.1) | collective-permute-done | bytes 1179680 | tf_op jit(solution)/shard_map/ppermute | solution.py:239
  546.1 1.6 convert_element_type.58
  547.7 28.1 %shard_map.111 = bf16[256,2304]{1,0:T(8,128)(2,1)} custom-call(s32[560]{0:T(1024)} %reshape.293.row_ref, s32[560]{0:T(1024)} %reshape.294.col_ref, s32[16]{0:T(128)S(1)} %add_maximum_fusion.1.first_ref, s32[16]{0:T(128)} %get-tuple-element.77.last_ref, s32[1]{0:T(128)} %bitcast.4.at_ref, bf16[72,256,128]{2,1,0:T(8,128)(2,1)} %shard_map.109.x_ref, ...), custom_call_target="tpu_custom_call" | custom-call | flops 18790481920 | bytes 18350080 | tf_op jit(solution)/shard_map/pallas_call | solution.py:108
  (58 shorter events, 3.6 us)
Async XLA Ops:
  6.5 5.4 copy-start
  6.5 1.6 copy-start.5
  6.5 264.8 %all-gather.7.cloned.1.call-start = ((), (), s32[]{:S(2)}) async-start(), calls=%async_computation | async-start | bytes 56262656 | tf_op jit(solution)/shard_map/all_gather | solution.py:173
  7.3 438.7 %all-gather.11.cloned.1.call-start = ((), (), s32[]{:S(2)}) async-start(), calls=%async_computation.2 | async-start | bytes 36765696 | tf_op jit(solution)/shard_map/all_gather | solution.py:173
  14.4 2.6 copy-start.6
  14.4 533.3 %all-gather.9.cloned.1.call-start = ((), (), s32[]{:S(2)}) async-start(), calls=%async_computation.1 | async-start | bytes 19496960 | tf_op jit(solution)/shard_map/all_gather | solution.py:173
  92.2 1.3 copy-start.2
  92.2 1.3 copy-start.3
  516.6 6.8 %copy-start.4 = (f32[2304]{0:T(1024)S(1)}, f32[2304]{0:T(1024)}, u32[]{:S(2)}) copy-start(f32[2304]{0:T(1024)} %param.23) | copy-start | bytes 27652
  517.9 28.2 %collective-permute-start.1 = (bf16[256,2304]{1,0:T(8,128)(2,1)S(1)}, bf16[256,2304]{1,0:T(8,128)(2,1)S(1)}, u32[]{:S(2)}, u32[]{:S(2)}) collective-permute-start(bf16[256,2304]{1,0:T(8,128)(2,1)S(1)} %constant_dynamic-slice_fusion.1), channel_id=1, source_target_pairs={{0,1},{1,0},{2,3},{3,2},{4,5},{5,4},{6,7},{7,6},{8,9},{9,8},{10,11... | collective-permute-start | bytes 3538952 | tf_op jit(solution)/shard_map/ppermute | solution.py:239
  547.7 28.1 %copy-start.1 = (bf16[1,1,101,128,128]{4,3,2,1,0:T(8,128)(2,1)S(1)}, bf16[1,1,101,128,128]{4,3,2,1,0:T(8,128)(2,1)}, u32[]{:S(2)}) copy-start(bf16[1,1,101,128,128]{4,3,2,1,0:T(8,128)(2,1)} %param.20) | copy-start | bytes 9928708
Sparse Core Ops, SparseCore 0:
  9.0 262.3 all-gather.6
  272.9 172.9 all-gather.10
  447.5 96.4 all-gather.8

commit v4 on v3

--- a/solution.py
+++ b/solution.py
@@ -8,39 +8,63 @@
 from jax.sharding import PartitionSpec as P
 
 UNROLL = 4
+STEPS = 4
 VMEM_BYTES = 56 * 1024 * 1024
 
 
-def add_tiles(row_ref, col_ref, first, last, base, x_ref, w_ref, acc):
-    def one(slot):
-        row, col = row_ref[base + slot], col_ref[base + slot]
-        acc[col] += jnp.dot(x_ref[row], w_ref[0, 0, slot], preferred_element_type=jnp.float32)
-
-    def several(step, carry):
+def pair_up(rows, cols, live, blocks, zero_row):
+    listed = rows.shape[1]
+    ids = jnp.arange(listed, dtype=jnp.int32)
+    block_ids = jnp.arange(blocks, dtype=jnp.int32)
+    size = -(-((listed + min(blocks, listed)) // 2) // UNROLL) * UNROLL
+    same = live[:, None, :] & (cols[:, :, None] == cols[:, None, :]) & (ids < ids[:, None])
+    rank = jnp.sum(same.astype(jnp.int32), axis=2)
+    in_block = live[:, None, :] & (cols[:, None, :] == block_ids[:, None])
+    need = (jnp.sum(in_block.astype(jnp.int32), axis=2) + 1) // 2
+    begin = jnp.cumsum(need, axis=1) - need
+    begin = jnp.sum(jnp.where(cols[:, :, None] == block_ids, begin[:, None, :], 0), axis=2)
+    place = jnp.where(live, begin + rank // 2, -1)
+    hit = place[:, None, :] == jnp.arange(size, dtype=jnp.int32)[:, None]
+    odd = (rank % 2 == 1)[:, None, :]
+
+    def chosen(mask, values, default):
+        found = jnp.sum(jnp.where(mask, values[:, None, :] - default, 0), axis=2)
+        return found + default
+
+    tile_ids = jnp.broadcast_to(ids, rows.shape)
+    fields = [
+        chosen(hit & ~odd, tile_ids, 0),
+        chosen(hit & ~odd, rows, zero_row),
+        chosen(hit & odd, tile_ids, 0),
+        chosen(hit & odd, rows, zero_row),
+        chosen(hit & ~odd, cols, 0),
+    ]
+    return jnp.stack(fields).reshape(-1), jnp.sum(need, axis=1)
+
+
+def add_block(field_ref, count_ref, x_ref, w_ref, acc):
+    step, steps = pl.program_id(0), pl.num_programs(0)
+    size = field_ref.shape[0] // (5 * steps)
+
+    def pair(at):
+        tile0, row0, tile1, row1, col = (field_ref[(f * steps + step) * size + at] for f in range(5))
+        left = jnp.concatenate([x_ref[row0], x_ref[row1]], axis=1)
+        right = jnp.concatenate([w_ref[tile0], w_ref[tile1]], axis=0)
+        acc[col] += jnp.dot(left, right, preferred_element_type=jnp.float32)
+
+    def several(turn, carry):
         for u in range(UNROLL):
-            one(first + step * UNROLL + u)
+            pair(turn * UNROLL + u)
         return carry
 
-    def single(slot, carry):
-        one(slot)
-        return carry
-
-    whole = lax.div(jnp.maximum(last - first, 0), jnp.int32(UNROLL))
-    lax.fori_loop(0, whole, several, 0)
-    lax.fori_loop(first + whole * UNROLL, last, single, 0)
-
-
-def add_block(row_ref, col_ref, first_ref, last_ref, x_ref, w_ref, acc):
-    step = pl.program_id(0)
-    base = step * w_ref.shape[2]
-    add_tiles(row_ref, col_ref, first_ref[step], last_ref[step], base, x_ref, w_ref, acc)
+    lax.fori_loop(0, lax.div(count_ref[step] + UNROLL - 1, jnp.int32(UNROLL)), several, 0)
 
 
 def at_end(work):
     pl.when(pl.program_id(0) == pl.num_programs(0) - 1)(work)
 
 
-def hidden_kernel(row_ref, col_ref, first_ref, last_ref, at_ref, x_ref, w_ref, bias_ref, out_ref, acc):
+def hidden_kernel(field_ref, count_ref, at_ref, x_ref, w_ref, bias_ref, out_ref, acc):
     blocks = acc.shape[0]
 
     @pl.when(pl.program_id(0) == 0)
@@ -51,7 +75,7 @@
 
         lax.fori_loop(0, blocks, fill, 0)
 
-    add_block(row_ref, col_ref, first_ref, last_ref, x_ref, w_ref, acc)
+    add_block(field_ref, count_ref, x_ref, w_ref, acc)
 
     @at_end
     def _():
@@ -60,14 +84,15 @@
             return carry
 
         lax.fori_loop(0, blocks, finish, 0)
-
-
-def partial_kernel(row_ref, col_ref, first_ref, last_ref, at_ref, x_ref, w_ref, sum_ref, out_ref, acc):
+        out_ref[blocks] = jnp.zeros(out_ref.shape[1:], out_ref.dtype)
+
+
+def partial_kernel(field_ref, count_ref, at_ref, x_ref, w_ref, sum_ref, out_ref, acc):
     @pl.when(pl.program_id(0) == 0)
     def _():
         acc[...] = jnp.zeros_like(acc)
 
-    add_block(row_ref, col_ref, first_ref, last_ref, x_ref, w_ref, acc)
+    add_block(field_ref, count_ref, x_ref, w_ref, acc)
 
     @at_end
     def _():
@@ -78,14 +103,14 @@
 
 
 def result_kernel(
-    row_ref, col_ref, first_ref, last_ref, at_ref,
+    field_ref, count_ref, at_ref,
     x_ref, w_ref, sum_ref, token_ref, other_ref, bias_ref, out_ref, acc,
 ):
     @pl.when(pl.program_id(0) == 0)
     def _():
         acc[...] = sum_ref[...]
 
-    add_block(row_ref, col_ref, first_ref, last_ref, x_ref, w_ref, acc)
+    add_block(field_ref, count_ref, x_ref, w_ref, acc)
 
     @at_end
     def _():
@@ -101,31 +126,34 @@
     return pl.BlockSpec(shape, lambda i, *_: (0,) * len(shape))
 
 
-def tile_pass(kernel, rows, cols, first, last, at, x, tiles, more, more_specs, out_shapes, blocks):
-    shards, slots, side = tiles.shape[0], tiles.shape[2], tiles.shape[3]
-    tokens = x.shape[1]
-    out_specs = [fixed(o.shape) for o in out_shapes]
+def tile_pass(kernel, rows, cols, live, at, x, tiles, more, more_specs, out_shapes, blocks):
+    shards, slots = rows.shape
+    side, tokens = tiles.shape[-1], x.shape[1]
+    steps = STEPS if shards % STEPS == 0 else 1
+    listed = shards // steps * slots
+    per_step = lambda v: v.reshape(steps, listed)
+    fields, counts = pair_up(per_step(rows), per_step(cols), per_step(live), blocks, x.shape[0] - 1)
     return pl.pallas_call(
         kernel,
         out_shape=out_shapes,
         grid_spec=pltpu.PrefetchScalarGridSpec(
-            num_scalar_prefetch=5,
-            grid=(shards,),
+            num_scalar_prefetch=3,
+            grid=(steps,),
             in_specs=[
                 fixed(x.shape),
-                pl.BlockSpec((1, 1, slots, side, side), lambda i, *_: (i, 0, 0, 0, 0)),
+                pl.BlockSpec((listed, side, side), lambda i, *_: (i, 0, 0)),
                 *more_specs,
             ],
-            out_specs=out_specs,
+            out_specs=[fixed(o.shape) for o in out_shapes],
             scratch_shapes=[pltpu.VMEM((blocks, tokens, side), jnp.float32)],
         ),
         compiler_params=pltpu.CompilerParams(vmem_limit_bytes=VMEM_BYTES),
         cost_estimate=pl.CostEstimate(
-            flops=8 * shards * slots * tokens * side * side,
+            flops=4 * shards * slots * tokens * side * side,
             bytes_accessed=shards * slots * side * side * 2,
             transcendentals=0,
         ),
-    )(rows.reshape(-1), cols.reshape(-1), first, last, at.reshape(1), x, tiles, *more)
+    )(fields, counts, at.reshape(1), x, tiles.reshape(-1, side, side), *more)
 
 
 def on_device(
@@ -190,36 +218,34 @@
     meta = lax.dynamic_index_in_dim(meta, ffn, 1, keepdims=False)
     index1, count1, count2 = meta[:, :slots], meta[:, 2 * slots], meta[:, 2 * slots + 1]
     index2, others = ordered(meta[:, slots : 2 * slots], count2, meta[:, slots : 2 * slots])
-    none = jnp.zeros_like(count1)
 
     rows_f = tokens.astype(jnp.float32)
     center = jnp.mean(rows_f, axis=1, keepdims=True)
     spread = jnp.mean((rows_f - center) ** 2, axis=1, keepdims=True)
     normed = ((rows_f - center) / jnp.sqrt(spread + 1e-05) * ln_gain + ln_bias).astype(jnp.bfloat16)
     normed_blocks = normed.reshape(token_rows, second_blocks, side).transpose(1, 0, 2)
+    normed_blocks = jnp.pad(normed_blocks, ((0, 1), (0, 0), (0, 0)))
 
     (hidden,) = tile_pass(
         hidden_kernel,
         index1 // first_blocks,
         index1 % first_blocks,
-        none,
-        count1,
+        slot_ids < count1[:, None],
         ffn,
         normed_blocks,
         tiles1,
         [fc1_bias.reshape(first_blocks, 1, side)],
         [fixed((first_blocks, 1, side))],
-        [jax.ShapeDtypeStruct((first_blocks, token_rows, side), jnp.bfloat16)],
+        [jax.ShapeDtypeStruct((first_blocks + 1, token_rows, side), jnp.bfloat16)],
         first_blocks,
     )
 
-    def second_pass(lo, hi, first, last, tiles):
+    def second_pass(lo, hi, before, tiles):
         return tile_pass(
             partial_kernel,
             index2[:, lo:hi] // second_blocks,
             index2[:, lo:hi] % second_blocks,
-            first,
-            last,
+            slot_ids[lo:hi] < before[:, None],
             ffn,
             hidden,
             tiles,
@@ -244,11 +270,10 @@
             branch = branch + arrived.astype(jnp.float32)
         return branch
 
-    count2a, count2b = jnp.minimum(count2, early), jnp.maximum(count2 - early, 0)
-    total, partial_value = second_pass(0, early, none, count2a, tiles2a)
+    total, partial_value = second_pass(0, early, count2, tiles2a)
 
     if not aligned:
-        more, late_value = second_pass(early, slots, none, count2b, tiles2b)
+        more, late_value = second_pass(early, slots, count2, tiles2b)
         both = total + more
         partial_value = both.transpose(1, 0, 2).reshape(token_rows, width).astype(jnp.bfloat16)
         own = lax.dynamic_slice_in_dim(partial_value, ffn * share, share, 1).astype(jnp.float32)
@@ -256,10 +281,9 @@
         return (own_cols + own + from_others(partial_value) + fc2_bias).astype(jnp.bfloat16)
 
     branch = from_others(partial_value)
-    late = jnp.maximum(others - early, 0)
 
     def with_late(branch, hidden, tiles):
-        return branch + from_others(second_pass(early, slots, none, late, tiles)[1])
+        return branch + from_others(second_pass(early, slots, others, tiles)[1])
 
     branch = lax.cond(some_late, with_late, lambda branch, *_: branch, branch, hidden, tiles2b)
     share_blocks = share // side
@@ -267,15 +291,14 @@
         result_kernel,
         index2[:, early:] // second_blocks,
         index2[:, early:] % second_blocks % share_blocks,
-        late,
-        count2b,
+        (slot_ids[early:] < count2[:, None]) & (slot_ids[early:] >= others[:, None]),
         ffn,
         hidden,
         tiles2b,
         [total, tokens, branch, fc2_bias.reshape(1, share)],
         [
-            pl.BlockSpec((share_blocks, token_rows, side), lambda i, r, c, f, l, at: (at[0], 0, 0)),
-            pl.BlockSpec((token_rows, share), lambda i, r, c, f, l, at: (0, at[0])),
+            pl.BlockSpec((share_blocks, token_rows, side), lambda i, fields, counts, at: (at[0], 0, 0)),
+            pl.BlockSpec((token_rows, share), lambda i, fields, counts, at: (0, at[0])),
             fixed((token_rows, share)),
             fixed((1, share)),
         ],

time: 584 us -> 570 us (0.976)
  Pallas kernels: 184 us -> 133 us
  other arithmetic: 14.7 us -> 38.7 us
  waiting for transfers between devices: 277 us -> 288 us
    pallas_call x3, Pallas kernels: 184 us -> 133 us  [tile_pass(): pl.pallas_call(kernel, out_shape=out_shapes, grid_spec=pltpu.PrefetchScal...]
    reduce_sum x0 -> x15, other arithmetic: none -> 23.6 us  [the longest x3 14.2 us: pair_up(): rank = jnp.sum(same.astype(jnp.int32), axis=2)]
    all_gather x3, waiting for transfers between devices: 254 us -> 264 us  [gathered(): return lax.all_gather(value, 'blk', axis=0, tiled=True)]
  transfers between devices with their start and end apart: 4 -> 4, of which waited for: 3 -> 4; matrix products, arithmetic and copies ran while one was open for 6% -> 10% of each run, Pallas kernels for 27% -> 20%
where the time goes in v4:
time: 570 us; the launch traced here: 569 us
  waiting for transfers between devices  288 us (51%)
  Pallas kernels  133 us (23%)
  blocking collectives  69.9 us (12%)
  other arithmetic  38.7 us (7%)
  local copies, waits for them, and re-layouts  20.5 us (4%)
  between operations  15.7 us (3%)
    all_gather x3, waiting for transfers between devices, gathered(): return lax.all_gather(value, 'blk', axis=0, tiled=True)  264 us
    pallas_call x3, Pallas kernels, tile_pass(): pl.pallas_call(kernel, out_shape=out_shapes, grid_spec=pltpu.PrefetchScal...  133 us
    all_gather x1, blocking collectives, on_device(): lax.all_gather(meta, ('blk', 'ffn'), axis=0, tiled=True)  69.9 us
    ppermute x1, waiting for transfers between devices, from_others(): lax.ppermute(lax.dynamic_slice_in_dim(partial_value, to * share, share, 1...  23.6 us
    reduce_sum x3, other arithmetic, pair_up(): rank = jnp.sum(same.astype(jnp.int32), axis=2)  14.2 us
  transfers between devices with their start and end apart: 4, of which 4 were waited for; matrix products, arithmetic and copies ran while one was open for 10% of the time, Pallas kernels for 20%

profile of v4, /device:TPU:0, one launch (start us, length us, event | category | flops | bytes accessed | tf_op | source)
XLA Modules:
  0.0 568.6 jit_solution(18294109525722493214)
XLA Ops:
  6.5 0.7 all-gather.7.cloned.1.call-update
  10.0 1.9 fusion.28
  12.0 2.4 gather_fusion.1
  14.5 1.8 gather_fusion
  17.1 69.9 %all-gather.2 = s32[32,1,204]{2,1,0:T(1,128)S(1)} all-gather(s32[1,1,204]{2,1,0:T(1,128)S(1)} %add_bitcast_fusion), channel_id=1, replica_groups=mesh['blk'=16,'ffn'=2] {'blk','ffn'}, dimensions={0}, use_global_device_ids=true | all-gather | bytes 26928 | tf_op jit(solution)/shard_map/all_gather | solution.py:212
  88.3 1.8 select_reduce_fusion.16
  90.7 0.7 convert_reduce_fusion.7
  93.3 1.1 select_reduce_fusion.12
  94.4 0.7 reshape.1001.field_ref
  95.8 10.9 %convert_reduce_fusion.3 = s32[4,404]{0,1:T(8,128)S(1)} fusion(s32[4,404]{1,0:T(4,128)S(1)} %eq.371, s32[4,404]{0,1:T(8,128)S(1)} %copy.178, pred[404,404]{1,0:T(8,128)(4,1)S(1)} %iota_compare_fusion.6, pred[4,404]{1,0:T(4,128)(4,1)S(1)} %broadcast_compare_fusion.3), kind=kLoop, calls=%fused_computation.58 | loop fusion | flops 3262704 | bytes 184224 | tf_op jit(solution)/shard_map/reduce_sum | solution.py:21
  107.0 0.7 fusion.69
  108.9 3.6 select_reduce_fusion.6
  112.6 0.7 reshape.996.field_ref
  113.2 2.8 copy.188
  117.5 3.4 fusion.17
  120.9 3.2 copy.189
  125.7 2.7 convert_reduce_fusion.6
  128.9 0.7 fusion.73
  130.7 1.7 pad.4.x_ref
  132.4 1.1 select_reduce_fusion.19
  133.4 137.9 %all-gather.7.cloned.1.call-done = bf16[16,1,101,128,128]{4,3,2,1,0:T(8,128)(2,1)} async-done(((bf16[1,1,101,128,128]{4,3,2,1,0:T(8,128)(2,1)}), bf16[16,1,101,128,128]{4,3,2,1,0:T(8,128)(2,1)}) %all-gather.7.cloned.1.call-update) | async-done | bytes 52953104 | tf_op jit(solution)/shard_map/all_gather | solution.py:201
  271.3 63.7 %shard_map.109.x_ref = bf16[73,256,128]{2,1,0:T(8,128)(2,1)} custom-call(s32[4800]{0:T(1024)} %reshape.996.field_ref, s32[4]{0:T(128)} %get-tuple-element.101.count_ref, s32[1]{0:T(128)} %bitcast.17.at_ref, bf16[37,256,128]{2,1,0:T(8,128)(2,1)} %pad.4.x_ref, bf16[1616,128,128]{2,1,0:T(8,128)(2,1)} %bitcast.83, f32[72,1,128]{2,1,0:T(1,128)} %bitcast.84), custom_call_target="tpu_custom_call" | custom-call | flops 27111981056 | bytes 52953088 | tf_op jit(solution)/shard_map/pallas_call | solution.py:136
  335.0 110.9 %all-gather.11.cloned.1.call-done.w_ref = bf16[1056,128,128]{2,1,0:T(8,128)(2,1)} async-done(((bf16[66,128,128]{2,1,0:T(8,128)(2,1)}), bf16[1056,128,128]{2,1,0:T(8,128)(2,1)}) %all-gather.11.cloned.1.call-update) | async-done | bytes 34603024 | tf_op jit(solution)/shard_map/all_gather | solution.py:201
  445.9 51.6 %shard_map.110 = (f32[36,256,128]{2,1,0:T(8,128)}, bf16[256,4608]{1,0:T(8,128)(2,1)}) custom-call(s32[3040]{0:T(1024)} %reshape.1001.field_ref, s32[4]{0:T(128)} %get-tuple-element.95.count_ref, s32[1]{0:T(128)} %bitcast.17.at_ref, bf16[73,256,128]{2,1,0:T(8,128)(2,1)} %shard_map.109.x_ref, bf16[1056,128,128]{2,1,0:T(8,128)(2,1)} %all-gather.11.cloned.1.call-done.w_ref), custom_call_target="tpu_custom_call" | custom-call | flops 17716740096 | bytes 34603008 | tf_op jit(solution)/shard_map/pallas_call | solution.py:136
  497.5 1.4 constant_dynamic-slice_fusion.1
  498.9 2.1 collective-permute-start.1
  501.0 0.7 compare_reduce_fusion
  502.5 0.7 reshape.994.field_ref
  503.8 23.6 %collective-permute-done.1 = bf16[256,2304]{1,0:T(8,128)(2,1)S(1)} collective-permute-done((bf16[256,2304]{1,0:T(8,128)(2,1)S(1)}, bf16[256,2304]{1,0:T(8,128)(2,1)S(1)}, u32[]{:S(2)}, u32[]{:S(2)}) %collective-permute-start.1) | collective-permute-done | bytes 1179680 | tf_op jit(solution)/shard_map/ppermute | solution.py:265
  527.4 1.6 convert_element_type.90
  529.0 15.1 %all-gather.9.cloned.1.call-done.w_ref = bf16[560,128,128]{2,1,0:T(8,128)(2,1)} async-done(((bf16[35,128,128]{2,1,0:T(8,128)(2,1)}), bf16[560,128,128]{2,1,0:T(8,128)(2,1)}) %all-gather.9.cloned.1.call-update) | async-done | bytes 18350096 | tf_op jit(solution)/shard_map/all_gather | solution.py:201
  544.1 18.0 %shard_map.111 = bf16[256,2304]{1,0:T(8,128)(2,1)} custom-call(s32[1600]{0:T(1024)} %reshape.994.field_ref, s32[4]{0:T(128)} %get-tuple-element.107.count_ref, s32[1]{0:T(128)} %bitcast.17.at_ref, bf16[73,256,128]{2,1,0:T(8,128)(2,1)} %shard_map.109.x_ref, bf16[560,128,128]{2,1,0:T(8,128)(2,1)} %all-gather.9.cloned.1.call-done.w_ref, ...), custom_call_target="tpu_custom_call" | custom-call | flops 9395240960 | bytes 18350080 | tf_op jit(solution)/shard_map/pallas_call | solution.py:136
  (142 shorter events, 13.2 us)
Async XLA Ops:
  6.5 5.4 copy-start
  6.5 1.6 copy-start.5
  6.5 264.8 %all-gather.7.cloned.1.call-start = ((), (), s32[]{:S(2)}) async-start(), calls=%async_computation | async-start | bytes 56262656 | tf_op jit(solution)/shard_map/all_gather | solution.py:201
  7.3 438.7 %all-gather.11.cloned.1.call-start = ((), (), s32[]{:S(2)}) async-start(), calls=%async_computation.2 | async-start | bytes 36765696 | tf_op jit(solution)/shard_map/all_gather | solution.py:201
  14.3 2.6 copy-start.6
  14.4 529.7 %all-gather.9.cloned.1.call-start = ((), (), s32[]{:S(2)}) async-start(), calls=%async_computation.1 | async-start | bytes 19496960 | tf_op jit(solution)/shard_map/all_gather | solution.py:201
  116.1 1.3 copy-start.2
  116.1 1.3 copy-start.3
  497.5 5.7 copy-start.4
  498.9 28.5 %collective-permute-start.1 = (bf16[256,2304]{1,0:T(8,128)(2,1)S(1)}, bf16[256,2304]{1,0:T(8,128)(2,1)S(1)}, u32[]{:S(2)}, u32[]{:S(2)}) collective-permute-start(bf16[256,2304]{1,0:T(8,128)(2,1)S(1)} %constant_dynamic-slice_fusion.1), channel_id=1, source_target_pairs={{0,1},{1,0},{2,3},{3,2},{4,5},{5,4},{6,7},{7,6},{8,9},{9,8},{10,11... | collective-permute-start | bytes 3538952 | tf_op jit(solution)/shard_map/ppermute | solution.py:265
  544.1 18.0 %copy-start.1 = (bf16[1,1,101,128,128]{4,3,2,1,0:T(8,128)(2,1)S(1)}, bf16[1,1,101,128,128]{4,3,2,1,0:T(8,128)(2,1)}, u32[]{:S(2)}) copy-start(bf16[1,1,101,128,128]{4,3,2,1,0:T(8,128)(2,1)} %param.20) | copy-start | bytes 9928708
Sparse Core Ops, SparseCore 0:
  9.0 262.2 all-gather.6
  272.9 172.9 all-gather.10
  447.5 96.4 all-gather.8

commit v5 on v4

--- a/solution.py
+++ b/solution.py
@@ -44,6 +44,7 @@
 
 def add_block(field_ref, count_ref, x_ref, w_ref, acc):
     step, steps = pl.program_id(0), pl.num_programs(0)
+    w_ref = w_ref.reshape(-1, *w_ref.shape[2:])
     size = field_ref.shape[0] // (5 * steps)
 
     def pair(at):
@@ -64,16 +65,28 @@
     pl.when(pl.program_id(0) == pl.num_programs(0) - 1)(work)
 
 
-def hidden_kernel(field_ref, count_ref, at_ref, x_ref, w_ref, bias_ref, out_ref, acc):
-    blocks = acc.shape[0]
-
+def first_kernel(field_ref, count_ref, at_ref, x_ref, w_ref, bias_ref, sum_ref, acc):
     @pl.when(pl.program_id(0) == 0)
     def _():
         def fill(c, carry):
             acc[c] = jnp.broadcast_to(bias_ref[c], acc.shape[1:])
             return carry
 
-        lax.fori_loop(0, blocks, fill, 0)
+        lax.fori_loop(0, acc.shape[0], fill, 0)
+
+    add_block(field_ref, count_ref, x_ref, w_ref, acc)
+
+    @at_end
+    def _():
+        sum_ref[...] = acc[...]
+
+
+def hidden_kernel(field_ref, count_ref, at_ref, x_ref, w_ref, sum_ref, out_ref, acc):
+    blocks = acc.shape[0]
+
+    @pl.when(pl.program_id(0) == 0)
+    def _():
+        acc[...] = sum_ref[...]
 
     add_block(field_ref, count_ref, x_ref, w_ref, acc)
 
@@ -141,7 +154,7 @@
             grid=(steps,),
             in_specs=[
                 fixed(x.shape),
-                pl.BlockSpec((listed, side, side), lambda i, *_: (i, 0, 0)),
+                pl.BlockSpec((shards // steps, slots, side, side), lambda i, *_: (i, 0, 0, 0)),
                 *more_specs,
             ],
             out_specs=[fixed(o.shape) for o in out_shapes],
@@ -153,7 +166,17 @@
             bytes_accessed=shards * slots * side * side * 2,
             transcendentals=0,
         ),
-    )(fields, counts, at.reshape(1), x, tiles.reshape(-1, side, side), *more)
+    )(fields, counts, at.reshape(1), x, tiles, *more)
+
+
+def swapped(values, stride):
+    return values.reshape(-1, 2, stride, *values.shape[1:])[:, ::-1].reshape(values.shape)
+
+
+def moved(values, by):
+    ids = jnp.arange(values.shape[1], dtype=jnp.int32)
+    hit = (ids[:, None] - by[:, None, None]) == ids
+    return jnp.sum(jnp.where(hit, values[:, None, :], 0), axis=2)
 
 
 def on_device(
@@ -177,47 +200,110 @@
     first_blocks = fc1_bias.shape[0] // side
     second_blocks = width // side
     share = width // ffn_size
-    ffn = lax.axis_index("ffn")
+    blk, ffn = lax.axis_index("blk"), lax.axis_index("ffn")
+    aligned = share % side == 0
+    opening = slots * 4 // 5
+    rest = slots - opening
+    held = slots - slots // 40
+    late_from = held - slots // 3
+    levels = [
+        (stride, max(slots // most, 1), max(slots // least, 1))
+        for stride, most, least in ((1, 6, 8), (2, 8, 10), (4, 12, 16))
+        if shards % (2 * stride) == 0
+    ]
     slot_ids = jnp.arange(slots, dtype=jnp.int32)
-    aligned = share % side == 0
-    early = slots - slots * 7 // 20
-
-    def in_share(index, at):
+    stream_ids = jnp.arange(rest + slots, dtype=jnp.int32)
+
+    def gathered(value):
+        return lax.all_gather(value, "blk", axis=0, tiled=True).reshape(shards, -1, side, side)
+
+    tiles1 = gathered(fc1_tiles[0, 0, :opening])
+    meta = jnp.concatenate([fc1_index[:, 0], fc2_index[:, 0], fc1_count, fc2_count], axis=1)
+    meta = lax.all_gather(meta, "blk", axis=0, tiled=True)
+    index1, index2 = meta[:, :slots], meta[:, slots : 2 * slots]
+    count1, count2 = meta[:, 2 * slots], meta[:, 2 * slots + 1]
+    left1 = jnp.maximum(count1 - opening, 0)
+
+    def in_own_share(index):
         if not aligned:
             return jnp.zeros(index.shape, jnp.bool_)
-        return index % second_blocks // (share // side) == at
-
-    def ordered(index, count, values):
+        return index % second_blocks // (share // side) == ffn
+
+    def streams(index, count, left, first_values, values):
         live = slot_ids < count[:, None]
-        own = in_share(index, ffn)
-        other = (live & ~own).astype(jnp.int32)
-        mine = (live & own).astype(jnp.int32)
-        others = jnp.sum(other, axis=1, keepdims=True)
-        place = jnp.where(own, others + jnp.cumsum(mine, axis=1) - 1, jnp.cumsum(other, axis=1) - 1)
-        hit = live[:, None, :] & (place[:, None, :] == slot_ids[:, None])
-        return jnp.sum(jnp.where(hit, values[:, None, :], 0), axis=2), others[:, 0]
-
-    def gathered(value):
-        return lax.all_gather(value, "blk", axis=0, tiled=True)
-
-    tiles1 = gathered(fc1_tiles)
-    order, _ = ordered(fc2_index[:, 0], fc2_count[:, 0], slot_ids[None])
-    pieces = [
-        jnp.take(fc2_tiles[0, 0], part, axis=0, mode="clip")[None, None]
-        for part in (order[0, :early], order[0, early:])
-    ]
-    tiles2a, tiles2b = gathered(pieces[0]), gathered(pieces[1])
-
-    meta = jnp.concatenate([fc1_index[:, 0], fc2_index[:, 0], fc1_count, fc2_count], axis=1)
-    meta = lax.all_gather(meta, ("blk", "ffn"), axis=0, tiled=True).reshape(shards, ffn_size, -1)
-    all_index2, all_count2 = meta[..., slots : 2 * slots], meta[..., 2 * slots + 1]
-    all_other = (slot_ids < all_count2[..., None]) & ~in_share(
-        all_index2, jnp.arange(ffn_size, dtype=jnp.int32)[:, None]
-    )
-    some_late = jnp.any(jnp.sum(all_other.astype(jnp.int32), axis=2) > early)
-    meta = lax.dynamic_index_in_dim(meta, ffn, 1, keepdims=False)
-    index1, count1, count2 = meta[:, :slots], meta[:, 2 * slots], meta[:, 2 * slots + 1]
-    index2, others = ordered(meta[:, slots : 2 * slots], count2, meta[:, slots : 2 * slots])
+        own = in_own_share(index)
+        front, back = live & ~own, live & own
+        front_place = left[:, None] + jnp.cumsum(front.astype(jnp.int32), axis=1) - 1
+        back_place = jnp.cumsum(back.astype(jnp.int32), axis=1) - 1
+
+        def placed(mask, place):
+            hit = mask[:, None, :] & (place[:, None, :] == stream_ids[:, None])
+            return jnp.sum(jnp.where(hit, values[:, None, :], 0), axis=2)
+
+        first = jnp.where(stream_ids < left[:, None], jnp.pad(first_values, ((0, 0), (0, slots))), 0)
+        return (
+            first + placed(front, front_place),
+            placed(back, back_place),
+            left + jnp.sum(front.astype(jnp.int32), axis=1),
+            jnp.sum(back.astype(jnp.int32), axis=1),
+        )
+
+    front, back, fronts, backs = streams(
+        index2, count2, left1, jnp.zeros((shards, rest), jnp.int32), index2
+    )
+    own_left = jnp.maximum(fc1_count[:, 0] - opening, 0)
+    own_front, own_back, _, _ = streams(
+        fc2_index[:, 0], fc2_count[:, 0], own_left, jnp.arange(rest, dtype=jnp.int32)[None], rest + slot_ids[None]
+    )
+    own_front, own_back = own_front[0], own_back[0]
+    sources = jnp.concatenate([fc1_tiles[0, 0, opening:], fc2_tiles[0, 0]], axis=0)
+
+    def evened(values, numbers, fixed_numbers, stride, most):
+        partners = swapped(numbers, stride)
+        sent = jnp.clip((numbers - partners) // 2, 0, jnp.minimum(most, numbers - fixed_numbers))
+        kept = numbers - sent
+        got = swapped(sent, stride)
+        arrived = moved(swapped(values, stride), kept - (partners - got))
+        return jnp.where(stream_ids < kept[:, None], values, arrived), kept, kept + got
+
+    def tail(stream, kept, most):
+        return lax.dynamic_slice_in_dim(jnp.pad(stream, (0, most)), kept, most)
+
+    for stride, most_front, most_back in levels:
+        front, kept_front, fronts = evened(front, fronts, left1, stride, most_front)
+        back, kept_back, backs = evened(back, backs, jnp.zeros_like(backs), stride, most_back)
+        kept_front, kept_back = kept_front[blk], kept_back[blk]
+        sending = jnp.concatenate(
+            [tail(own_front, kept_front, most_front), tail(own_back, kept_back, most_back)]
+        )
+        arrived = lax.ppermute(
+            jnp.take(sources, sending, axis=0, mode="clip"),
+            "blk",
+            [(i, i ^ stride) for i in range(shards)],
+        )
+        so_far = sources.shape[0]
+        own_front = jnp.where(stream_ids < kept_front, own_front, so_far + stream_ids - kept_front)
+        own_back = jnp.where(stream_ids < kept_back, own_back, so_far + most_front + stream_ids - kept_back)
+        sources = jnp.concatenate([sources, arrived], axis=0)
+
+    total_ids = jnp.arange(2 * stream_ids.shape[0] + slots // 4, dtype=jnp.int32)
+    double = ((0, 0), (0, total_ids.shape[0] - stream_ids.shape[0]))
+    lengths = fronts + backs
+    codes = jnp.where(
+        total_ids < fronts[:, None], jnp.pad(front, double), moved(jnp.pad(back, double), fronts)
+    )
+    own_fronts = fronts[blk]
+    order = jnp.where(
+        total_ids < own_fronts,
+        jnp.pad(own_front, double[1]),
+        moved(jnp.pad(own_back, double[1])[None], own_fronts[None])[0],
+    )
+    tiles2a = gathered(jnp.take(sources, order[:late_from], axis=0, mode="clip"))
+    tiles2b = gathered(jnp.take(sources, order[late_from:held], axis=0, mode="clip"))
+    chunk = slots // 4
+    misplaced = jnp.stack([jnp.max(fronts) - late_from, jnp.max(lengths) - held])
+    misplaced = lax.pmax(misplaced, "ffn")
+    some_late = jnp.max(misplaced) > 0
 
     rows_f = tokens.astype(jnp.float32)
     center = jnp.mean(rows_f, axis=1, keepdims=True)
@@ -226,26 +312,39 @@
     normed_blocks = normed.reshape(token_rows, second_blocks, side).transpose(1, 0, 2)
     normed_blocks = jnp.pad(normed_blocks, ((0, 1), (0, 0), (0, 0)))
 
-    (hidden,) = tile_pass(
-        hidden_kernel,
-        index1 // first_blocks,
-        index1 % first_blocks,
-        slot_ids < count1[:, None],
+    (total,) = tile_pass(
+        first_kernel,
+        index1[:, :opening] // first_blocks,
+        index1[:, :opening] % first_blocks,
+        slot_ids[:opening] < count1[:, None],
         ffn,
         normed_blocks,
         tiles1,
         [fc1_bias.reshape(first_blocks, 1, side)],
         [fixed((first_blocks, 1, side))],
+        [jax.ShapeDtypeStruct((first_blocks, token_rows, side), jnp.float32)],
+        first_blocks,
+    )
+    (hidden,) = tile_pass(
+        hidden_kernel,
+        index1[:, opening:] // first_blocks,
+        index1[:, opening:] % first_blocks,
+        slot_ids[opening:] < count1[:, None],
+        ffn,
+        normed_blocks,
+        tiles2a,
+        [total],
+        [fixed(total.shape)],
         [jax.ShapeDtypeStruct((first_blocks + 1, token_rows, side), jnp.bfloat16)],
         first_blocks,
     )
 
-    def second_pass(lo, hi, before, tiles):
+    def second_pass(places, live, tiles):
         return tile_pass(
             partial_kernel,
-            index2[:, lo:hi] // second_blocks,
-            index2[:, lo:hi] % second_blocks,
-            slot_ids[lo:hi] < before[:, None],
+            places // second_blocks,
+            places % second_blocks,
+            live,
             ffn,
             hidden,
             tiles,
@@ -258,6 +357,9 @@
             second_blocks,
         )
 
+    def own_cols(value):
+        return lax.dynamic_slice_in_dim(value, ffn * share, share, 1).astype(jnp.float32)
+
     def from_others(partial_value):
         branch = jnp.zeros((token_rows, share), jnp.float32)
         for shift in range(1, ffn_size):
@@ -270,28 +372,39 @@
             branch = branch + arrived.astype(jnp.float32)
         return branch
 
-    total, partial_value = second_pass(0, early, count2, tiles2a)
+    in_front = total_ids < fronts[:, None]
+    in_second = (total_ids >= left1[:, None]) & (total_ids < lengths[:, None])
+    total, partial_value = second_pass(codes[:, :late_from], in_second[:, :late_from], tiles2a)
+    last_codes = codes[:, late_from:held]
+    last_own = (in_second & ~in_front)[:, late_from:held]
+    branch = from_others(partial_value)
+
+    def with_late(branch):
+        _, late = second_pass(last_codes, (in_second & in_front)[:, late_from:held], tiles2b)
+        branch = branch + from_others(late) + own_cols(late)
+
+        def one_more(number, branch):
+            at = held + number * chunk
+            here = jnp.take(sources, lax.dynamic_slice_in_dim(order, at, chunk), axis=0, mode="clip")
+            part = [lax.dynamic_slice_in_dim(v, at, chunk, 1) for v in (codes, in_second)]
+            _, extra = second_pass(*part, gathered(here))
+            return branch + from_others(extra) + own_cols(extra)
+
+        return lax.fori_loop(0, (misplaced[1] + chunk - 1) // chunk, one_more, branch)
+
+    branch = lax.cond(some_late, with_late, lambda branch: branch, branch)
 
     if not aligned:
-        more, late_value = second_pass(early, slots, count2, tiles2b)
-        both = total + more
-        partial_value = both.transpose(1, 0, 2).reshape(token_rows, width).astype(jnp.bfloat16)
-        own = lax.dynamic_slice_in_dim(partial_value, ffn * share, share, 1).astype(jnp.float32)
-        own_cols = lax.dynamic_slice_in_dim(rows_f, ffn * share, share, 1)
-        return (own_cols + own + from_others(partial_value) + fc2_bias).astype(jnp.bfloat16)
-
-    branch = from_others(partial_value)
-
-    def with_late(branch, hidden, tiles):
-        return branch + from_others(second_pass(early, slots, others, tiles)[1])
-
-    branch = lax.cond(some_late, with_late, lambda branch, *_: branch, branch, hidden, tiles2b)
+        more, _ = second_pass(last_codes, last_own, tiles2b)
+        own = (total + more).transpose(1, 0, 2).reshape(token_rows, width)
+        return (own_cols(tokens) + own_cols(own) + branch + fc2_bias).astype(jnp.bfloat16)
+
     share_blocks = share // side
     (result,) = tile_pass(
         result_kernel,
-        index2[:, early:] // second_blocks,
-        index2[:, early:] % second_blocks % share_blocks,
-        (slot_ids[early:] < count2[:, None]) & (slot_ids[early:] >= others[:, None]),
+        last_codes // second_blocks,
+        last_codes % second_blocks % share_blocks,
+        last_own,
         ffn,
         hidden,
         tiles2b,

time: 570 us -> 548 us (0.961); the launches traced: 569 us -> 538 us
  waiting for transfers between devices: 288 us -> 140 us
  other arithmetic: 38.7 us -> 103 us
  local copies, waits for them, and re-layouts: 20.5 us -> 65.5 us
  blocking collectives: 69.9 us -> 50 us
  Pallas kernels: 133 us -> 147 us
  between operations: 15.7 us -> 29.7 us
    all_gather x3, waiting for transfers between devices: 264 us -> 90.5 us  [gathered(): lax.all_gather(value, 'blk', axis=0, tiled=True)]
    ppermute x0 -> x3, waiting for transfers between devices: none -> 49.1 us  [on_device(): lax.ppermute(jnp.take(sources, sending, axis=0, mode='clip'), 'blk', [(i,...]
    all_gather x1, blocking collectives: 69.9 us -> 23.1 us  [on_device(): meta = lax.all_gather(meta, 'blk', axis=0, tiled=True)]
    reduce_sum x4 -> x12, other arithmetic: 4.78 us -> 40.6 us  [the longest x8 36.9 us: moved(): return jnp.sum(jnp.where(hit, values[:, None, :], 0), axis=2)]
    pmax x0 -> x1, blocking collectives: none -> 26.9 us  [on_device(): misplaced = lax.pmax(misplaced, 'ffn')]
    ppermute x1, waiting for transfers between devices: 23.6 us -> 0.01 us  [from_others(): lax.ppermute(lax.dynamic_slice_in_dim(partial_value, to * share, share, 1...]
    gather x2 -> x5, local copies, waits for them, and re-layouts: 4.18 us -> 21 us  [the longest x3 11.1 us: on_device(): jnp.take(sources, sending, axis=0, mode='clip')]
    reduce_sum x3 -> x4, other arithmetic: 5.75 us -> 19.6 us  [chosen(): found = jnp.sum(jnp.where(mask, values[:, None, :] - default, 0), axis=2)]
  transfers between devices with their start and end apart: 4 -> 7, of which waited for: 4 -> 3; matrix products, arithmetic and copies ran while one was open for 10% -> 30% of each run, Pallas kernels for 20% -> 23%
where the time goes in v5:
time: 548 us; the launch traced here: 538 us
  Pallas kernels  147 us (27%)
  waiting for transfers between devices  140 us (26%)
  other arithmetic  103 us (19%)
  local copies, waits for them, and re-layouts  65.5 us (12%)
  blocking collectives  50 us (9%)
  between operations  29.7 us (5%)
    pallas_call x4, Pallas kernels, tile_pass(): pl.pallas_call(kernel, out_shape=out_shapes, grid_spec=pltpu.PrefetchScal...  147 us
    all_gather x3, waiting for transfers between devices, gathered(): lax.all_gather(value, 'blk', axis=0, tiled=True)  90.5 us
    ppermute x3, waiting for transfers between devices, on_device(): lax.ppermute(jnp.take(sources, sending, axis=0, mode='clip'), 'blk', [(i,...  49.1 us
    reduce_sum x8, other arithmetic, moved(): return jnp.sum(jnp.where(hit, values[:, None, :], 0), axis=2)  36.9 us
    pmax x1, blocking collectives, on_device(): misplaced = lax.pmax(misplaced, 'ffn')  26.9 us
    all_gather x1, blocking collectives, on_device(): meta = lax.all_gather(meta, 'blk', axis=0, tiled=True)  23.1 us
    reduce_sum x4, other arithmetic, chosen(): found = jnp.sum(jnp.where(mask, values[:, None, :] - default, 0), axis=2)  19.6 us
    unnamed x168, local copies, waits for them, and re-layouts  13 us
  transfers between devices with their start and end apart: 7, of which 3 were waited for; matrix products, arithmetic and copies ran while one was open for 30% of the time, Pallas kernels for 23%

profile of v5, /device:TPU:0, one launch (start us, length us, event | category | flops | bytes accessed | tf_op | source)
XLA Modules:
  0.0 537.7 jit_solution(11317284239220065823)
XLA Ops:
  6.5 3.6 slice.93
  11.9 23.1 %all-gather.4 = s32[16,1,204]{2,1,0:T(1,128)S(1)} all-gather(s32[1,1,204]{2,1,0:T(1,128)S(1)} %add_bitcast_fusion.4), channel_id=1, replica_groups=mesh['blk'=16,'ffn'=2] {'blk'}, dimensions={0}, use_global_device_ids=true | all-gather | bytes 13872 | tf_op jit(solution)/shard_map/all_gather | solution.py:222
  53.6 2.5 compare_select_fusion.3
  60.6 3.7 gather_fusion.1
  77.3 6.1 %fusion.35 = s32[269]{0:T(512)S(1)} fusion(s32[269]{0:T(512)S(1)} %iota_subtract_fusion.7, s32[269]{0:T(512)S(1)} %pad.58), kind=kLoop, calls=%fused_computation.161 | loop fusion | flops 216814 | bytes 3228 | tf_op jit(solution)/shard_map/reduce_sum | solution.py:179
  83.4 4.1 pad_maximum_fusion.1
  87.5 4.0 gather_fusion.2
  95.5 30.4 %collective-permute-done.3 = bf16[22,128,128]{2,1,0:T(8,128)(2,1)S(1)} collective-permute-done((bf16[22,128,128]{2,1,0:T(8,128)(2,1)}, bf16[22,128,128]{2,1,0:T(8,128)(2,1)S(1)}, u32[]{:S(2)}, u32[]{:S(2)}) %collective-permute-start.3) | collective-permute-done | bytes 720928 | tf_op jit(solution)/shard_map/ppermute | solution.py:279
  126.7 5.4 %pad_maximum_fusion = bf16[172,128,128]{2,1,0:T(8,128)(2,1)} fusion(bf16[22,128,128]{2,1,0:T(8,128)(2,1)S(1)} %collective-permute-done.3, bf16[28,128,128]{2,1,0:T(8,128)(2,1)} %collective-permute-done.2, bf16[101,128,128]{2,1,0:T(8,128)(2,1)S(1)} %bitcast.159, bf16[21,128,128]{2,1,0:T(8,128)(2,1)S(1)} %copy-done.2), kind=kLoop, calls=%fused_computation.107 | loop fusion | flops 8454144 | bytes 11272192 | tf_op jit(solution)/shard_map/concatenate | solution.py:287
  132.2 3.3 gather_fusion.3
  136.3 2.4 constant_dynamic-update-slice_fusion.22
  139.6 18.7 %collective-permute-done.4 = bf16[14,128,128]{2,1,0:T(8,128)(2,1)S(1)} collective-permute-done((bf16[14,128,128]{2,1,0:T(8,128)(2,1)S(1)}, bf16[14,128,128]{2,1,0:T(8,128)(2,1)S(1)}, u32[]{:S(2)}, u32[]{:S(2)}) %collective-permute-start.4) | collective-permute-done | bytes 458784 | tf_op jit(solution)/shard_map/ppermute | solution.py:279
  159.1 5.2 gather_fusion.4
  164.8 4.7 gather_fusion.5
  180.4 2.4 select_reduce_fusion.20
  183.0 2.4 select_reduce_fusion.19
  185.6 2.4 select_reduce_fusion.18
  188.3 2.4 select_reduce_fusion.23
  190.8 2.4 select_reduce_fusion.22
  193.4 12.8 %select_reduce_fusion.21 = s32[16,122]{0,1:T(8,128)S(1)} fusion(s32[16,122]{1,0:T(8,128)S(1)} %bitcast.195, s32[16,122]{0,1:T(8,128)S(1)} %iota_subtract_fusion.4), kind=kLoop, calls=%fused_computation.133 | loop fusion | flops 712480 | bytes 23424 | tf_op jit(solution)/shard_map/reduce_sum | solution.py:179
  206.3 5.9 %select_reduce_fusion.12 = s32[16,269]{0,1:T(8,128)S(1)} fusion(s32[16,269]{1,0:T(8,128)S(1)} %pad.49, s32[16,269]{0,1:T(8,128)S(1)} %iota_subtract_fusion), kind=kLoop, calls=%fused_computation.103 | loop fusion | flops 3469024 | bytes 51648 | tf_op jit(solution)/shard_map/reduce_sum | solution.py:179
  219.8 2.5 convert_reduce_fusion.7
  225.7 17.0 %select_reduce_fusion.14 = (s32[4,196]{0,1:T(8,128)S(1)}, s32[4,196]{0,1:T(8,128)S(1)}, s32[4,196]{0,1:T(8,128)S(1)}, s32[4,196]{0,1:T(8,128)S(1)}, s32[4,196]{0,1:T(8,128)S(1)}) fusion(s32[4,320]{1,0:T(4,128)S(1)} %sub.1092, s32[4,320]{1,0:T(4,128)S(1)} %fusion.101, pred[4,320]{1,0:T(4,128)(4,1)S(1)} %get-tuple-element.348, ...), kind=kLoop, calls=%fused_computation.120 | loop fusion | flops 3257520 | bytes 33600 | tf_op jit(solution)/shard_map/reduce_sum | solution.py:31
  243.9 3.2 copy.347
  248.5 3.7 fusion.27
  252.2 3.1 copy.348
  259.1 61.3 %shard_map.109.sum_ref = f32[72,256,128]{2,1,0:T(8,128)} custom-call(s32[3920]{0:T(1024)} %reshape.2441.field_ref, s32[4]{0:T(128)} %get-tuple-element.345.count_ref, s32[1]{0:T(128)} %bitcast.44.at_ref, bf16[37,256,128]{2,1,0:T(8,128)(2,1)} %pad.50.x_ref, bf16[16,80,128,128]{3,2,1,0:T(8,128)(2,1)} %bitcast.204, f32[72,1,128]{2,1,0:T(1,128)} %bitcast.208), custom_call_target="tpu_custom_call" | custom-call | flops 21474836480 | bytes 41943040 | tf_op jit(solution)/shard_map/pallas_call | solution.py:149
  320.3 90.5 %all-gather.12.cloned.1.call-done = bf16[1056,128,128]{2,1,0:T(8,128)(2,1)} async-done(((bf16[66,128,128]{2,1,0:T(8,128)(2,1)}), bf16[1056,128,128]{2,1,0:T(8,128)(2,1)}) %all-gather.12.cloned.1.call-update) | async-done | bytes 34603024 | tf_op jit(solution)/shard_map/all_gather | solution.py:218
  410.8 16.0 %shard_map.110.x_ref = bf16[73,256,128]{2,1,0:T(8,128)(2,1)S(1)} custom-call(s32[1600]{0:T(1024)} %reshape.2436.field_ref, s32[4]{0:T(128)} %get-tuple-element.363.count_ref, s32[1]{0:T(128)} %bitcast.44.at_ref, bf16[37,256,128]{2,1,0:T(8,128)(2,1)} %pad.50.x_ref, bf16[16,66,128,128]{3,2,1,0:T(8,128)(2,1)} %bitcast.160, f32[72,256,128]{2,1,0:T(8,128)} %shard_map.109.sum_ref), custom_call_target="tpu_custom_call" | custom-call | flops 5637144576 | bytes 11010048 | tf_op jit(solution)/shard_map/pallas_call | solution.py:149
  426.9 47.8 %shard_map.111 = (f32[36,256,128]{2,1,0:T(8,128)}, bf16[256,4608]{1,0:T(8,128)(2,1)}) custom-call(s32[3040]{0:T(1024)} %reshape.2446.field_ref, s32[4]{0:T(128)} %get-tuple-element.339.count_ref, s32[1]{0:T(128)} %bitcast.44.at_ref, bf16[73,256,128]{2,1,0:T(8,128)(2,1)S(1)} %shard_map.110.x_ref, bf16[16,66,128,128]{3,2,1,0:T(8,128)(2,1)} %bitcast.161), custom_call_target="tpu_custom_call" | custom-call | flops 17716740096 | bytes 34603008 | tf_op jit(solution)/shard_map/pallas_call | solution.py:149
  477.4 26.9 %pmax.7 = s32[2]{0:T(128)S(1)} all-reduce(s32[2]{0:T(128)S(1)} %pad_add_fusion.3), channel_id=1, replica_groups=mesh['blk'=16,'ffn'=2] {'ffn'}, use_global_device_ids=true, to_apply=%region_62.63 | all-reduce | flops 2 | bytes 16 | tf_op jit(solution)/shard_map/pmax | solution.py:305
  508.9 22.0 %shard_map.112 = bf16[256,2304]{1,0:T(8,128)(2,1)} custom-call(s32[1520]{0:T(1024)} %reshape.2434.field_ref, s32[4]{0:T(128)} %get-tuple-element.369.count_ref, s32[1]{0:T(128)} %bitcast.44.at_ref, bf16[73,256,128]{2,1,0:T(8,128)(2,1)} %copy-done.3, bf16[16,33,128,128]{3,2,1,0:T(8,128)(2,1)} %bitcast.206, f32[36,256,128]{2,1,0:T(8,128)} %get-tuple-element.265.sum_ref, ...), custom_call_target="tpu_custom_call" | custom-call | flops 8858370048 | bytes 17301504 | tf_op jit(solution)/shard_map/pallas_call | solution.py:149
  (457 shorter events, 66.1 us)
Async XLA Ops:
  6.5 252.5 %all-gather.14.cloned.1.call-start = ((), (), s32[]{:S(2)}) async-start(), calls=%async_computation.1 | async-start | bytes 44564480 | tf_op jit(solution)/shard_map/all_gather | solution.py:218
  10.1 48.2 %copy-start = (bf16[1,1,101,128,128]{4,3,2,1,0:T(8,128)(2,1)S(1)}, bf16[1,1,101,128,128]{4,3,2,1,0:T(8,128)(2,1)}, u32[]{:S(2)}) copy-start(bf16[1,1,101,128,128]{4,3,2,1,0:T(8,128)(2,1)} %param.22) | copy-start | bytes 9928708
  10.1 400.7 %all-gather.12.cloned.1.call-start = ((), (), s32[]{:S(2)}) async-start(), calls=%async_computation | async-start | bytes 36765696 | tf_op jit(solution)/shard_map/all_gather | solution.py:218
  40.4 129.4 %copy-start.15 = (s32[2,2,4]{2,1,0:T(2,128)}, s32[2,2,4]{2,1,0:T(2,128)S(1)}, u32[]{:S(2)}) copy-start(s32[2,2,4]{2,1,0:T(2,128)S(1)} %rev.59) | copy-start | bytes 196
  45.5 124.7 %copy-start.17 = (s32[2,2,4]{2,1,0:T(2,128)}, s32[2,2,4]{2,1,0:T(2,128)S(1)}, u32[]{:S(2)}) copy-start(s32[2,2,4]{2,1,0:T(2,128)S(1)} %rev.65) | copy-start | bytes 196
  64.3 19.0 %collective-permute-start.2 = (bf16[28,128,128]{2,1,0:T(8,128)(2,1)}, bf16[28,128,128]{2,1,0:T(8,128)(2,1)}, u32[]{:S(2)}, u32[]{:S(2)}) collective-permute-start(bf16[28,128,128]{2,1,0:T(8,128)(2,1)} %gather_fusion.1), channel_id=1, source_target_pairs={{0,2},{2,0},{4,6},{6,4},{8,10},{10,8},{12,14},{14,12},{16,18},{18,... | collective-permute-start | bytes 2752520 | tf_op jit(solution)/shard_map/ppermute | solution.py:279
  91.5 34.4 %collective-permute-start.3 = (bf16[22,128,128]{2,1,0:T(8,128)(2,1)}, bf16[22,128,128]{2,1,0:T(8,128)(2,1)S(1)}, u32[]{:S(2)}, u32[]{:S(2)}) collective-permute-start(bf16[22,128,128]{2,1,0:T(8,128)(2,1)} %gather_fusion.2), channel_id=1, source_target_pairs={{0,4},{2,6},{4,0},{6,2},{8,12},{10,14},{12,8},{14,10},{16,20},{18,... | collective-permute-start | bytes 2162696 | tf_op jit(solution)/shard_map/ppermute | solution.py:279
  93.5 33.2 %copy-start.2 = (bf16[21,128,128]{2,1,0:T(8,128)(2,1)S(1)}, bf16[21,128,128]{2,1,0:T(8,128)(2,1)}, u32[]{:S(2)}) copy-start(bf16[21,128,128]{2,1,0:T(8,128)(2,1)} %copy-done.1) | copy-start | bytes 2064388
  135.5 22.7 %collective-permute-start.4 = (bf16[14,128,128]{2,1,0:T(8,128)(2,1)S(1)}, bf16[14,128,128]{2,1,0:T(8,128)(2,1)S(1)}, u32[]{:S(2)}, u32[]{:S(2)}) collective-permute-start(bf16[14,128,128]{2,1,0:T(8,128)(2,1)S(1)} %gather_fusion.3), channel_id=1, source_target_pairs={{0,8},{2,10},{4,12},{6,14},{8,0},{10,2},{12,4},{14,6},{16,24},{18,... | collective-permute-start | bytes 1376264 | tf_op jit(solution)/shard_map/ppermute | solution.py:279
  136.2 28.4 %copy-start.64 = (s32[269]{0:T(512)}, s32[269]{0:T(512)S(1)}, u32[]{:S(2)}) copy-start(s32[269]{0:T(512)S(1)} %pad_select_fusion.1) | copy-start | bytes 3232
  164.3 18.6 %copy-start.51 = (s32[16]{0:T(128)S(1)}, s32[16]{0:T(128)}, u32[]{:S(2)}) copy-start(s32[16]{0:T(128)} %copy-done.50) | copy-start | bytes 196
  164.4 342.8 %all-gather.16.cloned.1.call-start = ((), (), s32[]{:S(2)}) async-start(), calls=%async_computation.2 | async-start | bytes 18382848 | tf_op jit(solution)/shard_map/all_gather | solution.py:218
  164.8 20.7 %copy-start.37 = (s32[2,2,4]{2,1,0:T(2,128)S(1)}, s32[2,2,4]{2,1,0:T(2,128)}, u32[]{:S(2)}) copy-start(s32[2,2,4]{2,1,0:T(2,128)} %get-tuple-element.388) | copy-start | bytes 196
  164.8 20.7 %copy-start.38 = (s32[2,2,4]{2,1,0:T(2,128)S(1)}, s32[2,2,4]{2,1,0:T(2,128)}, u32[]{:S(2)}) copy-start(s32[2,2,4]{2,1,0:T(2,128)} %get-tuple-element.389) | copy-start | bytes 196
  164.8 20.8 %copy-start.60 = (s32[16]{0:T(128)S(1)}, s32[16]{0:T(128)}, u32[]{:S(2)}) copy-start(s32[16]{0:T(128)} %get-tuple-element.383) | copy-start | bytes 196
  164.8 23.4 %copy-start.43 = (s32[16]{0:T(128)S(1)}, s32[16]{0:T(128)}, u32[]{:S(2)}) copy-start(s32[16]{0:T(128)} %copy-done.42) | copy-start | bytes 196
  164.8 23.4 %copy-start.45 = (s32[16]{0:T(128)S(1)}, s32[16]{0:T(128)}, u32[]{:S(2)}) copy-start(s32[16]{0:T(128)} %copy-done.44) | copy-start | bytes 196
  164.8 23.4 %copy-start.47 = (s32[16]{0:T(128)S(1)}, s32[16]{0:T(128)}, u32[]{:S(2)}) copy-start(s32[16]{0:T(128)} %copy-done.46) | copy-start | bytes 196
  164.8 23.4 %copy-start.49 = (s32[16]{0:T(128)S(1)}, s32[16]{0:T(128)}, u32[]{:S(2)}) copy-start(s32[16]{0:T(128)} %copy-done.48) | copy-start | bytes 196
  164.8 23.4 %copy-start.67 = (s32[16]{0:T(128)S(1)}, s32[16]{0:T(128)}, u32[]{:S(2)}) copy-start(s32[16]{0:T(128)} %copy-done.66) | copy-start | bytes 196
  164.8 23.4 %copy-start.69 = (s32[16]{0:T(128)S(1)}, s32[16]{0:T(128)}, u32[]{:S(2)}) copy-start(s32[16]{0:T(128)} %copy-done.68) | copy-start | bytes 196
  169.5 23.9 %copy-start.58 = (s32[16]{0:T(128)S(1)}, s32[16]{0:T(128)}, u32[]{:S(2)}) copy-start(s32[16]{0:T(128)} %get-tuple-element.376) | copy-start | bytes 196
  169.5 36.8 %copy-start.71 = (s32[16]{0:T(128)S(1)}, s32[16]{0:T(128)}, u32[]{:S(2)}) copy-start(s32[16]{0:T(128)} %copy-done.70) | copy-start | bytes 196
  217.6 25.6 %copy-start.6 = (s32[4,132]{0,1:T(8,128)}, s32[4,132]{0,1:T(8,128)S(1)}, u32[]{:S(2)}) copy-start(s32[4,132]{0,1:T(8,128)S(1)} %copy.332) | copy-start | bytes 6340
  426.8 47.9 %copy-start.3 = (bf16[73,256,128]{2,1,0:T(8,128)(2,1)}, bf16[73,256,128]{2,1,0:T(8,128)(2,1)S(1)}, u32[]{:S(2)}) copy-start(bf16[73,256,128]{2,1,0:T(8,128)(2,1)S(1)} %shard_map.110.x_ref) | copy-start | bytes 14352388
  426.8 49.6 %copy-start.7 = (s32[4,132]{0,1:T(8,128)S(1)}, s32[4,132]{0,1:T(8,128)}, u32[]{:S(2)}) copy-start(s32[4,132]{0,1:T(8,128)} %copy-done.6) | copy-start | bytes 6340
  426.8 49.5 %copy-start.9 = (s32[4,132]{0,1:T(8,128)S(1)}, s32[4,132]{0,1:T(8,128)}, u32[]{:S(2)}) copy-start(s32[4,132]{0,1:T(8,128)} %copy.339) | copy-start | bytes 6340
  426.8 49.5 %copy-start.10 = (s32[4,132]{0,1:T(8,128)S(1)}, s32[4,132]{0,1:T(8,128)}, u32[]{:S(2)}) copy-start(s32[4,132]{0,1:T(8,128)} %copy.337) | copy-start | bytes 6340
  426.8 49.5 %copy-start.11 = (pred[4,132]{0,1:T(8,128)(4,1)S(1)}, pred[4,132]{0,1:T(8,128)(4,1)}, u32[]{:S(2)}) copy-start(pred[4,132]{0,1:T(8,128)(4,1)} %copy.338) | copy-start | bytes 1588
  426.9 49.5 %copy-start.12 = (pred[4,132]{0,1:T(8,128)(4,1)S(1)}, pred[4,132]{0,1:T(8,128)(4,1)}, u32[]{:S(2)}) copy-start(pred[4,132]{0,1:T(8,128)(4,1)} %copy.340) | copy-start | bytes 1588
  474.7 29.6 %copy-start.36 = (f32[2304]{0:T(1024)S(1)}, f32[2304]{0:T(1024)}, u32[]{:S(2)}) copy-start(f32[2304]{0:T(1024)} %param.25) | copy-start | bytes 27652
  476.1 31.0 %collective-permute-start.5 = (bf16[256,2304]{1,0:T(8,128)(2,1)S(1)}, bf16[256,2304]{1,0:T(8,128)(2,1)S(1)}, u32[]{:S(2)}, u32[]{:S(2)}) collective-permute-start(bf16[256,2304]{1,0:T(8,128)(2,1)S(1)} %constant_dynamic-slice_fusion.3), channel_id=1, source_target_pairs={{0,1},{1,0},{2,3},{3,2},{4,5},{5,4},{6,7},{7,6},{8,9},{9,8},{10,11... | collective-permute-start | bytes 3538952 | tf_op jit(solution)/shard_map/ppermute | solution.py:367
  (51 other events, 385.3 us)
Sparse Core Ops, SparseCore 0:
  10.3 225.3 all-gather.13
  237.3 173.4 all-gather.11
  412.4 91.5 all-gather.15

commit v6 on v5

--- a/solution.py
+++ b/solution.py
@@ -8,54 +8,52 @@
 from jax.sharding import PartitionSpec as P
 
 UNROLL = 4
-STEPS = 4
 VMEM_BYTES = 56 * 1024 * 1024
-
-
-def pair_up(rows, cols, live, blocks, zero_row):
+LAST_VMEM_BYTES = 36 * 1024 * 1024
+
+
+def group_up(rows, cols, live, blocks, zero_row, group):
     listed = rows.shape[1]
     ids = jnp.arange(listed, dtype=jnp.int32)
     block_ids = jnp.arange(blocks, dtype=jnp.int32)
-    size = -(-((listed + min(blocks, listed)) // 2) // UNROLL) * UNROLL
+    most = (listed + (group - 1) * min(blocks, listed)) // group
+    size = -(-most // UNROLL) * UNROLL
     same = live[:, None, :] & (cols[:, :, None] == cols[:, None, :]) & (ids < ids[:, None])
     rank = jnp.sum(same.astype(jnp.int32), axis=2)
     in_block = live[:, None, :] & (cols[:, None, :] == block_ids[:, None])
-    need = (jnp.sum(in_block.astype(jnp.int32), axis=2) + 1) // 2
+    need = (jnp.sum(in_block.astype(jnp.int32), axis=2) + group - 1) // group
     begin = jnp.cumsum(need, axis=1) - need
     begin = jnp.sum(jnp.where(cols[:, :, None] == block_ids, begin[:, None, :], 0), axis=2)
-    place = jnp.where(live, begin + rank // 2, -1)
+    place = jnp.where(live, begin + rank // group, -1)
     hit = place[:, None, :] == jnp.arange(size, dtype=jnp.int32)[:, None]
-    odd = (rank % 2 == 1)[:, None, :]
+    turn = (rank % group)[:, None, :]
 
     def chosen(mask, values, default):
         found = jnp.sum(jnp.where(mask, values[:, None, :] - default, 0), axis=2)
         return found + default
 
     tile_ids = jnp.broadcast_to(ids, rows.shape)
-    fields = [
-        chosen(hit & ~odd, tile_ids, 0),
-        chosen(hit & ~odd, rows, zero_row),
-        chosen(hit & odd, tile_ids, 0),
-        chosen(hit & odd, rows, zero_row),
-        chosen(hit & ~odd, cols, 0),
-    ]
+    fields = [chosen(hit & (turn == 0), cols, 0)]
+    fields += [chosen(hit & (turn == g), tile_ids, 0) for g in range(group)]
+    fields += [chosen(hit & (turn == g), rows, zero_row) for g in range(group)]
     return jnp.stack(fields).reshape(-1), jnp.sum(need, axis=1)
 
 
-def add_block(field_ref, count_ref, x_ref, w_ref, acc):
+def add_block(field_ref, count_ref, x_ref, w_ref, acc, group):
     step, steps = pl.program_id(0), pl.num_programs(0)
     w_ref = w_ref.reshape(-1, *w_ref.shape[2:])
-    size = field_ref.shape[0] // (5 * steps)
-
-    def pair(at):
-        tile0, row0, tile1, row1, col = (field_ref[(f * steps + step) * size + at] for f in range(5))
-        left = jnp.concatenate([x_ref[row0], x_ref[row1]], axis=1)
-        right = jnp.concatenate([w_ref[tile0], w_ref[tile1]], axis=0)
+    fields = 2 * group + 1
+    size = field_ref.shape[0] // (fields * steps)
+
+    def one(at):
+        col, *parts = (field_ref[(f * steps + step) * size + at] for f in range(fields))
+        left = jnp.concatenate([x_ref[row] for row in parts[group:]], axis=1)
+        right = jnp.concatenate([w_ref[tile] for tile in parts[:group]], axis=0)
         acc[col] += jnp.dot(left, right, preferred_element_type=jnp.float32)
 
     def several(turn, carry):
         for u in range(UNROLL):
-            pair(turn * UNROLL + u)
+            one(turn * UNROLL + u)
         return carry
 
     lax.fori_loop(0, lax.div(count_ref[step] + UNROLL - 1, jnp.int32(UNROLL)), several, 0)
@@ -65,7 +63,7 @@
     pl.when(pl.program_id(0) == pl.num_programs(0) - 1)(work)
 
 
-def first_kernel(field_ref, count_ref, at_ref, x_ref, w_ref, bias_ref, sum_ref, acc):
+def first_kernel(group, field_ref, count_ref, at_ref, x_ref, w_ref, bias_ref, sum_ref, acc):
     @pl.when(pl.program_id(0) == 0)
     def _():
         def fill(c, carry):
@@ -74,21 +72,21 @@
 
         lax.fori_loop(0, acc.shape[0], fill, 0)
 
-    add_block(field_ref, count_ref, x_ref, w_ref, acc)
+    add_block(field_ref, count_ref, x_ref, w_ref, acc, group)
 
     @at_end
     def _():
         sum_ref[...] = acc[...]
 
 
-def hidden_kernel(field_ref, count_ref, at_ref, x_ref, w_ref, sum_ref, out_ref, acc):
+def hidden_kernel(group, field_ref, count_ref, at_ref, x_ref, w_ref, sum_ref, out_ref, acc):
     blocks = acc.shape[0]
 
     @pl.when(pl.program_id(0) == 0)
     def _():
         acc[...] = sum_ref[...]
 
-    add_block(field_ref, count_ref, x_ref, w_ref, acc)
+    add_block(field_ref, count_ref, x_ref, w_ref, acc, group)
 
     @at_end
     def _():
@@ -100,30 +98,29 @@
         out_ref[blocks] = jnp.zeros(out_ref.shape[1:], out_ref.dtype)
 
 
-def partial_kernel(field_ref, count_ref, at_ref, x_ref, w_ref, sum_ref, out_ref, acc):
+def partial_kernel(group, field_ref, count_ref, at_ref, x_ref, w_ref, sum_ref, out_ref):
     @pl.when(pl.program_id(0) == 0)
     def _():
-        acc[...] = jnp.zeros_like(acc)
-
-    add_block(field_ref, count_ref, x_ref, w_ref, acc)
+        sum_ref[...] = jnp.zeros_like(sum_ref)
+
+    add_block(field_ref, count_ref, x_ref, w_ref, sum_ref, group)
 
     @at_end
     def _():
-        width = acc.shape[2]
-        sum_ref[...] = acc[...]
-        for c in range(acc.shape[0]):
-            out_ref[:, c * width : (c + 1) * width] = acc[c].astype(out_ref.dtype)
+        width = sum_ref.shape[2]
+        for c in range(sum_ref.shape[0]):
+            out_ref[:, c * width : (c + 1) * width] = sum_ref[c].astype(out_ref.dtype)
 
 
 def result_kernel(
-    field_ref, count_ref, at_ref,
+    group, field_ref, count_ref, at_ref,
     x_ref, w_ref, sum_ref, token_ref, other_ref, bias_ref, out_ref, acc,
 ):
     @pl.when(pl.program_id(0) == 0)
     def _():
         acc[...] = sum_ref[...]
 
-    add_block(field_ref, count_ref, x_ref, w_ref, acc)
+    add_block(field_ref, count_ref, x_ref, w_ref, acc, group)
 
     @at_end
     def _():
@@ -136,18 +133,26 @@
 
 
 def fixed(shape):
-    return pl.BlockSpec(shape, lambda i, *_: (0,) * len(shape))
-
-
-def tile_pass(kernel, rows, cols, live, at, x, tiles, more, more_specs, out_shapes, blocks):
+    return pl.BlockSpec(shape, lambda i, *_: (0,) * len(shape), pipeline_mode=pl.Buffered(1))
+
+
+def planned(rows, cols, live, blocks, zero_row, steps, group):
+    steps = steps if rows.shape[0] % steps == 0 else 1
+    return group_up(*(v.reshape(steps, -1) for v in (rows, cols, live)), blocks, zero_row, group)
+
+
+def tile_pass(
+    kernel, rows, cols, live, at, x, tiles, more, more_specs, out_shapes, blocks,
+    steps=4, group=2, scratch=True, vmem=VMEM_BYTES, plan=None,
+):
     shards, slots = rows.shape
     side, tokens = tiles.shape[-1], x.shape[1]
-    steps = STEPS if shards % STEPS == 0 else 1
-    listed = shards // steps * slots
-    per_step = lambda v: v.reshape(steps, listed)
-    fields, counts = pair_up(per_step(rows), per_step(cols), per_step(live), blocks, x.shape[0] - 1)
+    steps = steps if shards % steps == 0 else 1
+    if plan is None:
+        plan = planned(rows, cols, live, blocks, x.shape[0] - 1, steps, group)
+    fields, counts = plan
     return pl.pallas_call(
-        kernel,
+        functools.partial(kernel, group),
         out_shape=out_shapes,
         grid_spec=pltpu.PrefetchScalarGridSpec(
             num_scalar_prefetch=3,
@@ -157,10 +162,12 @@
                 pl.BlockSpec((shards // steps, slots, side, side), lambda i, *_: (i, 0, 0, 0)),
                 *more_specs,
             ],
-            out_specs=[fixed(o.shape) for o in out_shapes],
-            scratch_shapes=[pltpu.VMEM((blocks, tokens, side), jnp.float32)],
+            out_specs=[
+                pl.BlockSpec(o.shape, lambda i, *_, rank=len(o.shape): (0,) * rank) for o in out_shapes
+            ],
+            scratch_shapes=[pltpu.VMEM((blocks, tokens, side), jnp.float32)] if scratch else [],
         ),
-        compiler_params=pltpu.CompilerParams(vmem_limit_bytes=VMEM_BYTES),
+        compiler_params=pltpu.CompilerParams(vmem_limit_bytes=vmem),
         cost_estimate=pl.CostEstimate(
             flops=4 * shards * slots * tokens * side * side,
             bytes_accessed=shards * slots * side * side * 2,
@@ -204,11 +211,11 @@
     aligned = share % side == 0
     opening = slots * 4 // 5
     rest = slots - opening
-    held = slots - slots // 40
-    late_from = held - slots // 3
+    held = slots
+    late_from = held - slots * 3 // 10
     levels = [
         (stride, max(slots // most, 1), max(slots // least, 1))
-        for stride, most, least in ((1, 6, 8), (2, 8, 10), (4, 12, 16))
+        for stride, most, least in ((1, 6, 8), (2, 12, 16), (4, 16, 24))
         if shards % (2 * stride) == 0
     ]
     slot_ids = jnp.arange(slots, dtype=jnp.int32)
@@ -303,7 +310,6 @@
     chunk = slots // 4
     misplaced = jnp.stack([jnp.max(fronts) - late_from, jnp.max(lengths) - held])
     misplaced = lax.pmax(misplaced, "ffn")
-    some_late = jnp.max(misplaced) > 0
 
     rows_f = tokens.astype(jnp.float32)
     center = jnp.mean(rows_f, axis=1, keepdims=True)
@@ -311,6 +317,8 @@
     normed = ((rows_f - center) / jnp.sqrt(spread + 1e-05) * ln_gain + ln_bias).astype(jnp.bfloat16)
     normed_blocks = normed.reshape(token_rows, second_blocks, side).transpose(1, 0, 2)
     normed_blocks = jnp.pad(normed_blocks, ((0, 1), (0, 0), (0, 0)))
+    normed_blocks, misplaced = lax.optimization_barrier((normed_blocks, misplaced))
+    some_late = jnp.max(misplaced) > 0
 
     (total,) = tile_pass(
         first_kernel,
@@ -355,6 +363,9 @@
                 jax.ShapeDtypeStruct((token_rows, width), jnp.bfloat16),
             ],
             second_blocks,
+            steps=2,
+            group=4,
+            scratch=False,
         )
 
     def own_cols(value):
@@ -392,33 +403,51 @@
 
         return lax.fori_loop(0, (misplaced[1] + chunk - 1) // chunk, one_more, branch)
 
-    branch = lax.cond(some_late, with_late, lambda branch: branch, branch)
-
     if not aligned:
+        branch = lax.cond(some_late, with_late, lambda branch: branch, branch)
         more, _ = second_pass(last_codes, last_own, tiles2b)
         own = (total + more).transpose(1, 0, 2).reshape(token_rows, width)
         return (own_cols(tokens) + own_cols(own) + branch + fc2_bias).astype(jnp.bfloat16)
 
     share_blocks = share // side
-    (result,) = tile_pass(
+    last_rows, last_cols = last_codes // second_blocks, last_codes % second_blocks % share_blocks
+    last_plan = planned(last_rows, last_cols, last_own, share_blocks, first_blocks, 2, 4)
+    last_plan, branch = lax.optimization_barrier((last_plan, branch))
+    last_pass = functools.partial(
+        tile_pass,
         result_kernel,
-        last_codes // second_blocks,
-        last_codes % second_blocks % share_blocks,
+        last_rows,
+        last_cols,
         last_own,
         ffn,
         hidden,
         tiles2b,
-        [total, tokens, branch, fc2_bias.reshape(1, share)],
-        [
-            pl.BlockSpec((share_blocks, token_rows, side), lambda i, fields, counts, at: (at[0], 0, 0)),
-            pl.BlockSpec((token_rows, share), lambda i, fields, counts, at: (0, at[0])),
+        more_specs=[
+            pl.BlockSpec(
+                (share_blocks, token_rows, side),
+                lambda i, fields, counts, at: (at[0], 0, 0),
+                pipeline_mode=pl.Buffered(1),
+            ),
+            pl.BlockSpec(
+                (token_rows, share),
+                lambda i, fields, counts, at: (0, at[0]),
+                pipeline_mode=pl.Buffered(1),
+            ),
             fixed((token_rows, share)),
             fixed((1, share)),
         ],
-        [jax.ShapeDtypeStruct((token_rows, share), jnp.bfloat16)],
-        share_blocks,
-    )
-    return result
+        out_shapes=[jax.ShapeDtypeStruct((token_rows, share), jnp.bfloat16)],
+        blocks=share_blocks,
+        steps=2,
+        group=4,
+        vmem=LAST_VMEM_BYTES,
+        plan=last_plan,
+    )
+
+    def finished(branch):
+        return last_pass(more=[total, tokens, branch, fc2_bias.reshape(1, share)])[0]
+
+    return lax.cond(some_late, lambda branch: finished(with_late(branch)), finished, branch)
 
 
 def solution(mesh):

time: 548 us -> 575 us (1.049)
  other arithmetic: 103 us -> 141 us
  blocking collectives: 50 us -> 28.1 us
  local copies, waits for them, and re-layouts: 65.5 us -> 82 us
  Pallas kernels: 147 us -> 133 us
  waiting for transfers between devices: 140 us -> 148 us
    reduce_sum x4, other arithmetic: 19.6 us -> 56 us  [chosen(): found = jnp.sum(jnp.where(mask, values[:, None, :] - default, 0), axis=2)]
    pmax x1, blocking collectives: 26.9 us -> 5.02 us  [on_device(): misplaced = lax.pmax(misplaced, 'ffn')]
    ppermute x3, waiting for transfers between devices: 49.1 us -> 34.3 us  [on_device(): lax.ppermute(jnp.take(sources, sending, axis=0, mode='clip'), 'blk', [(i,...]
    pallas_call x4, Pallas kernels: 147 us -> 133 us  [tile_pass(): pl.pallas_call(functools.partial(kernel, group), out_shape=out_shapes, gr...]
    ppermute x1, waiting for transfers between devices: 0.01 us -> 11.5 us  [from_others(): lax.ppermute(lax.dynamic_slice_in_dim(partial_value, to * share, share, 1...]
    all_gather x3, waiting for transfers between devices: 90.5 us -> 102 us  [gathered(): lax.all_gather(value, 'blk', axis=0, tiled=True)]
    unnamed x168 -> x163, local copies, waits for them, and re-layouts: 13 us -> 23.6 us
  transfers between devices with their start and end apart: 7 -> 7, of which waited for: 3 -> 5; matrix products, arithmetic and copies ran while one was open for 30% -> 38% of each run, Pallas kernels for 23% -> 21%
where the time goes in v6:
time: 575 us; the launch traced here: 565 us
  waiting for transfers between devices  148 us (26%)
  other arithmetic  141 us (25%)
  Pallas kernels  133 us (23%)
  local copies, waits for them, and re-layouts  82 us (14%)
  between operations  29.9 us (5%)
  blocking collectives  28.1 us (5%)
    pallas_call x4, Pallas kernels, tile_pass(): pl.pallas_call(functools.partial(kernel, group), out_shape=out_shapes, gr...  133 us
    all_gather x3, waiting for transfers between devices, gathered(): lax.all_gather(value, 'blk', axis=0, tiled=True)  102 us
    reduce_sum x4, other arithmetic, chosen(): found = jnp.sum(jnp.where(mask, values[:, None, :] - default, 0), axis=2)  56 us
    reduce_sum x8, other arithmetic, moved(): return jnp.sum(jnp.where(hit, values[:, None, :], 0), axis=2)  36.9 us
    ppermute x3, waiting for transfers between devices, on_device(): lax.ppermute(jnp.take(sources, sending, axis=0, mode='clip'), 'blk', [(i,...  34.3 us
    unnamed x163, local copies, waits for them, and re-layouts  23.6 us
    all_gather x1, blocking collectives, on_device(): meta = lax.all_gather(meta, 'blk', axis=0, tiled=True)  23.1 us
  transfers between devices with their start and end apart: 7, of which 5 were waited for; matrix products, arithmetic and copies ran while one was open for 38% of the time, Pallas kernels for 21%

profile of v6, /device:TPU:0, one launch (start us, length us, event | category | flops | bytes accessed | tf_op | source)
XLA Modules:
  0.0 565.1 jit_solution(17827845032476266544)
XLA Ops:
  6.5 3.8 slice.95
  12.1 23.1 %all-gather.4 = s32[16,1,204]{2,1,0:T(1,128)S(1)} all-gather(s32[1,1,204]{2,1,0:T(1,128)S(1)} %add_bitcast_fusion.10), channel_id=1, replica_groups=mesh['blk'=16,'ffn'=2] {'blk'}, dimensions={0}, use_global_device_ids=true | all-gather | bytes 13872 | tf_op jit(solution)/shard_map/all_gather | solution.py:229
  52.7 2.6 compare_select_fusion.7
  59.8 3.8 gather_fusion.1
  73.3 6.1 %fusion.38 = s32[269]{0:T(512)S(1)} fusion(s32[269]{0:T(512)S(1)} %iota_subtract_fusion.7, s32[269]{0:T(512)S(1)} %pad.58), kind=kLoop, calls=%fused_computation.185 | loop fusion | flops 216814 | bytes 3228 | tf_op jit(solution)/shard_map/reduce_sum | solution.py:186
  85.0 4.1 pad_maximum_fusion.1
  89.1 3.8 gather_fusion.2
  94.9 21.3 %collective-permute-done.3 = bf16[14,128,128]{2,1,0:T(8,128)(2,1)S(1)} collective-permute-done((bf16[14,128,128]{2,1,0:T(8,128)(2,1)}, bf16[14,128,128]{2,1,0:T(8,128)(2,1)S(1)}, u32[]{:S(2)}, u32[]{:S(2)}) %collective-permute-start.3) | collective-permute-done | bytes 458784 | tf_op jit(solution)/shard_map/ppermute | solution.py:286
  116.9 5.4 pad_maximum_fusion
  122.3 3.4 gather_fusion.3
  129.9 13.0 %collective-permute-done.4 = bf16[10,128,128]{2,1,0:T(8,128)(2,1)S(1)} collective-permute-done((bf16[10,128,128]{2,1,0:T(8,128)(2,1)S(1)}, bf16[10,128,128]{2,1,0:T(8,128)(2,1)S(1)}, u32[]{:S(2)}, u32[]{:S(2)}) %collective-permute-start.4) | collective-permute-done | bytes 327712 | tf_op jit(solution)/shard_map/ppermute | solution.py:286
  143.7 5.2 gather_fusion.4
  149.3 4.3 gather_fusion.5
  155.7 5.0 pmax.7
  182.6 2.4 select_reduce_fusion.25
  185.2 12.8 %select_reduce_fusion.24 = s32[16,122]{0,1:T(8,128)S(1)} fusion(s32[16,122]{1,0:T(8,128)S(1)} %bitcast.240, s32[16,122]{0,1:T(8,128)S(1)} %iota_subtract_fusion.1), kind=kLoop, calls=%fused_computation.142 | loop fusion | flops 712480 | bytes 23424 | tf_op jit(solution)/shard_map/reduce_sum | solution.py:186
  198.2 5.9 %select_reduce_fusion.18 = s32[16,269]{0,1:T(8,128)S(1)} fusion(s32[16,269]{1,0:T(8,128)S(1)} %pad.50, s32[16,269]{0,1:T(8,128)S(1)} %iota_subtract_fusion), kind=kLoop, calls=%fused_computation.117 | loop fusion | flops 3469024 | bytes 51648 | tf_op jit(solution)/shard_map/reduce_sum | solution.py:186
  209.1 11.8 %fusion.48 = (s32[2,76]{0,1:T(8,128)S(1)}, s32[2,76]{0,1:T(8,128)S(1)}, s32[2,76]{0,1:T(8,128)S(1)}, s32[2,76]{0,1:T(8,128)}, s32[2,76]{0,1:T(8,128)S(1)}, /*ind...) fusion(pred[2,240]{1,0:T(4,128)(4,1)S(1)} %get-tuple-element.567, ...), kind=kLoop, calls=%fused_computation.213 | loop fusion | flops 837672 | bytes 13152 | tf_op jit(solution)/shard_map/reduce_sum | solution.py:32
  227.1 17.0 %select_reduce_fusion.19 = (s32[4,196]{0,1:T(8,128)S(1)}, s32[4,196]{0,1:T(8,128)S(1)}, s32[4,196]{0,1:T(8,128)S(1)}, s32[4,196]{0,1:T(8,128)S(1)}, s32[4,196]{0,1:T(8,128)S(1)}) fusion(s32[4,320]{1,0:T(4,128)S(1)} %sub.1149, s32[4,320]{1,0:T(4,128)S(1)} %fusion.111, pred[4,320]{1,0:T(4,128)(4,1)S(1)} %broadcast_compare_fusion.14, ...), kind=kLoop, calls=%fused_computation.134 | loop fusion | flops 3257520 | bytes 33600 | tf_op jit(solution)/shard_map/reduce_sum | solution.py:32
  246.7 26.7 %fusion.33 = (s32[2,172]{0,1:T(8,128)S(1)}, s32[2,172]{0,1:T(8,128)S(1)}, s32[2,172]{0,1:T(8,128)S(1)}, s32[2,172]{0,1:T(8,128)S(1)}, s32[2,172]{0,1:T(8,128)S(1...) fusion(pred[2,568]{1,0:T(4,128)(4,1)S(1)} %get-tuple-element.562, ...), kind=kLoop, calls=%fused_computation.165 | loop fusion | flops 4490920 | bytes 30560 | tf_op jit(solution)/shard_map/reduce_sum | solution.py:32
  275.1 2.8 copy.223
  279.3 3.4 fusion.25
  282.7 3.0 copy.224
  287.4 60.9 %shard_map.111.sum_ref = f32[72,256,128]{2,1,0:T(8,128)} custom-call(s32[3920]{0:T(1024)} %reshape.2592.field_ref, s32[4]{0:T(128)} %get-tuple-element.494.count_ref, s32[1]{0:T(128)} %bitcast.70.at_ref, bf16[37,256,128]{2,1,0:T(8,128)(2,1)} %pad.47.x_ref, bf16[16,80,128,128]{3,2,1,0:T(8,128)(2,1)} %bitcast.250, f32[72,1,128]{2,1,0:T(1,128)} %bitcast.252), custom_call_target="tpu_custom_call" | custom-call | flops 21474836480 | bytes 41943040 | tf_op jit(solution)/shard_map/pallas_call | solution.py:154
  348.3 69.4 %all-gather.12.cloned.1.call-done = bf16[1136,128,128]{2,1,0:T(8,128)(2,1)} async-done(((bf16[71,128,128]{2,1,0:T(8,128)(2,1)}), bf16[1136,128,128]{2,1,0:T(8,128)(2,1)}) %all-gather.12.cloned.1.call-update) | async-done | bytes 37224464 | tf_op jit(solution)/shard_map/all_gather | solution.py:225
  417.7 14.0 %shard_map.112.x_ref = bf16[73,256,128]{2,1,0:T(8,128)(2,1)S(1)} custom-call(s32[1600]{0:T(1024)} %reshape.2588.field_ref, s32[4]{0:T(128)} %get-tuple-element.512.count_ref, s32[1]{0:T(128)} %bitcast.70.at_ref, bf16[37,256,128]{2,1,0:T(8,128)(2,1)} %pad.47.x_ref, bf16[16,71,128,128]{3,2,1,0:T(8,128)(2,1)} %bitcast.198, f32[72,256,128]{2,1,0:T(8,128)} %shard_map.111.sum_ref), custom_call_target="tpu_custom_call" | custom-call | flops 5637144576 | bytes 11010048 | tf_op jit(solution)/shard_map/pallas_call | solution.py:154
  431.7 43.7 %shard_map.113 = (f32[36,256,128]{2,1,0:T(8,128)}, bf16[256,4608]{1,0:T(8,128)(2,1)}) custom-call(s32[3096]{0:T(1024)} %reshape.2586.field_ref, s32[2]{0:T(128)} %get-tuple-element.516.count_ref, s32[1]{0:T(128)} %bitcast.70.at_ref, bf16[73,256,128]{2,1,0:T(8,128)(2,1)S(1)} %shard_map.112.x_ref, bf16[16,71,128,128]{3,2,1,0:T(8,128)(2,1)} %bitcast.199), custom_call_target="tpu_custom_call" | custom-call | flops 19058917376 | bytes 37224448 | tf_op jit(solution)/shard_map/pallas_call | solution.py:154
  475.4 2.5 constant_dynamic-slice_fusion.3
  494.8 11.5 %collective-permute-done.5 = bf16[256,2304]{1,0:T(8,128)(2,1)S(1)} collective-permute-done((bf16[256,2304]{1,0:T(8,128)(2,1)}, bf16[256,2304]{1,0:T(8,128)(2,1)S(1)}, u32[]{:S(2)}, u32[]{:S(2)}) %collective-permute-start.5) | collective-permute-done | bytes 1179680 | tf_op jit(solution)/shard_map/ppermute | solution.py:378
  507.9 32.5 %all-gather.16.cloned.1.call-done = bf16[480,128,128]{2,1,0:T(8,128)(2,1)} async-done(((bf16[30,128,128]{2,1,0:T(8,128)(2,1)}), bf16[480,128,128]{2,1,0:T(8,128)(2,1)}) %all-gather.16.cloned.1.call-update) | async-done | bytes 15728656 | tf_op jit(solution)/shard_map/all_gather | solution.py:225
  540.4 16.7 %conditional.1 = (bf16[256,2304]{1,0:T(8,128)(2,1)S(1)}) conditional(s32[]{:T(128)} %convert_element_type.114, (s32[]{:T(128)}, f32[2304]{0:T(1024)}, s32[1368]{0:T(1024)S(1)}, s32[2]{0:T(128)}, bf16[73,256,128]{2,1,0:T(8,128)(2,1)}, /*index=5*/bf16[16,30,128,128]{3,2,1,0:T(8,128)(2,1)}, f32[36,256,128]{2,1,0:T(8,128)}, ...), branch_computations={%region_72.73_spmd, %region_73.104_spmd} | conditional | flops 22824779776 | bytes 126139328 | solution.py:450
  541.1 14.8 %branch_0_fun.1 = bf16[256,2304]{1,0:T(8,128)(2,1)S(1)} custom-call(s32[1368]{0:T(1024)S(1)} %get-tuple-element.350.field_ref, s32[2]{0:T(128)} %get-tuple-element.351.count_ref, s32[1]{0:T(128)} %bitcast.at_ref, bf16[73,256,128]{2,1,0:T(8,128)(2,1)} %get-tuple-element.353.x_ref, bf16[16,30,128,128]{3,2,1,0:T(8,128)(2,1)} %get-tuple-element.354.w_ref, ...), custom_call_target="tpu_custom_call" | custom-call | flops 8053063680 | bytes 15728640 | tf_op jit(solution)/shard_map/cond/branch_0_fun/pallas_call | solution.py:154
  (473 shorter events, 93.8 us)
Async XLA Ops:
  6.5 280.9 %all-gather.14.cloned.1.call-start = ((), (), s32[]{:S(2)}) async-start(), calls=%async_computation.1 | async-start | bytes 44564480 | tf_op jit(solution)/shard_map/all_gather | solution.py:225
  10.3 47.3 %copy-start = (bf16[1,1,101,128,128]{4,3,2,1,0:T(8,128)(2,1)S(1)}, bf16[1,1,101,128,128]{4,3,2,1,0:T(8,128)(2,1)}, u32[]{:S(2)}) copy-start(bf16[1,1,101,128,128]{4,3,2,1,0:T(8,128)(2,1)} %param.22) | copy-start | bytes 9928708
  10.3 407.4 %all-gather.12.cloned.1.call-start = ((), (), s32[]{:S(2)}) async-start(), calls=%async_computation | async-start | bytes 39550976 | tf_op jit(solution)/shard_map/all_gather | solution.py:225
  63.6 21.4 %collective-permute-start.2 = (bf16[28,128,128]{2,1,0:T(8,128)(2,1)}, bf16[28,128,128]{2,1,0:T(8,128)(2,1)}, u32[]{:S(2)}, u32[]{:S(2)}) collective-permute-start(bf16[28,128,128]{2,1,0:T(8,128)(2,1)} %gather_fusion.1), channel_id=1, source_target_pairs={{0,2},{2,0},{4,6},{6,4},{8,10},{10,8},{12,14},{14,12},{16,18},{18,... | collective-permute-start | bytes 2752520 | tf_op jit(solution)/shard_map/ppermute | solution.py:286
  92.9 23.2 %collective-permute-start.3 = (bf16[14,128,128]{2,1,0:T(8,128)(2,1)}, bf16[14,128,128]{2,1,0:T(8,128)(2,1)S(1)}, u32[]{:S(2)}, u32[]{:S(2)}) collective-permute-start(bf16[14,128,128]{2,1,0:T(8,128)(2,1)} %gather_fusion.2), channel_id=1, source_target_pairs={{0,4},{2,6},{4,0},{6,2},{8,12},{10,14},{12,8},{14,10},{16,20},{18,... | collective-permute-start | bytes 1376264 | tf_op jit(solution)/shard_map/ppermute | solution.py:286
  92.9 24.0 %copy-start.5 = (bf16[21,128,128]{2,1,0:T(8,128)(2,1)S(1)}, bf16[21,128,128]{2,1,0:T(8,128)(2,1)}, u32[]{:S(2)}) copy-start(bf16[21,128,128]{2,1,0:T(8,128)(2,1)} %copy-done.4) | copy-start | bytes 2064388
  94.9 30.9 %slice-start = ((s32[269]{0:T(512)}), s32[71]{0:T(128)S(1)}, s32[]{:S(2)}) async-start(s32[269]{0:T(512)} %copy-done.60), calls=%async_computation.4 | async-start | bytes 1024 | tf_op jit(solution)/shard_map/slice | solution.py:308
  125.7 17.2 %collective-permute-start.4 = (bf16[10,128,128]{2,1,0:T(8,128)(2,1)S(1)}, bf16[10,128,128]{2,1,0:T(8,128)(2,1)S(1)}, u32[]{:S(2)}, u32[]{:S(2)}) collective-permute-start(bf16[10,128,128]{2,1,0:T(8,128)(2,1)S(1)} %gather_fusion.3), channel_id=1, source_target_pairs={{0,8},{2,10},{4,12},{6,14},{8,0},{10,2},{12,4},{14,6},{16,24},{18,... | collective-permute-start | bytes 983048 | tf_op jit(solution)/shard_map/ppermute | solution.py:286
  148.9 17.1 %copy-start.21 = (s32[16]{0:T(128)S(1)}, s32[16]{0:T(128)}, u32[]{:S(2)}) copy-start(s32[16]{0:T(128)} %copy-done.20) | copy-start | bytes 196
  149.0 23.2 %copy-start.41 = (s32[16]{0:T(128)S(1)}, s32[16]{0:T(128)}, u32[]{:S(2)}) copy-start(s32[16]{0:T(128)} %copy-done.40) | copy-start | bytes 196
  149.0 23.2 %copy-start.45 = (s32[16]{0:T(128)S(1)}, s32[16]{0:T(128)}, u32[]{:S(2)}) copy-start(s32[16]{0:T(128)} %copy-done.44) | copy-start | bytes 196
  149.0 23.2 %copy-start.65 = (s32[16]{0:T(128)S(1)}, s32[16]{0:T(128)}, u32[]{:S(2)}) copy-start(s32[16]{0:T(128)} %copy-done.64) | copy-start | bytes 196
  149.0 25.8 %copy-start.39 = (s32[16]{0:T(128)S(1)}, s32[16]{0:T(128)}, u32[]{:S(2)}) copy-start(s32[16]{0:T(128)} %copy-done.38) | copy-start | bytes 196
  149.0 25.8 %copy-start.43 = (s32[16]{0:T(128)S(1)}, s32[16]{0:T(128)}, u32[]{:S(2)}) copy-start(s32[16]{0:T(128)} %copy-done.42) | copy-start | bytes 196
  149.0 25.8 %copy-start.63 = (s32[16]{0:T(128)S(1)}, s32[16]{0:T(128)}, u32[]{:S(2)}) copy-start(s32[16]{0:T(128)} %copy-done.62) | copy-start | bytes 196
  149.0 28.4 %copy-start.54 = (s32[16]{0:T(128)S(1)}, s32[16]{0:T(128)}, u32[]{:S(2)}) copy-start(s32[16]{0:T(128)} %get-tuple-element.529) | copy-start | bytes 196
  149.0 30.9 %copy-start.37 = (s32[16]{0:T(128)S(1)}, s32[16]{0:T(128)}, u32[]{:S(2)}) copy-start(s32[16]{0:T(128)} %copy-done.36) | copy-start | bytes 196
  149.1 30.8 %copy-start.49 = (s32[16]{0:T(128)S(1)}, s32[16]{0:T(128)}, u32[]{:S(2)}) copy-start(s32[16]{0:T(128)} %copy-done.48) | copy-start | bytes 196
  149.1 30.9 %copy-start.53 = (s32[16]{0:T(128)S(1)}, s32[16]{0:T(128)}, u32[]{:S(2)}) copy-start(s32[16]{0:T(128)} %copy-done.52) | copy-start | bytes 196
  149.1 33.4 %copy-start.31 = (s32[4,2,2]{2,1,0:T(2,128)S(1)}, s32[4,2,2]{2,1,0:T(2,128)}, u32[]{:S(2)}) copy-start(s32[4,2,2]{2,1,0:T(2,128)} %get-tuple-element.546) | copy-start | bytes 196
  149.1 33.5 %copy-start.47 = (s32[16]{0:T(128)S(1)}, s32[16]{0:T(128)}, u32[]{:S(2)}) copy-start(s32[16]{0:T(128)} %copy-done.46) | copy-start | bytes 196
  149.1 33.5 %copy-start.51 = (s32[16]{0:T(128)S(1)}, s32[16]{0:T(128)}, u32[]{:S(2)}) copy-start(s32[16]{0:T(128)} %copy-done.50) | copy-start | bytes 196
  149.1 36.0 %copy-start.32 = (s32[2,2,4]{2,1,0:T(2,128)S(1)}, s32[2,2,4]{2,1,0:T(2,128)}, u32[]{:S(2)}) copy-start(s32[2,2,4]{2,1,0:T(2,128)} %get-tuple-element.543) | copy-start | bytes 196
  149.1 35.9 %copy-start.33 = (s32[2,2,4]{2,1,0:T(2,128)S(1)}, s32[2,2,4]{2,1,0:T(2,128)}, u32[]{:S(2)}) copy-start(s32[2,2,4]{2,1,0:T(2,128)} %get-tuple-element.544) | copy-start | bytes 196
  149.1 36.0 %copy-start.56 = (s32[16]{0:T(128)S(1)}, s32[16]{0:T(128)}, u32[]{:S(2)}) copy-start(s32[16]{0:T(128)} %get-tuple-element.533) | copy-start | bytes 196
  149.1 391.2 %all-gather.16.cloned.1.call-start = ((), (), s32[]{:S(2)}) async-start(), calls=%async_computation.2 | async-start | bytes 16711680 | tf_op jit(solution)/shard_map/all_gather | solution.py:225
  166.9 77.6 %copy-start.30 = (pred[16,269]{1,0:T(8,128)(4,1)}, pred[16,269]{1,0:T(8,128)(4,1)S(1)}, u32[]{:S(2)}) copy-start(pred[16,269]{1,0:T(8,128)(4,1)S(1)} %iota_compare_fusion.25) | copy-start | bytes 12916
  204.4 39.7 %copy-start.8 = (s32[16,269]{1,0:T(8,128)}, s32[16,269]{1,0:T(8,128)S(1)}, u32[]{:S(2)}) copy-start(s32[16,269]{1,0:T(8,128)S(1)} %pad_select_fusion) | copy-start | bytes 51652
  431.7 43.7 %copy-start.1 = (bf16[73,256,128]{2,1,0:T(8,128)(2,1)}, bf16[73,256,128]{2,1,0:T(8,128)(2,1)S(1)}, u32[]{:S(2)}) copy-start(bf16[73,256,128]{2,1,0:T(8,128)(2,1)S(1)} %shard_map.112.x_ref) | copy-start | bytes 14352388
  475.4 65.0 %copy-start.2 = (bf16[256,4608]{1,0:T(8,128)(2,1)S(1)}, bf16[256,4608]{1,0:T(8,128)(2,1)}, u32[]{:S(2)}) copy-start(bf16[256,4608]{1,0:T(8,128)(2,1)} %param.15) | copy-start | bytes 7077892
  475.4 65.0 %copy-start.11 = (s32[16,30]{1,0:T(8,128)S(1)}, s32[16,30]{1,0:T(8,128)}, u32[]{:S(2)}) copy-start(s32[16,30]{1,0:T(8,128)} %get-tuple-element.557) | copy-start | bytes 5764
  477.9 28.4 %collective-permute-start.5 = (bf16[256,2304]{1,0:T(8,128)(2,1)}, bf16[256,2304]{1,0:T(8,128)(2,1)S(1)}, u32[]{:S(2)}, u32[]{:S(2)}) collective-permute-start(bf16[256,2304]{1,0:T(8,128)(2,1)} %constant_dynamic-slice_fusion.3), channel_id=1, source_target_pairs={{0,1},{1,0},{2,3},{3,2},{4,5},{5,4},{6,7},{7,6},{8,9},{9,8},{10,11... | collective-permute-start | bytes 3538952 | tf_op jit(solution)/shard_map/ppermute | solution.py:378
  (43 other events, 298.5 us)
Sparse Core Ops, SparseCore 0:
  10.4 219.7 all-gather.13
  231.9 185.7 all-gather.11
  420.0 120.3 all-gather.15

commit v7 on v6

--- a/solution.py
+++ b/solution.py
@@ -12,31 +12,64 @@
 LAST_VMEM_BYTES = 36 * 1024 * 1024
 
 
+def group_kernel(group, size, zero_row, row_ref, col_ref, field_ref, count_ref, fill_ref, open_ref):
+    step, steps = pl.program_id(0), pl.num_programs(0)
+    listed = row_ref.shape[0] // steps
+
+    def field(number, at):
+        return (number * steps + step) * size + at
+
+    def clear(at, carry):
+        field_ref[field(0, at)] = 0
+        for g in range(group):
+            field_ref[field(1 + g, at)] = 0
+            field_ref[field(1 + group + g, at)] = zero_row
+        return carry
+
+    def no_group(c, carry):
+        fill_ref[c] = 0
+        open_ref[c] = 0
+        return carry
+
+    def place(tile, groups):
+        col = col_ref[step * listed + tile]
+        held = jnp.maximum(col, 0)
+        filled = fill_ref[held]
+        opens = (col >= 0) & (filled == 0)
+        at = jnp.where(opens, groups, open_ref[held])
+
+        @pl.when(col >= 0)
+        def _():
+            open_ref[held] = at
+            fill_ref[held] = jnp.where(filled == group - 1, 0, filled + 1)
+            field_ref[field(0, at)] = col
+            field_ref[field(1 + filled, at)] = tile
+            field_ref[field(1 + group + filled, at)] = row_ref[step * listed + tile]
+
+        return groups + opens.astype(jnp.int32)
+
+    lax.fori_loop(0, size, clear, 0)
+    lax.fori_loop(0, fill_ref.shape[0], no_group, 0)
+    count_ref[step] = lax.fori_loop(0, listed, place, jnp.int32(0))
+
+
 def group_up(rows, cols, live, blocks, zero_row, group):
-    listed = rows.shape[1]
-    ids = jnp.arange(listed, dtype=jnp.int32)
-    block_ids = jnp.arange(blocks, dtype=jnp.int32)
+    steps, listed = rows.shape
     most = (listed + (group - 1) * min(blocks, listed)) // group
     size = -(-most // UNROLL) * UNROLL
-    same = live[:, None, :] & (cols[:, :, None] == cols[:, None, :]) & (ids < ids[:, None])
-    rank = jnp.sum(same.astype(jnp.int32), axis=2)
-    in_block = live[:, None, :] & (cols[:, None, :] == block_ids[:, None])
-    need = (jnp.sum(in_block.astype(jnp.int32), axis=2) + group - 1) // group
-    begin = jnp.cumsum(need, axis=1) - need
-    begin = jnp.sum(jnp.where(cols[:, :, None] == block_ids, begin[:, None, :], 0), axis=2)
-    place = jnp.where(live, begin + rank // group, -1)
-    hit = place[:, None, :] == jnp.arange(size, dtype=jnp.int32)[:, None]
-    turn = (rank % group)[:, None, :]
-
-    def chosen(mask, values, default):
-        found = jnp.sum(jnp.where(mask, values[:, None, :] - default, 0), axis=2)
-        return found + default
-
-    tile_ids = jnp.broadcast_to(ids, rows.shape)
-    fields = [chosen(hit & (turn == 0), cols, 0)]
-    fields += [chosen(hit & (turn == g), tile_ids, 0) for g in range(group)]
-    fields += [chosen(hit & (turn == g), rows, zero_row) for g in range(group)]
-    return jnp.stack(fields).reshape(-1), jnp.sum(need, axis=1)
+    smem = pl.BlockSpec(memory_space=pltpu.SMEM)
+    return pl.pallas_call(
+        functools.partial(group_kernel, group, size, zero_row),
+        out_shape=[
+            jax.ShapeDtypeStruct(((2 * group + 1) * steps * size,), jnp.int32),
+            jax.ShapeDtypeStruct((steps,), jnp.int32),
+        ],
+        grid=(steps,),
+        in_specs=[smem, smem],
+        out_specs=[smem, smem],
+        scratch_shapes=[pltpu.SMEM((blocks,), jnp.int32), pltpu.SMEM((blocks,), jnp.int32)],
+        cost_estimate=pl.CostEstimate(flops=0, bytes_accessed=16 * steps * listed, transcendentals=0),
+    )(rows.reshape(-1), jnp.where(live, cols, -1).reshape(-1))
 
 
 def add_block(field_ref, count_ref, x_ref, w_ref, acc, group):
@@ -59,77 +92,101 @@
     lax.fori_loop(0, lax.div(count_ref[step] + UNROLL - 1, jnp.int32(UNROLL)), several, 0)
 
 
+def for_blocks(count, work):
+    def turn(c, carry):
+        work(c)
+        return carry
+
+    lax.fori_loop(0, count, turn, 0)
+
+
+def columns(c, width):
+    return pl.ds(pl.multiple_of(c * width, width), width)
+
+
+def at_start(work):
+    pl.when(pl.program_id(0) == 0)(work)
+
+
 def at_end(work):
     pl.when(pl.program_id(0) == pl.num_programs(0) - 1)(work)
 
 
-def first_kernel(group, field_ref, count_ref, at_ref, x_ref, w_ref, bias_ref, sum_ref, acc):
-    @pl.when(pl.program_id(0) == 0)
-    def _():
-        def fill(c, carry):
-            acc[c] = jnp.broadcast_to(bias_ref[c], acc.shape[1:])
-            return carry
-
-        lax.fori_loop(0, acc.shape[0], fill, 0)
-
-    add_block(field_ref, count_ref, x_ref, w_ref, acc, group)
-
-    @at_end
-    def _():
-        sum_ref[...] = acc[...]
+def first_kernel(group, field_ref, count_ref, at_ref, x_ref, w_ref, bias_ref, sum_ref):
+    @at_start
+    def _():
+        def fill(c):
+            sum_ref[c] = jnp.broadcast_to(bias_ref[c], sum_ref.shape[1:])
+
+        for_blocks(sum_ref.shape[0], fill)
+
+    add_block(field_ref, count_ref, x_ref, w_ref, sum_ref, group)
 
 
 def hidden_kernel(group, field_ref, count_ref, at_ref, x_ref, w_ref, sum_ref, out_ref, acc):
     blocks = acc.shape[0]
 
-    @pl.when(pl.program_id(0) == 0)
-    def _():
-        acc[...] = sum_ref[...]
+    @at_start
+    def _():
+        def fill(c):
+            acc[c] = sum_ref[c]
+
+        for_blocks(blocks, fill)
 
     add_block(field_ref, count_ref, x_ref, w_ref, acc, group)
 
     @at_end
     def _():
-        def finish(c, carry):
+        def finish(c):
             out_ref[c] = jnp.maximum(acc[c], 0.0).astype(out_ref.dtype)
-            return carry
-
-        lax.fori_loop(0, blocks, finish, 0)
+
+        for_blocks(blocks, finish)
         out_ref[blocks] = jnp.zeros(out_ref.shape[1:], out_ref.dtype)
 
 
 def partial_kernel(group, field_ref, count_ref, at_ref, x_ref, w_ref, sum_ref, out_ref):
-    @pl.when(pl.program_id(0) == 0)
-    def _():
-        sum_ref[...] = jnp.zeros_like(sum_ref)
+    blocks, width = sum_ref.shape[0], sum_ref.shape[2]
+
+    @at_start
+    def _():
+        def fill(c):
+            sum_ref[c] = jnp.zeros(sum_ref.shape[1:], sum_ref.dtype)
+
+        for_blocks(blocks, fill)
 
     add_block(field_ref, count_ref, x_ref, w_ref, sum_ref, group)
 
     @at_end
     def _():
-        width = sum_ref.shape[2]
-        for c in range(sum_ref.shape[0]):
-            out_ref[:, c * width : (c + 1) * width] = sum_ref[c].astype(out_ref.dtype)
+        def finish(c):
+            out_ref[:, columns(c, width)] = sum_ref[c].astype(out_ref.dtype)
+
+        for_blocks(blocks, finish)
 
 
 def result_kernel(
     group, field_ref, count_ref, at_ref,
     x_ref, w_ref, sum_ref, token_ref, other_ref, bias_ref, out_ref, acc,
 ):
-    @pl.when(pl.program_id(0) == 0)
-    def _():
-        acc[...] = sum_ref[...]
+    blocks, width = acc.shape[0], acc.shape[2]
+
+    @at_start
+    def _():
+        def fill(c):
+            acc[c] = sum_ref[c]
+
+        for_blocks(blocks, fill)
 
     add_block(field_ref, count_ref, x_ref, w_ref, acc, group)
 
     @at_end
     def _():
-        width = acc.shape[2]
-        for c in range(acc.shape[0]):
-            cols = slice(c * width, (c + 1) * width)
-            branch = acc[c] + other_ref[:, cols]
-            value = token_ref[:, cols].astype(jnp.float32) + branch + bias_ref[:, cols]
-            out_ref[:, cols] = value.astype(out_ref.dtype)
+        def finish(c):
+            cols = columns(c, width)
+            value = token_ref[:, cols].astype(jnp.float32) + (acc[c] + other_ref[:, cols])
+            out_ref[:, cols] = (value + bias_ref[:, cols]).astype(out_ref.dtype)
+
+        for_blocks(blocks, finish)
 
 
 def fixed(shape):
@@ -212,7 +269,7 @@
     opening = slots * 4 // 5
     rest = slots - opening
     held = slots
-    late_from = held - slots * 3 // 10
+    late_from = held - slots // 3
     levels = [
         (stride, max(slots // most, 1), max(slots // least, 1))
         for stride, most, least in ((1, 6, 8), (2, 12, 16), (4, 16, 24))
@@ -307,8 +364,7 @@
     )
     tiles2a = gathered(jnp.take(sources, order[:late_from], axis=0, mode="clip"))
     tiles2b = gathered(jnp.take(sources, order[late_from:held], axis=0, mode="clip"))
-    chunk = slots // 4
-    misplaced = jnp.stack([jnp.max(fronts) - late_from, jnp.max(lengths) - held])
+    misplaced = jnp.stack([jnp.max(fronts) - late_from, jnp.max(lengths) - held, jnp.max(lengths)])
     misplaced = lax.pmax(misplaced, "ffn")
 
     rows_f = tokens.astype(jnp.float32)
@@ -318,7 +374,7 @@
     normed_blocks = normed.reshape(token_rows, second_blocks, side).transpose(1, 0, 2)
     normed_blocks = jnp.pad(normed_blocks, ((0, 1), (0, 0), (0, 0)))
     normed_blocks, misplaced = lax.optimization_barrier((normed_blocks, misplaced))
-    some_late = jnp.max(misplaced) > 0
+    some_late = jnp.max(misplaced[:2]) > 0
 
     (total,) = tile_pass(
         first_kernel,
@@ -332,6 +388,7 @@
         [fixed((first_blocks, 1, side))],
         [jax.ShapeDtypeStruct((first_blocks, token_rows, side), jnp.float32)],
         first_blocks,
+        scratch=False,
     )
     (hidden,) = tile_pass(
         hidden_kernel,
@@ -347,7 +404,7 @@
         first_blocks,
     )
 
-    def second_pass(places, live, tiles):
+    def second_pass(places, live, tiles, steps=2, group=4):
         return tile_pass(
             partial_kernel,
             places // second_blocks,
@@ -363,8 +420,8 @@
                 jax.ShapeDtypeStruct((token_rows, width), jnp.bfloat16),
             ],
             second_blocks,
-            steps=2,
-            group=4,
+            steps=steps,
+            group=group,
             scratch=False,
         )
 
@@ -391,17 +448,18 @@
     branch = from_others(partial_value)
 
     def with_late(branch):
-        _, late = second_pass(last_codes, (in_second & in_front)[:, late_from:held], tiles2b)
-        branch = branch + from_others(late) + own_cols(late)
+        chunk = slots // 4
+        start = jnp.where(misplaced[0] > 0, late_from, held)
+        late = in_second & (in_front | (total_ids >= held))
 
         def one_more(number, branch):
-            at = held + number * chunk
+            at = start + number * chunk
             here = jnp.take(sources, lax.dynamic_slice_in_dim(order, at, chunk), axis=0, mode="clip")
-            part = [lax.dynamic_slice_in_dim(v, at, chunk, 1) for v in (codes, in_second)]
-            _, extra = second_pass(*part, gathered(here))
+            part = [lax.dynamic_slice_in_dim(v, at, chunk, 1) for v in (codes, late)]
+            _, extra = second_pass(*part, gathered(here), steps=1, group=1)
             return branch + from_others(extra) + own_cols(extra)
 
-        return lax.fori_loop(0, (misplaced[1] + chunk - 1) // chunk, one_more, branch)
+        return lax.fori_loop(0, (misplaced[2] - start + chunk - 1) // chunk, one_more, branch)
 
     if not aligned:
         branch = lax.cond(some_late, with_late, lambda branch: branch, branch)
@@ -412,7 +470,8 @@
     share_blocks = share // side
     last_rows, last_cols = last_codes // second_blocks, last_codes % second_blocks % share_blocks
     last_plan = planned(last_rows, last_cols, last_own, share_blocks, first_blocks, 2, 4)
-    last_plan, branch = lax.optimization_barrier((last_plan, branch))
+    bias_row = fc2_bias.reshape(1, share)
+    last_plan, branch, bias_row = lax.optimization_barrier((last_plan, branch, bias_row))
     last_pass = functools.partial(
         tile_pass,
         result_kernel,
@@ -445,7 +504,7 @@
     )
 
     def finished(branch):
-        return last_pass(more=[total, tokens, branch, fc2_bias.reshape(1, share)])[0]
+        return last_pass(more=[total, tokens, branch, bias_row])[0]
 
     return lax.cond(some_late, lambda branch: finished(with_late(branch)), finished, branch)
 

time: 575 us -> 529 us (0.920); the launches traced: 565 us -> 529 us
  Pallas kernels: 133 us -> 223 us
  other arithmetic: 141 us -> 63.3 us
  waiting for transfers between devices: 148 us -> 120 us
  local copies, waits for them, and re-layouts: 82 us -> 63.3 us
    pallas_call x0 -> x4, Pallas kernels: none -> 89.1 us  [group_up(): pl.pallas_call(functools.partial(group_kernel, group, size, zero_row), ou...]
    reduce_sum x20 -> x0, other arithmetic: 64.2 us -> none  [the longest x4 56 us: chosen(): found = jnp.sum(jnp.where(mask, values[:, None, :] - default, 0), axis=2)]
    all_gather x3, waiting for transfers between devices: 102 us -> 76.8 us  [gathered(): lax.all_gather(value, 'blk', axis=0, tiled=True)]
    reduce_sum x8, other arithmetic: 36.9 us -> 26.7 us  [moved(): return jnp.sum(jnp.where(hit, values[:, None, :], 0), axis=2)]
    unnamed x163 -> x148, local copies, waits for them, and re-layouts: 23.6 us -> 14.2 us
  transfers between devices with their start and end apart: 7 -> 7, of which waited for: 5 -> 5; matrix products, arithmetic and copies ran while one was open for 38% -> 23% of each run, Pallas kernels for 21% -> 39%
where the time goes in v7:
time: 529 us
  Pallas kernels  223 us (42%)
  waiting for transfers between devices  120 us (23%)
  local copies, waits for them, and re-layouts  63.3 us (12%)
  other arithmetic  63.3 us (12%)
  between operations  29 us (5%)
  blocking collectives  27.8 us (5%)
    pallas_call x4, Pallas kernels, tile_pass(): pl.pallas_call(functools.partial(kernel, group), out_shape=out_shapes, gr...  134 us
    pallas_call x4, Pallas kernels, group_up(): pl.pallas_call(functools.partial(group_kernel, group, size, zero_row), ou...  89.1 us
    all_gather x3, waiting for transfers between devices, gathered(): lax.all_gather(value, 'blk', axis=0, tiled=True)  76.8 us
    ppermute x3, waiting for transfers between devices, on_device(): lax.ppermute(jnp.take(sources, sending, axis=0, mode='clip'), 'blk', [(i,...  34.2 us
    reduce_sum x8, other arithmetic, moved(): return jnp.sum(jnp.where(hit, values[:, None, :], 0), axis=2)  26.7 us
    all_gather x1, blocking collectives, on_device(): meta = lax.all_gather(meta, 'blk', axis=0, tiled=True)  23.1 us
    unnamed x148, local copies, waits for them, and re-layouts  14.2 us
    gather x3, local copies, waits for them, and re-layouts, on_device(): jnp.take(sources, sending, axis=0, mode='clip')  11 us
  transfers between devices with their start and end apart: 7, of which 5 were waited for; matrix products, arithmetic and copies ran while one was open for 23% of the time, Pallas kernels for 39%

profile of v7, /device:TPU:0, one launch (start us, length us, event | category | flops | bytes accessed | tf_op | source)
XLA Modules:
  0.0 528.8 jit_solution(6636977790645452040)
XLA Ops:
  6.5 3.9 slice.97
  11.9 23.1 %all-gather.4 = s32[16,1,204]{2,1,0:T(1,128)S(1)} all-gather(s32[1,1,204]{2,1,0:T(1,128)S(1)} %add_bitcast_fusion), channel_id=1, replica_groups=mesh['blk'=16,'ffn'=2] {'blk'}, dimensions={0}, use_global_device_ids=true | all-gather | bytes 13872 | tf_op jit(solution)/shard_map/all_gather | solution.py:286
  52.6 2.5 compare_select_fusion.4
  59.6 3.8 gather_fusion.1
  73.5 6.1 %fusion.10 = s32[269]{0:T(512)S(1)} fusion(s32[269]{0:T(512)S(1)} %iota_subtract_fusion.7, s32[269]{0:T(512)S(1)} %pad.58), kind=kLoop, calls=%fused_computation.50 | loop fusion | flops 216814 | bytes 3228 | tf_op jit(solution)/shard_map/reduce_sum | solution.py:243
  85.3 4.2 pad_maximum_fusion.1
  89.5 3.8 gather_fusion.2
  95.3 21.2 %collective-permute-done.2 = bf16[14,128,128]{2,1,0:T(8,128)(2,1)S(1)} collective-permute-done((bf16[14,128,128]{2,1,0:T(8,128)(2,1)}, bf16[14,128,128]{2,1,0:T(8,128)(2,1)S(1)}, u32[]{:S(2)}, u32[]{:S(2)}) %collective-permute-start.2) | collective-permute-done | bytes 458784 | tf_op jit(solution)/shard_map/ppermute | solution.py:343
  117.3 5.4 %pad_maximum_fusion = bf16[164,128,128]{2,1,0:T(8,128)(2,1)} fusion(bf16[14,128,128]{2,1,0:T(8,128)(2,1)S(1)} %collective-permute-done.2, bf16[28,128,128]{2,1,0:T(8,128)(2,1)} %collective-permute-done.1, bf16[101,128,128]{2,1,0:T(8,128)(2,1)S(1)} %bitcast.99, bf16[21,128,128]{2,1,0:T(8,128)(2,1)S(1)} %copy-done.2), kind=kLoop, calls=%fused_computation.23 | loop fusion | flops 8060928 | bytes 10747904 | tf_op jit(solution)/shard_map/concatenate | solution.py:351
  122.6 3.4 gather_fusion.3
  130.2 13.0 %collective-permute-done.3 = bf16[10,128,128]{2,1,0:T(8,128)(2,1)S(1)} collective-permute-done((bf16[10,128,128]{2,1,0:T(8,128)(2,1)S(1)}, bf16[10,128,128]{2,1,0:T(8,128)(2,1)S(1)}, u32[]{:S(2)}, u32[]{:S(2)}) %collective-permute-start.3) | collective-permute-done | bytes 327712 | tf_op jit(solution)/shard_map/ppermute | solution.py:343
  144.1 5.2 gather_fusion.4
  149.6 4.4 gather_fusion.5
  156.6 4.7 pmax.7
  181.2 2.6 select_reduce_fusion.1
  184.0 5.9 %select_reduce_fusion = s32[16,269]{0,1:T(8,128)S(1)} fusion(s32[16,269]{1,0:T(8,128)S(1)} %pad.50, s32[16,269]{0,1:T(8,128)S(1)} %iota_subtract_fusion), kind=kLoop, calls=%fused_computation.17 | loop fusion | flops 3469024 | bytes 51648 | tf_op jit(solution)/shard_map/reduce_sum | solution.py:243
  191.9 2.9 copy.145
  196.1 3.4 fusion.7
  199.5 3.1 copy.146
  204.9 12.6 %shard_map.113 = (s32[1600]{0:T(1024)}, s32[4]{0:T(128)}) custom-call(s32[336]{0:T(512)} %reshape_reshape.14.row_ref, s32[336]{0:T(512)} %compare_select_fusion.10.col_ref), custom_call_target="tpu_custom_call" | custom-call | bytes 5376 | tf_op jit(solution)/shard_map/pallas_call | solution.py:61
  218.1 35.5 %shard_map.114 = (s32[3920]{0:T(1024)}, s32[4]{0:T(128)}) custom-call(s32[1280]{0:T(1024)} %reshape_reshape.15.row_ref, s32[1280]{0:T(1024)} %compare_select_fusion.2.col_ref), custom_call_target="tpu_custom_call" | custom-call | bytes 20480 | tf_op jit(solution)/shard_map/pallas_call | solution.py:61
  253.6 27.1 %shard_map.112 = (s32[2952]{0:T(1024)}, s32[2]{0:T(128)}) custom-call(s32[1088]{0:T(1024)} %reshape_reshape.13.row_ref, s32[1088]{0:T(1024)} %select_n.587.col_ref), custom_call_target="tpu_custom_call" | custom-call | bytes 17408 | tf_op jit(solution)/shard_map/pallas_call | solution.py:61
  280.7 60.6 %shard_map.115.sum_ref = f32[72,256,128]{2,1,0:T(8,128)} custom-call(s32[3920]{0:T(1024)} %get-tuple-element.264.field_ref, s32[4]{0:T(128)} %get-tuple-element.265.count_ref, s32[1]{0:T(128)} %bitcast.35.at_ref, bf16[37,256,128]{2,1,0:T(8,128)(2,1)} %pad.47.x_ref, bf16[16,80,128,128]{3,2,1,0:T(8,128)(2,1)} %bitcast.139, f32[72,1,128]{2,1,0:T(1,128)} %bitcast.143), custom_call_target="tpu_custom_call" | custom-call | flops 21474836480 | bytes 41943040 | tf_op jit(solution)/shard_map/pallas_call | solution.py:211
  341.3 69.1 %all-gather.12.cloned.1.call-done = bf16[1088,128,128]{2,1,0:T(8,128)(2,1)} async-done(((bf16[68,128,128]{2,1,0:T(8,128)(2,1)}), bf16[1088,128,128]{2,1,0:T(8,128)(2,1)}) %all-gather.12.cloned.1.call-update) | async-done | bytes 35651600 | tf_op jit(solution)/shard_map/all_gather | solution.py:282
  410.5 13.7 %shard_map.116.x_ref = bf16[73,256,128]{2,1,0:T(8,128)(2,1)S(1)} custom-call(s32[1600]{0:T(1024)} %get-tuple-element.261.field_ref, s32[4]{0:T(128)} %get-tuple-element.262.count_ref, s32[1]{0:T(128)} %bitcast.35.at_ref, bf16[37,256,128]{2,1,0:T(8,128)(2,1)} %pad.47.x_ref, bf16[16,68,128,128]{3,2,1,0:T(8,128)(2,1)} %bitcast.100, ...), custom_call_target="tpu_custom_call" | custom-call | flops 5637144576 | bytes 11010048 | tf_op jit(solution)/shard_map/pallas_call | solution.py:211
  424.2 41.6 %shard_map.117 = (f32[36,256,128]{2,1,0:T(8,128)}, bf16[256,4608]{1,0:T(8,128)(2,1)}) custom-call(s32[2952]{0:T(1024)} %get-tuple-element.259.field_ref, s32[2]{0:T(128)} %get-tuple-element.260.count_ref, s32[1]{0:T(128)} %bitcast.35.at_ref, bf16[73,256,128]{2,1,0:T(8,128)(2,1)S(1)} %shard_map.116.x_ref, bf16[16,68,128,128]{3,2,1,0:T(8,128)(2,1)} %bitcast.101), custom_call_target="tpu_custom_call" | custom-call | flops 18253611008 | bytes 35651584 | tf_op jit(solution)/shard_map/pallas_call | solution.py:211
  467.2 2.5 collective-permute-start.4
  473.2 13.9 %shard_map.111 = (s32[1440]{0:T(1024)S(1)}, s32[2]{0:T(128)}) custom-call(s32[528]{0:T(1024)} %reshape_reshape.12.row_ref, s32[528]{0:T(1024)} %select_n.583.col_ref), custom_call_target="tpu_custom_call" | custom-call | bytes 8448 | tf_op jit(solution)/shard_map/pallas_call | solution.py:61
  487.1 8.8 %collective-permute-done.4 = bf16[256,2304]{1,0:T(8,128)(2,1)S(1)} collective-permute-done((bf16[256,2304]{1,0:T(8,128)(2,1)S(1)}, bf16[256,2304]{1,0:T(8,128)(2,1)S(1)}, u32[]{:S(2)}, u32[]{:S(2)}) %collective-permute-start.4) | collective-permute-done | bytes 1179680 | tf_op jit(solution)/shard_map/ppermute | solution.py:435
  496.0 7.6 %all-gather.16.cloned.1.call-done = bf16[528,128,128]{2,1,0:T(8,128)(2,1)} async-done(((bf16[33,128,128]{2,1,0:T(8,128)(2,1)}), bf16[528,128,128]{2,1,0:T(8,128)(2,1)}) %all-gather.16.cloned.1.call-update) | async-done | bytes 17301520 | tf_op jit(solution)/shard_map/all_gather | solution.py:282
  503.7 17.6 %conditional.1 = (bf16[256,2304]{1,0:T(8,128)(2,1)S(1)}) conditional(s32[]{:T(128)} %convert_element_type.50, (s32[]{:T(128)}, s32[1440]{0:T(1024)S(1)}, s32[2]{0:T(128)}, bf16[73,256,128]{2,1,0:T(8,128)(2,1)}, bf16[16,33,128,128]{3,2,1,0:T(8,128)(2,1)}, /*index=5*/f32[36,256,128]{2,1,0:T(8,128)}, bf16[256,4608]{1,0:T(8,128)(2,1)}, ...), branch_computations={%region_24.25_spmd, %region_25.28_spmd} | conditional | flops 15571630080 | bytes 88065992 | solution.py:509
  503.7 17.6 %branch_0_fun.1 = bf16[256,2304]{1,0:T(8,128)(2,1)S(1)} custom-call(s32[1440]{0:T(1024)S(1)} %get-tuple-element.197.field_ref, s32[2]{0:T(128)} %get-tuple-element.198.count_ref, s32[1]{0:T(128)} %bitcast.at_ref, bf16[73,256,128]{2,1,0:T(8,128)(2,1)} %get-tuple-element.200.x_ref, bf16[16,33,128,128]{3,2,1,0:T(8,128)(2,1)} %get-tuple-element.201.w_ref, ...), custom_call_target="tpu_custom_call" | custom-call | flops 8858370048 | bytes 17301504 | tf_op jit(solution)/shard_map/cond/branch_0_fun/pallas_call | solution.py:211
  (374 shorter events, 66.5 us)
Async XLA Ops:
  6.5 274.2 %all-gather.14.cloned.1.call-start = ((), (), s32[]{:S(2)}) async-start(), calls=%async_computation.1 | async-start | bytes 44564480 | tf_op jit(solution)/shard_map/all_gather | solution.py:282
  6.5 50.8 %copy-start = (bf16[1,1,101,128,128]{4,3,2,1,0:T(8,128)(2,1)S(1)}, bf16[1,1,101,128,128]{4,3,2,1,0:T(8,128)(2,1)}, u32[]{:S(2)}) copy-start(bf16[1,1,101,128,128]{4,3,2,1,0:T(8,128)(2,1)} %param.22) | copy-start | bytes 9928708
  10.5 400.0 %all-gather.12.cloned.1.call-start = ((), (), s32[]{:S(2)}) async-start(), calls=%async_computation | async-start | bytes 37879808 | tf_op jit(solution)/shard_map/all_gather | solution.py:282
  63.4 21.9 %collective-permute-start.1 = (bf16[28,128,128]{2,1,0:T(8,128)(2,1)}, bf16[28,128,128]{2,1,0:T(8,128)(2,1)}, u32[]{:S(2)}, u32[]{:S(2)}) collective-permute-start(bf16[28,128,128]{2,1,0:T(8,128)(2,1)} %gather_fusion.1), channel_id=1, source_target_pairs={{0,2},{2,0},{4,6},{6,4},{8,10},{10,8},{12,14},{14,12},{16,18},{18,... | collective-permute-start | bytes 2752520 | tf_op jit(solution)/shard_map/ppermute | solution.py:343
  93.3 23.2 %collective-permute-start.2 = (bf16[14,128,128]{2,1,0:T(8,128)(2,1)}, bf16[14,128,128]{2,1,0:T(8,128)(2,1)S(1)}, u32[]{:S(2)}, u32[]{:S(2)}) collective-permute-start(bf16[14,128,128]{2,1,0:T(8,128)(2,1)} %gather_fusion.2), channel_id=1, source_target_pairs={{0,4},{2,6},{4,0},{6,2},{8,12},{10,14},{12,8},{14,10},{16,20},{18,... | collective-permute-start | bytes 1376264 | tf_op jit(solution)/shard_map/ppermute | solution.py:343
  95.3 30.8 %slice-start = ((s32[269]{0:T(512)}), s32[68]{0:T(128)S(1)}, s32[]{:S(2)}) async-start(s32[269]{0:T(512)} %copy-done.57), calls=%async_computation.4 | async-start | bytes 1024 | tf_op jit(solution)/shard_map/slice | solution.py:365
  126.0 17.2 %collective-permute-start.3 = (bf16[10,128,128]{2,1,0:T(8,128)(2,1)S(1)}, bf16[10,128,128]{2,1,0:T(8,128)(2,1)S(1)}, u32[]{:S(2)}, u32[]{:S(2)}) collective-permute-start(bf16[10,128,128]{2,1,0:T(8,128)(2,1)S(1)} %gather_fusion.3), channel_id=1, source_target_pairs={{0,8},{2,10},{4,12},{6,14},{8,0},{10,2},{12,4},{14,6},{16,24},{18,... | collective-permute-start | bytes 983048 | tf_op jit(solution)/shard_map/ppermute | solution.py:343
  144.0 24.1 %copy-start.37 = (s32[16]{0:T(128)S(1)}, s32[16]{0:T(128)}, u32[]{:S(2)}) copy-start(s32[16]{0:T(128)} %copy-done.36) | copy-start | bytes 196
  144.1 24.1 %copy-start.41 = (s32[16]{0:T(128)S(1)}, s32[16]{0:T(128)}, u32[]{:S(2)}) copy-start(s32[16]{0:T(128)} %copy-done.40) | copy-start | bytes 196
  144.1 24.1 %copy-start.63 = (s32[16]{0:T(128)S(1)}, s32[16]{0:T(128)}, u32[]{:S(2)}) copy-start(s32[16]{0:T(128)} %copy-done.62) | copy-start | bytes 196
  144.1 26.7 %copy-start.35 = (s32[16]{0:T(128)S(1)}, s32[16]{0:T(128)}, u32[]{:S(2)}) copy-start(s32[16]{0:T(128)} %copy-done.34) | copy-start | bytes 196
  144.1 26.7 %copy-start.39 = (s32[16]{0:T(128)S(1)}, s32[16]{0:T(128)}, u32[]{:S(2)}) copy-start(s32[16]{0:T(128)} %copy-done.38) | copy-start | bytes 196
  144.1 26.7 %copy-start.61 = (s32[16]{0:T(128)S(1)}, s32[16]{0:T(128)}, u32[]{:S(2)}) copy-start(s32[16]{0:T(128)} %copy-done.60) | copy-start | bytes 196
  149.3 24.1 %copy-start.50 = (s32[16]{0:T(128)S(1)}, s32[16]{0:T(128)}, u32[]{:S(2)}) copy-start(s32[16]{0:T(128)} %get-tuple-element.332) | copy-start | bytes 196
  149.3 26.6 %copy-start.33 = (s32[16]{0:T(128)S(1)}, s32[16]{0:T(128)}, u32[]{:S(2)}) copy-start(s32[16]{0:T(128)} %copy-done.32) | copy-start | bytes 196
  149.3 26.6 %copy-start.45 = (s32[16]{0:T(128)S(1)}, s32[16]{0:T(128)}, u32[]{:S(2)}) copy-start(s32[16]{0:T(128)} %copy-done.44) | copy-start | bytes 196
  149.3 26.6 %copy-start.49 = (s32[16]{0:T(128)S(1)}, s32[16]{0:T(128)}, u32[]{:S(2)}) copy-start(s32[16]{0:T(128)} %copy-done.48) | copy-start | bytes 196
  149.3 29.1 %copy-start.26 = (s32[4,2,2]{2,1,0:T(2,128)S(1)}, s32[4,2,2]{2,1,0:T(2,128)}, u32[]{:S(2)}) copy-start(s32[4,2,2]{2,1,0:T(2,128)} %get-tuple-element.349) | copy-start | bytes 196
  149.3 29.2 %copy-start.31 = (s32[16]{0:T(128)S(1)}, s32[16]{0:T(128)}, u32[]{:S(2)}) copy-start(s32[16]{0:T(128)} %get-tuple-element.338) | copy-start | bytes 196
  149.3 29.2 %copy-start.43 = (s32[16]{0:T(128)S(1)}, s32[16]{0:T(128)}, u32[]{:S(2)}) copy-start(s32[16]{0:T(128)} %copy-done.42) | copy-start | bytes 196
  149.3 29.2 %copy-start.47 = (s32[16]{0:T(128)S(1)}, s32[16]{0:T(128)}, u32[]{:S(2)}) copy-start(s32[16]{0:T(128)} %copy-done.46) | copy-start | bytes 196
  149.3 31.7 %copy-start.28 = (s32[2,2,4]{2,1,0:T(2,128)S(1)}, s32[2,2,4]{2,1,0:T(2,128)}, u32[]{:S(2)}) copy-start(s32[2,2,4]{2,1,0:T(2,128)} %get-tuple-element.346) | copy-start | bytes 196
  149.4 31.7 %copy-start.29 = (s32[2,2,4]{2,1,0:T(2,128)S(1)}, s32[2,2,4]{2,1,0:T(2,128)}, u32[]{:S(2)}) copy-start(s32[2,2,4]{2,1,0:T(2,128)} %get-tuple-element.347) | copy-start | bytes 196
  149.4 31.8 %copy-start.53 = (s32[16]{0:T(128)S(1)}, s32[16]{0:T(128)}, u32[]{:S(2)}) copy-start(s32[16]{0:T(128)} %get-tuple-element.336) | copy-start | bytes 196
  149.4 34.5 %copy-start.52 = (s32[16]{0:T(128)S(1)}, s32[16]{0:T(128)}, u32[]{:S(2)}) copy-start(s32[16]{0:T(128)} %get-tuple-element.337) | copy-start | bytes 196
  149.4 34.6 %copy-start.66 = (s32[16]{0:T(128)S(1)}, s32[16]{0:T(128)}, u32[]{:S(2)}) copy-start(s32[16]{0:T(128)} %copy-done.65) | copy-start | bytes 196
  149.4 354.2 %all-gather.16.cloned.1.call-start = ((), (), s32[]{:S(2)}) async-start(), calls=%async_computation.2 | async-start | bytes 18382848 | tf_op jit(solution)/shard_map/all_gather | solution.py:282
  424.1 41.7 %copy-start.3 = (bf16[73,256,128]{2,1,0:T(8,128)(2,1)}, bf16[73,256,128]{2,1,0:T(8,128)(2,1)S(1)}, u32[]{:S(2)}) copy-start(bf16[73,256,128]{2,1,0:T(8,128)(2,1)S(1)} %shard_map.116.x_ref) | copy-start | bytes 14352388
  424.1 45.5 %copy-start.27 = (f32[2304]{0:T(1024)S(1)}, f32[2304]{0:T(1024)}, u32[]{:S(2)}) copy-start(f32[2304]{0:T(1024)} %param.25) | copy-start | bytes 27652
  424.2 46.2 %copy-start.6 = (s32[16,269]{1,0:T(8,128)S(1)}, s32[16,269]{1,0:T(8,128)}, u32[]{:S(2)}) copy-start(s32[16,269]{1,0:T(8,128)} %copy-done.5) | copy-start | bytes 51652
  424.2 47.7 %copy-start.59 = (s32[3]{0:T(128)S(1)}, s32[3]{0:T(128)}, u32[]{:S(2)}) copy-start(s32[3]{0:T(128)} %pmax.7) | copy-start | bytes 40
  467.2 28.7 %collective-permute-start.4 = (bf16[256,2304]{1,0:T(8,128)(2,1)S(1)}, bf16[256,2304]{1,0:T(8,128)(2,1)S(1)}, u32[]{:S(2)}, u32[]{:S(2)}) collective-permute-start(bf16[256,2304]{1,0:T(8,128)(2,1)S(1)} %constant_dynamic-slice_fusion.1), channel_id=1, source_target_pairs={{0,1},{1,0},{2,3},{3,2},{4,5},{5,4},{6,7},{7,6},{8,9},{9,8},{10,11... | collective-permute-start | bytes 3538952 | tf_op jit(solution)/shard_map/ppermute | solution.py:435
  (47 other events, 432.4 us)
Sparse Core Ops, SparseCore 0:
  10.6 219.8 all-gather.13
  232.0 178.3 all-gather.11
  412.1 91.5 all-gather.15
